TPU v7x, 256 devices: a whole 4x4x8 slice. The times are simulated.
256 devices in a mesh: pb: 64 (over y, z, x_lo), ka: 4 (over x_hi, core).
Axes of the slice: x: 4 (x_hi: 2, x_lo: 2; x = x_hi * 2 + x_lo), y: 4, z: 8, core: 2. Of those that a mesh axis runs over, the one named last changes fastest.
Arguments:
- queries: bfloat16 [16384, 4096], P('pb', 'ka'), may hold values from -25 to 25
- output_gradient: bfloat16 [16384, 4096], P('pb', 'ka'), may hold values from -6 to 6
- key_states: bfloat16 [16384, 2048], P(('pb', 'ka')), may hold values from -6 to 6
- value_inputs: bfloat16 [16384, 2048], P(('pb', 'ka')), may hold values from -6 to 6
- turn_ids: int32 [16384], replicated, may hold values from 0 to 31, never falling along the last dimension, each value on 1 to 1792 neighbouring positions
- listed: int32 [2, 128, 14], replicated, may hold values 0 or 1
Outputs:
- grad_queries: float32 [16384, 4096], P('pb', 'ka')
- grad_keys: float32 [16384, 2048], P(('pb', 'ka'))
- grad_values: float32 [16384, 2048], P(('pb', 'ka'))
Inputs may be any that keep to these rules, and one draw needn't show every extreme that they name: `turn_ids`: turn numbers never fall along the window; every turn spans 1 to 1792 positions, and some turn spans exactly 1792.
All inputs are finite; a program needn't handle non-finite values.
Results may differ from a plain program's by a relative error of at most 0.003.
Values may be sent and summed in bfloat16 or wider, within the bound.
No kernel may reach another device: no remote copies, remote signals or barrier semaphores. Data moves between devices by JAX's collectives and lax.ppermute only.
A program may use at most 128 MiB of HBM per device.

v0:
```python
import jax
import jax.numpy as jnp
from jax import lax
from jax.sharding import PartitionSpec as P

QUERY_HEADS = 32
KEY_VALUE_HEADS = 16
HEAD_SIZE = 128
HEAD_GROUPS = 2
BLOCK_POSITIONS = 128
BACK = 14


SCORE_SCALE = 1.0 / 12.0
NEG_LARGE = -1e30


def shifted(x, axis, by):
    count = lax.axis_size(axis)
    pairs = [(i, i + by) for i in range(count) if 0 <= i + by < count]
    return lax.ppermute(x, axis, pairs)


def combined_all(x, axis, combine):
    everything = jax.tree.map(lambda part: lax.all_gather(part, axis), x)
    first = jax.tree.map(lambda part: part[0], everything)

    def hop(k, so_far):
        return combine(so_far, jax.tree.map(lambda part: part[k], everything))

    return lax.fori_loop(1, lax.axis_size(axis), hop, first)


def visible_mask(turn_ids, listed, query_begin, key_pos, tok_rows):
    query_pos = query_begin + jnp.arange(tok_rows, dtype=jnp.int32)
    query_turn = lax.dynamic_slice_in_dim(turn_ids, query_begin, tok_rows, 0)
    key_turn = turn_ids[jnp.clip(key_pos, 0, turn_ids.shape[0] - 1)]
    blk_count = tok_rows // BLOCK_POSITIONS
    query_blocks = query_begin // BLOCK_POSITIONS + jnp.arange(blk_count, dtype=jnp.int32)
    list_table = lax.dynamic_slice_in_dim(listed, query_begin // BLOCK_POSITIONS, blk_count, 1)
    offsets = query_blocks[:, None] - key_pos[None, :] // BLOCK_POSITIONS - 1
    onehot = (offsets[:, :, None] == jnp.arange(BACK, dtype=jnp.int32)[None, None, :]).astype(
        jnp.float32
    )
    listed_hit = jnp.einsum("gbo,bko->gbk", list_table.astype(jnp.float32), onehot) > 0.5
    listed_hit = jnp.repeat(listed_hit, BLOCK_POSITIONS, axis=1)
    causal_ok = (key_pos[None, :] <= query_pos[:, None]) & (key_pos[None, :] >= 0)
    same_turn = query_turn[:, None] == key_turn[None, :]
    return causal_ok[None] & (same_turn[None] | listed_hit)


def combine_terms(earlier_terms, later_terms):
    peak_max = jnp.maximum(earlier_terms[0], later_terms[0])
    first_factor = jnp.exp(earlier_terms[0] - peak_max)
    second_factor = jnp.exp(later_terms[0] - peak_max)
    return (
        peak_max,
        earlier_terms[1] * first_factor + later_terms[1] * second_factor,
        earlier_terms[2] * first_factor + later_terms[2] * second_factor,
    )


def fetch_window(stacked, win_depth):
    received = [stacked]
    moving = stacked
    for offset_dev in range(1, win_depth):
        moving = shifted(moving, "pb", 1)
        received.append(moving)
    return jnp.concatenate(received[::-1], axis=1)


def send_back(key_gradient, value_gradient, piece_rows, win_depth):

    def part_of(offset_dev):
        column = (win_depth - 1 - offset_dev) * piece_rows
        return jnp.stack(
            [
                key_gradient[column : column + piece_rows],
                value_gradient[column : column + piece_rows],
            ]
        )

    total_grad = part_of(0)
    for offset_dev in range(1, win_depth):
        total_grad = total_grad + shifted(part_of(offset_dev), "pb", -offset_dev)
    return total_grad


def per_device(queries, output_gradient, key_states, value_inputs, turn_ids, listed):
    tok_rows = queries.shape[0]
    win_depth = (BACK * BLOCK_POSITIONS + tok_rows - 1) // tok_rows + 1
    group_width = QUERY_HEADS // KEY_VALUE_HEADS
    head_cols = group_width * HEAD_SIZE
    group_head_count = KEY_VALUE_HEADS // HEAD_GROUPS
    pb_index = lax.axis_index("pb")
    ka_index = lax.axis_index("ka")
    piece_rows = key_states.shape[0]
    full_q, full_grad = (
        lax.all_gather(queries, "ka", axis=1, tiled=True),
        lax.all_gather(output_gradient, "ka", axis=1, tiled=True),
    )
    window = fetch_window(jnp.stack([key_states, value_inputs]), win_depth)
    key_total = win_depth * piece_rows
    column_ids = jnp.arange(key_total, dtype=jnp.int32)
    key_pos = (
        (pb_index - (win_depth - 1) + column_ids // piece_rows) * tok_rows
        + ka_index * piece_rows
        + column_ids % piece_rows
    )
    masks_all = visible_mask(turn_ids, listed, pb_index * tok_rows, key_pos, tok_rows)

    def scores_for(kv_head):
        query_cols = lax.dynamic_slice_in_dim(full_q, kv_head * head_cols, head_cols, 1).reshape(
            tok_rows, group_width, HEAD_SIZE
        )
        grad_cols = lax.dynamic_slice_in_dim(full_grad, kv_head * head_cols, head_cols, 1).reshape(
            tok_rows, group_width, HEAD_SIZE
        )
        key_head = lax.dynamic_slice_in_dim(window[0], kv_head * HEAD_SIZE, HEAD_SIZE, 1)
        value_head = lax.dynamic_slice_in_dim(window[1], kv_head * HEAD_SIZE, HEAD_SIZE, 1)
        allowed = lax.dynamic_index_in_dim(
            masks_all, kv_head // group_head_count, 0, keepdims=False
        )[None]
        raw_scores = (
            jnp.einsum("rqd,kd->qrk", query_cols, key_head, preferred_element_type=jnp.float32)
            * SCORE_SCALE
        )
        scores = jnp.where(allowed, raw_scores, NEG_LARGE)
        grad_prob = jnp.einsum(
            "rqd,kd->qrk", grad_cols, value_head, preferred_element_type=jnp.float32
        )
        return (query_cols, grad_cols, key_head, allowed, scores, grad_prob)

    def opening_sweep(kv_head, running):
        row_max, row_sum, row_dot = running
        query_cols, grad_cols, key_head, allowed, scores, grad_prob = scores_for(kv_head)
        local_max = jnp.max(scores, axis=2)
        weights = jnp.where(allowed, jnp.exp(scores - local_max[:, :, None]), 0.0)
        row_max = lax.dynamic_update_slice_in_dim(row_max, local_max, kv_head * group_width, 0)
        row_sum = lax.dynamic_update_slice_in_dim(
            row_sum, jnp.sum(weights, axis=2), kv_head * group_width, 0
        )
        row_dot = lax.dynamic_update_slice_in_dim(
            row_dot, jnp.sum(weights * grad_prob, axis=2), kv_head * group_width, 0
        )
        return (row_max, row_sum, row_dot)

    initial_terms = (
        jnp.full((QUERY_HEADS, tok_rows), NEG_LARGE, jnp.float32),
        jnp.zeros((QUERY_HEADS, tok_rows), jnp.float32),
        jnp.zeros((QUERY_HEADS, tok_rows), jnp.float32),
    )
    nearby_terms = lax.fori_loop(0, KEY_VALUE_HEADS, opening_sweep, initial_terms)
    peak_all, total_all, dot_all = combined_all(nearby_terms, "ka", combine_terms)
    delta_all = dot_all / total_all

    def closing_sweep(kv_head, running):
        query_gradient, key_gradient, value_gradient = running
        query_cols, grad_cols, key_head, allowed, scores, grad_prob = scores_for(kv_head)
        peak_max = lax.dynamic_slice_in_dim(peak_all, kv_head * group_width, group_width, 0)[
            :, :, None
        ]
        total_sum = lax.dynamic_slice_in_dim(total_all, kv_head * group_width, group_width, 0)[
            :, :, None
        ]
        delta_row = lax.dynamic_slice_in_dim(delta_all, kv_head * group_width, group_width, 0)[
            :, :, None
        ]
        soft_prob = jnp.where(allowed, jnp.exp(scores - peak_max), 0.0) / total_sum
        blended_rows = (SCORE_SCALE * soft_prob * (grad_prob - delta_row)).astype(jnp.bfloat16)
        probability_floor = soft_prob.astype(jnp.bfloat16)
        grad_q_head = jnp.einsum(
            "qrk,kd->rqd", blended_rows, key_head, preferred_element_type=jnp.float32
        ).reshape(tok_rows, head_cols)
        grad_k_head = jnp.einsum(
            "qrk,rqd->kd", blended_rows, query_cols, preferred_element_type=jnp.float32
        )
        grad_v_head = jnp.einsum(
            "qrk,rqd->kd", probability_floor, grad_cols, preferred_element_type=jnp.float32
        )
        query_gradient = lax.dynamic_update_slice_in_dim(
            query_gradient, grad_q_head, kv_head * head_cols, 1
        )
        key_gradient = lax.dynamic_update_slice_in_dim(
            key_gradient, grad_k_head, kv_head * HEAD_SIZE, 1
        )
        value_gradient = lax.dynamic_update_slice_in_dim(
            value_gradient, grad_v_head, kv_head * HEAD_SIZE, 1
        )
        return (query_gradient, key_gradient, value_gradient)

    initial_gradients = (
        jnp.zeros((tok_rows, QUERY_HEADS * HEAD_SIZE), jnp.float32),
        jnp.zeros((key_total, KEY_VALUE_HEADS * HEAD_SIZE), jnp.float32),
        jnp.zeros((key_total, KEY_VALUE_HEADS * HEAD_SIZE), jnp.float32),
    )
    query_gradient, key_gradient, value_gradient = lax.fori_loop(
        0, KEY_VALUE_HEADS, closing_sweep, initial_gradients
    )
    grad_queries = lax.psum_scatter(query_gradient, "ka", scatter_dimension=1, tiled=True)
    total_grad = send_back(key_gradient, value_gradient, piece_rows, win_depth)
    return (grad_queries, total_grad[0], total_grad[1])


def solution(mesh):
    in_specs = (
        P("pb", "ka"),
        P("pb", "ka"),
        P(("pb", "ka"), None),
        P(("pb", "ka"), None),
        P(),
        P(),
    )
    out_specs = (P("pb", "ka"), P(("pb", "ka"), None), P(("pb", "ka"), None))
    return jax.shard_map(
        per_device, mesh=mesh, in_specs=in_specs, out_specs=out_specs, check_vma=False
    )
```

profile of v0, /device:TPU:24, one launch (start us, length us, event | category | flops | bytes accessed | tf_op | source)
XLA Modules:
  0.0 787.9 jit_solution(13421518541701689419)
XLA Ops:
  10.4 3.4 collective-permute-start
  13.8 17.5 %collective-permute-done = bf16[2,64,2048]{2,1,0:T(8,128)(2,1)S(1)} collective-permute-done((bf16[2,64,2048]{2,1,0:T(8,128)(2,1)S(1)}, bf16[2,64,2048]{2,1,0:T(8,128)(2,1)S(1)}, u32[]{:S(2)}, u32[]{:S(2)}) %collective-permute-start) | collective-permute-done | bytes 524320 | tf_op jit(solution)/shard_map/ppermute | solution.py:21
  33.2 16.1 %collective-permute-done.1 = bf16[2,64,2048]{2,1,0:T(8,128)(2,1)S(1)} collective-permute-done((bf16[2,64,2048]{2,1,0:T(8,128)(2,1)S(1)}, bf16[2,64,2048]{2,1,0:T(8,128)(2,1)S(1)}, u32[]{:S(2)}, u32[]{:S(2)}) %collective-permute-start.1) | collective-permute-done | bytes 524320 | tf_op jit(solution)/shard_map/ppermute | solution.py:21
  49.3 3.6 collective-permute-start.2
  53.0 15.2 %collective-permute-done.2 = bf16[2,64,2048]{2,1,0:T(8,128)(2,1)S(1)} collective-permute-done((bf16[2,64,2048]{2,1,0:T(8,128)(2,1)S(1)}, bf16[2,64,2048]{2,1,0:T(8,128)(2,1)S(1)}, u32[]{:S(2)}, u32[]{:S(2)}) %collective-permute-start.2) | collective-permute-done | bytes 524320 | tf_op jit(solution)/shard_map/ppermute | solution.py:21
  72.2 12.8 %collective-permute-done.3 = bf16[2,64,2048]{2,1,0:T(8,128)(2,1)S(1)} collective-permute-done((bf16[2,64,2048]{2,1,0:T(8,128)(2,1)S(1)}, bf16[2,64,2048]{2,1,0:T(8,128)(2,1)S(1)}, u32[]{:S(2)}, u32[]{:S(2)}) %collective-permute-start.3) | collective-permute-done | bytes 524320 | tf_op jit(solution)/shard_map/ppermute | solution.py:21
  87.2 3.1 gather_fusion
  90.4 16.6 %collective-permute-done.4 = bf16[2,64,2048]{2,1,0:T(8,128)(2,1)S(1)} collective-permute-done((bf16[2,64,2048]{2,1,0:T(8,128)(2,1)S(1)}, bf16[2,64,2048]{2,1,0:T(8,128)(2,1)S(1)}, u32[]{:S(2)}, u32[]{:S(2)}) %collective-permute-start.4) | collective-permute-done | bytes 524320 | tf_op jit(solution)/shard_map/ppermute | solution.py:21
  107.0 4.4 collective-permute-start.5
  111.6 12.2 %collective-permute-done.5 = bf16[2,64,2048]{2,1,0:T(8,128)(2,1)} collective-permute-done((bf16[2,64,2048]{2,1,0:T(8,128)(2,1)S(1)}, bf16[2,64,2048]{2,1,0:T(8,128)(2,1)}, u32[]{:S(2)}, u32[]{:S(2)}) %collective-permute-start.5) | collective-permute-done | bytes 524320 | tf_op jit(solution)/shard_map/ppermute | solution.py:21
  126.8 13.2 %collective-permute-done.6 = bf16[2,64,2048]{2,1,0:T(8,128)(2,1)} collective-permute-done((bf16[2,64,2048]{2,1,0:T(8,128)(2,1)}, bf16[2,64,2048]{2,1,0:T(8,128)(2,1)}, u32[]{:S(2)}, u32[]{:S(2)}) %collective-permute-start.6) | collective-permute-done | bytes 524320 | tf_op jit(solution)/shard_map/ppermute | solution.py:21
  150.0 89.4 %while.57 = (s32[]{:T(128)}, f32[32,256]{1,0:T(8,128)S(1)}, f32[32,256]{1,0:T(8,128)S(1)}, f32[32,256]{1,0:T(8,128)S(1)}, pred[2,256,512]{1,2,0:T(8,128)(4,1)S(1...) while((s32[]{:T(128)}, f32[32,256]{1,0:T(8,128)S(1)}, ...), condition=%wide.region_4.5_spmd, body=%wide.region_0.4_spmd.sunk | while | flops 136837648 | bytes 13261259 | solution.py:153
  151.9 2.7 fusion.103
  157.5 2.7 fusion.103
  163.0 2.7 fusion.103
  168.6 2.7 fusion.103
  174.2 2.7 fusion.103
  179.8 2.7 fusion.103
  185.4 2.7 fusion.103
  191.0 2.7 fusion.103
  196.6 2.7 fusion.103
  202.2 2.7 fusion.103
  207.8 2.7 fusion.103
  213.3 2.7 fusion.103
  218.9 2.7 fusion.103
  230.1 2.7 fusion.103
  239.4 7.3 all-gather.2
  246.6 7.1 all-gather
  253.7 6.9 all-gather.1
  268.5 123.6 %while.59 = (s32[]{:T(128)}, f32[256,4096]{1,0:T(8,128)}, f32[512,2048]{1,0:T(8,128)}, f32[512,2048]{1,0:T(8,128)}, bf16[2,512,2048]{2,1,0:T(8,128)(2,1)}, /*ind...) while((s32[]{:T(128)}, f32[256,4096]{1,0:T(8,128)}, ...), condition=%wide.region_8.9_spmd, body=%wide.region_7.8_spmd.sunk | while | flops 338165792 | bytes 16796144 | solution.py:197
  269.5 2.7 fusion.119
  285.0 2.7 fusion.119
  292.7 2.7 fusion.119
  300.4 2.7 fusion.119
  308.1 2.7 fusion.119
  323.6 2.7 fusion.119
  331.3 2.7 fusion.119
  339.0 2.7 fusion.119
  346.7 2.7 fusion.119
  377.6 2.7 fusion.119
  402.2 3.7 collective-permute-start.10
  406.0 4.3 collective-permute-start.11
  410.4 39.8 %collective-permute-done.7 = f32[2,64,2048]{2,1,0:T(8,128)S(1)} collective-permute-done((f32[2,64,2048]{2,1,0:T(8,128)S(1)}, f32[2,64,2048]{2,1,0:T(8,128)S(1)}, u32[]{:S(2)}, u32[]{:S(2)}) %collective-permute-start.7) | collective-permute-done | bytes 1048608 | tf_op jit(solution)/shard_map/ppermute | solution.py:21
  452.1 33.6 %collective-permute-done.8 = f32[2,64,2048]{2,1,0:T(8,128)S(1)} collective-permute-done((f32[2,64,2048]{2,1,0:T(8,128)S(1)}, f32[2,64,2048]{2,1,0:T(8,128)S(1)}, u32[]{:S(2)}, u32[]{:S(2)}) %collective-permute-start.8) | collective-permute-done | bytes 1048608 | tf_op jit(solution)/shard_map/ppermute | solution.py:21
  487.6 54.5 %collective-permute-done.9 = f32[2,64,2048]{2,1,0:T(8,128)S(1)} collective-permute-done((f32[2,64,2048]{2,1,0:T(8,128)S(1)}, f32[2,64,2048]{2,1,0:T(8,128)S(1)}, u32[]{:S(2)}, u32[]{:S(2)}) %collective-permute-start.9) | collective-permute-done | bytes 1048608 | tf_op jit(solution)/shard_map/ppermute | solution.py:21
  542.1 91.5 %collective-permute-done.10 = f32[2,64,2048]{2,1,0:T(8,128)S(1)} collective-permute-done((f32[2,64,2048]{2,1,0:T(8,128)S(1)}, f32[2,64,2048]{2,1,0:T(8,128)S(1)}, u32[]{:S(2)}, u32[]{:S(2)}) %collective-permute-start.10) | collective-permute-done | bytes 1048608 | tf_op jit(solution)/shard_map/ppermute | solution.py:21
  633.6 123.7 %collective-permute-done.11 = f32[2,64,2048]{2,1,0:T(8,128)S(1)} collective-permute-done((f32[2,64,2048]{2,1,0:T(8,128)S(1)}, f32[2,64,2048]{2,1,0:T(8,128)S(1)}, u32[]{:S(2)}, u32[]{:S(2)}) %collective-permute-start.11) | collective-permute-done | bytes 1048608 | tf_op jit(solution)/shard_map/ppermute | solution.py:21
  757.3 22.2 %collective-permute-done.12 = f32[2,64,2048]{2,1,0:T(8,128)S(1)} collective-permute-done((f32[2,64,2048]{2,1,0:T(8,128)S(1)}, f32[2,64,2048]{2,1,0:T(8,128)S(1)}, u32[]{:S(2)}, u32[]{:S(2)}) %collective-permute-start.12) | collective-permute-done | bytes 1048608 | tf_op jit(solution)/shard_map/ppermute | solution.py:21
  (403 shorter events, 193.7 us)
Async XLA Ops:
  7.2 79.8 %copy-start = (s32[2,128,14]{1,0,2:T(2,128)S(1)}, s32[2,128,14]{1,0,2:T(2,128)}, u32[]{:S(2)}) copy-start(s32[2,128,14]{1,0,2:T(2,128)} %param.17) | copy-start | bytes 43012
  7.2 79.9 %copy-start.2 = (s32[16384]{0:T(1024)S(1)}, s32[16384]{0:T(1024)}, u32[]{:S(2)}) copy-start(s32[16384]{0:T(1024)} %param.16) | copy-start | bytes 196612
  7.2 142.7 %all-gather.6.cloned.1.call-start = ((), (), s32[]{:S(2)}) async-start(), calls=%async_computation.1 | async-start | bytes 2621440 | tf_op jit(solution)/shard_map/all_gather | solution.py:99
  9.3 140.6 %all-gather.8.cloned.1.call-start = ((), (), s32[]{:S(2)}) async-start(), calls=%async_computation.2 | async-start | bytes 2621440 | tf_op jit(solution)/shard_map/all_gather | solution.py:100
  10.4 20.9 %collective-permute-start = (bf16[2,64,2048]{2,1,0:T(8,128)(2,1)S(1)}, bf16[2,64,2048]{2,1,0:T(8,128)(2,1)S(1)}, u32[]{:S(2)}, u32[]{:S(2)}) collective-permute-start(bf16[2,64,2048]{2,1,0:T(8,128)(2,1)S(1)} %pad_maximum_fusion.7), channel_id=1, source_target_pairs={{0,4},{4,8},{8,12},{12,16},{16,20},{20,24},{24,28},{28,32},{32,36}... | collective-permute-start | bytes 1572872 | tf_op jit(solution)/shard_map/ppermute | solution.py:21
  31.3 18.0 %collective-permute-start.1 = (bf16[2,64,2048]{2,1,0:T(8,128)(2,1)S(1)}, bf16[2,64,2048]{2,1,0:T(8,128)(2,1)S(1)}, u32[]{:S(2)}, u32[]{:S(2)}) collective-permute-start(bf16[2,64,2048]{2,1,0:T(8,128)(2,1)S(1)} %collective-permute-done), channel_id=1, source_target_pairs={{0,4},{4,8},{8,12},{12,16},{16,20},{20,24},{24,28},{28,32},{32,36}... | collective-permute-start | bytes 1572872 | tf_op jit(solution)/shard_map/ppermute | solution.py:21
  49.3 18.9 %collective-permute-start.2 = (bf16[2,64,2048]{2,1,0:T(8,128)(2,1)S(1)}, bf16[2,64,2048]{2,1,0:T(8,128)(2,1)S(1)}, u32[]{:S(2)}, u32[]{:S(2)}) collective-permute-start(bf16[2,64,2048]{2,1,0:T(8,128)(2,1)S(1)} %collective-permute-done.1), channel_id=1, source_target_pairs={{0,4},{4,8},{8,12},{12,16},{16,20},{20,24},{24,28},{28,32},{32,36}... | collective-permute-start | bytes 1572872 | tf_op jit(solution)/shard_map/ppermute | solution.py:21
  68.2 16.9 %collective-permute-start.3 = (bf16[2,64,2048]{2,1,0:T(8,128)(2,1)S(1)}, bf16[2,64,2048]{2,1,0:T(8,128)(2,1)S(1)}, u32[]{:S(2)}, u32[]{:S(2)}) collective-permute-start(bf16[2,64,2048]{2,1,0:T(8,128)(2,1)S(1)} %collective-permute-done.2), channel_id=1, source_target_pairs={{0,4},{4,8},{8,12},{12,16},{16,20},{20,24},{24,28},{28,32},{32,36}... | collective-permute-start | bytes 1572872 | tf_op jit(solution)/shard_map/ppermute | solution.py:21
  72.2 709.2 %reduce-scatter.2.cloned.1.call-start = ((), (), s32[]{:S(2)}) async-start(), calls=%async_computation.3 | async-start | bytes 5242880 | tf_op jit(solution)/shard_map/reduce_scatter | solution.py:200
  85.0 22.0 %collective-permute-start.4 = (bf16[2,64,2048]{2,1,0:T(8,128)(2,1)S(1)}, bf16[2,64,2048]{2,1,0:T(8,128)(2,1)S(1)}, u32[]{:S(2)}, u32[]{:S(2)}) collective-permute-start(bf16[2,64,2048]{2,1,0:T(8,128)(2,1)S(1)} %collective-permute-done.3), channel_id=1, source_target_pairs={{0,4},{4,8},{8,12},{12,16},{16,20},{20,24},{24,28},{28,32},{32,36}... | collective-permute-start | bytes 1572872 | tf_op jit(solution)/shard_map/ppermute | solution.py:21
  107.0 18.9 %copy-start.6 = (bf16[2,64,2048]{2,1,0:T(8,128)(2,1)}, bf16[2,64,2048]{2,1,0:T(8,128)(2,1)S(1)}, u32[]{:S(2)}) copy-start(bf16[2,64,2048]{2,1,0:T(8,128)(2,1)S(1)} %collective-permute-done.4) | copy-start | bytes 1572868
  107.0 16.9 %collective-permute-start.5 = (bf16[2,64,2048]{2,1,0:T(8,128)(2,1)S(1)}, bf16[2,64,2048]{2,1,0:T(8,128)(2,1)}, u32[]{:S(2)}, u32[]{:S(2)}) collective-permute-start(bf16[2,64,2048]{2,1,0:T(8,128)(2,1)S(1)} %collective-permute-done.4), channel_id=1, source_target_pairs={{0,4},{4,8},{8,12},{12,16},{16,20},{20,24},{24,28},{28,32},{32,36}... | collective-permute-start | bytes 1572872 | tf_op jit(solution)/shard_map/ppermute | solution.py:21
  123.9 16.1 %collective-permute-start.6 = (bf16[2,64,2048]{2,1,0:T(8,128)(2,1)}, bf16[2,64,2048]{2,1,0:T(8,128)(2,1)}, u32[]{:S(2)}, u32[]{:S(2)}) collective-permute-start(bf16[2,64,2048]{2,1,0:T(8,128)(2,1)} %collective-permute-done.5), channel_id=1, source_target_pairs={{0,4},{4,8},{8,12},{12,16},{16,20},{20,24},{24,28},{28,32},{32,36}... | collective-permute-start | bytes 1572872 | tf_op jit(solution)/shard_map/ppermute | solution.py:21
  126.1 23.0 %copy-start.4 = (bf16[64,2048]{1,0:T(8,128)(2,1)S(1)}, bf16[64,2048]{1,0:T(8,128)(2,1)}, u32[]{:S(2)}) copy-start(bf16[64,2048]{1,0:T(8,128)(2,1)} %param.15) | copy-start | bytes 786436
  126.1 22.9 %copy-start.5 = (bf16[64,2048]{1,0:T(8,128)(2,1)S(1)}, bf16[64,2048]{1,0:T(8,128)(2,1)}, u32[]{:S(2)}) copy-start(bf16[64,2048]{1,0:T(8,128)(2,1)} %param.14) | copy-start | bytes 786436
  392.1 3.4 copy-start.3
  396.1 54.1 %collective-permute-start.7 = (f32[2,64,2048]{2,1,0:T(8,128)S(1)}, f32[2,64,2048]{2,1,0:T(8,128)S(1)}, u32[]{:S(2)}, u32[]{:S(2)}) collective-permute-start(f32[2,64,2048]{2,1,0:T(8,128)S(1)} %pad_maximum_fusion), channel_id=1, source_target_pairs={{4,0},{8,4},{12,8},{16,12},{20,16},{24,20},{28,24},{32,28},{36,32}... | collective-permute-start | bytes 3145736 | tf_op jit(solution)/shard_map/ppermute | solution.py:21
  398.1 87.6 %collective-permute-start.8 = (f32[2,64,2048]{2,1,0:T(8,128)S(1)}, f32[2,64,2048]{2,1,0:T(8,128)S(1)}, u32[]{:S(2)}, u32[]{:S(2)}) collective-permute-start(f32[2,64,2048]{2,1,0:T(8,128)S(1)} %pad_maximum_fusion.1), channel_id=1, source_target_pairs={{8,0},{12,4},{16,8},{20,12},{24,16},{28,20},{32,24},{36,28},{40,32... | collective-permute-start | bytes 3145736 | tf_op jit(solution)/shard_map/ppermute | solution.py:21
  400.2 142.0 %collective-permute-start.9 = (f32[2,64,2048]{2,1,0:T(8,128)S(1)}, f32[2,64,2048]{2,1,0:T(8,128)S(1)}, u32[]{:S(2)}, u32[]{:S(2)}) collective-permute-start(f32[2,64,2048]{2,1,0:T(8,128)S(1)} %pad_maximum_fusion.2), channel_id=1, source_target_pairs={{12,0},{16,4},{20,8},{24,12},{28,16},{32,20},{36,24},{40,28},{44,3... | collective-permute-start | bytes 3145736 | tf_op jit(solution)/shard_map/ppermute | solution.py:21
  402.2 231.4 %collective-permute-start.10 = (f32[2,64,2048]{2,1,0:T(8,128)S(1)}, f32[2,64,2048]{2,1,0:T(8,128)S(1)}, u32[]{:S(2)}, u32[]{:S(2)}) collective-permute-start(f32[2,64,2048]{2,1,0:T(8,128)S(1)} %pad_maximum_fusion.3), channel_id=1, source_target_pairs={{16,0},{20,4},{24,8},{28,12},{32,16},{36,20},{40,24},{44,28},{48,3... | collective-permute-start | bytes 3145736 | tf_op jit(solution)/shard_map/ppermute | solution.py:21
  406.0 351.3 %collective-permute-start.11 = (f32[2,64,2048]{2,1,0:T(8,128)S(1)}, f32[2,64,2048]{2,1,0:T(8,128)S(1)}, u32[]{:S(2)}, u32[]{:S(2)}) collective-permute-start(f32[2,64,2048]{2,1,0:T(8,128)S(1)} %pad_maximum_fusion.4), channel_id=1, source_target_pairs={{20,0},{24,4},{28,8},{32,12},{36,16},{40,20},{44,24},{48,28},{52,3... | collective-permute-start | bytes 3145736 | tf_op jit(solution)/shard_map/ppermute | solution.py:21
  450.2 329.3 %collective-permute-start.12 = (f32[2,64,2048]{2,1,0:T(8,128)S(1)}, f32[2,64,2048]{2,1,0:T(8,128)S(1)}, u32[]{:S(2)}, u32[]{:S(2)}) collective-permute-start(f32[2,64,2048]{2,1,0:T(8,128)S(1)} %pad_maximum_fusion.5), channel_id=1, source_target_pairs={{24,0},{28,4},{32,8},{36,12},{40,16},{44,20},{48,24},{52,28},{56,3... | collective-permute-start | bytes 3145736 | tf_op jit(solution)/shard_map/ppermute | solution.py:21
  485.7 293.8 %collective-permute-start.13 = (f32[2,64,2048]{2,1,0:T(8,128)S(1)}, f32[2,64,2048]{2,1,0:T(8,128)S(1)}, u32[]{:S(2)}, u32[]{:S(2)}) collective-permute-start(f32[2,64,2048]{2,1,0:T(8,128)S(1)} %pad_maximum_fusion.6), channel_id=1, source_target_pairs={{28,0},{32,4},{36,8},{40,12},{44,16},{48,20},{52,24},{56,28},{60,3... | collective-permute-start | bytes 3145736 | tf_op jit(solution)/shard_map/ppermute | solution.py:21
  779.5 1.9 copy-start.1
Sparse Core Ops, SparseCore 0:
  10.4 36.4 all-gather.5
  72.3 38.7 all-gather.7
  392.2 54.3 reduce-scatter.1
where the time goes:
time: 793 us; the launch traced here: 788 us
  waiting for transfers between devices  469 us (59%)
  local copies, waits for them, and re-layouts  177 us (22%)
  matrix products  59.4 us (7%)
  starting transfers between devices  36.7 us (5%)
  blocking collectives  21.3 us (3%)
  between operations  14.2 us (2%)
    ppermute x14, waiting for transfers between devices, shifted(): return lax.ppermute(x, axis, pairs)  469 us
    slice x32, local copies, waits for them, and re-layouts, scores_for(): window[1]  87.2 us
    ppermute x14, starting transfers between devices, shifted(): return lax.ppermute(x, axis, pairs)  36.6 us
    dynamic_slice x32, local copies, waits for them, and re-layouts, scores_for(): lax.dynamic_slice_in_dim(full_grad, kv_head * head_cols, head_cols, 1)  30.6 us
    all_gather x3, blocking collectives, combined_all(): everything = jax.tree.map(lambda part: lax.all_gather(part, axis), x)  21.3 us
    dot_general x16, matrix products, closing_sweep(): jnp.einsum('qrk,rqd->kd', probability_floor, grad_cols, preferred_element...  16.5 us
    dot_general x16, matrix products, closing_sweep(): jnp.einsum('qrk,rqd->kd', blended_rows, query_cols, preferred_element_typ...  16.5 us
  transfers between devices with their start and end apart: 17, of which 13 were waited for; matrix products, arithmetic and copies ran while one was open for 3% of the time, Pallas kernels for 0%

commit v1 on v0

v1 whole, which is shorter than its diff:
```python
import functools
import math

import jax
import jax.numpy as jnp
from jax import lax
from jax.experimental import pallas as pl
from jax.experimental.pallas import tpu as pltpu
from jax.sharding import Mesh
from jax.sharding import PartitionSpec as P

QUERY_HEADS = 32
KEY_VALUE_HEADS = 16
HEAD_SIZE = 128
HEAD_GROUPS = 2
BLOCK = 128
BACK = 14
SPAN = 256
SLAB = 2 * SPAN
HALO = BACK * BLOCK
WINDOW = HALO + SLAB
LOCAL_HEADS = 2
Q_BLOCKS = SLAB // BLOCK
K_BLOCKS = BACK + 1

SCORE_SCALE = 1.0 / 12.0
EXP2_SCALE = SCORE_SCALE * math.log2(math.e)
NEG_LARGE = -1e30

SLAB_AXES = ("y", "z")
MEMBER_AXES = ("xl", "xh", "core")


def slab_shift(x, by):
    count = lax.axis_size(SLAB_AXES)
    return lax.ppermute(x, SLAB_AXES, [(i, (i + by) % count) for i in range(count)])


def dot(a, b, contract):
    return lax.dot_general(a, b, ((contract[0], contract[1]), ((), ())), preferred_element_type=jnp.float32)


def attention_kernel(
    hit_ref, start_ref, q_ref, do_ref, p4_ref, p3_ref, p2_ref, p1_ref, p0_ref, dq_ref, dkv_ref,
    win, s_scr, dp_scr, ds_scr, p_scr,
):
    row = 0
    for piece in (p4_ref, p3_ref, p2_ref, p1_ref, p0_ref):
        rows = piece.shape[0]
        win[row : row + rows, :] = piece[...]
        row += rows
    dkv_ref[...] = jnp.zeros_like(dkv_ref)
    key_iota = lax.broadcasted_iota(jnp.int32, (BLOCK, BLOCK), 0)
    row_iota = lax.broadcasted_iota(jnp.int32, (BLOCK, BLOCK), 1)

    def step(t, carry):
        h = t // Q_BLOCKS
        i = t % Q_BLOCKS
        row0 = pl.multiple_of(i * BLOCK, BLOCK)
        lane0 = pl.multiple_of(h * HEAD_SIZE, HEAD_SIZE)
        vlane0 = pl.multiple_of((h + LOCAL_HEADS) * HEAD_SIZE, HEAD_SIZE)
        qlane0 = pl.multiple_of(h * 2 * HEAD_SIZE, HEAD_SIZE)
        qlane1 = pl.multiple_of(h * 2 * HEAD_SIZE + HEAD_SIZE, HEAD_SIZE)

        def both(ref):
            return jnp.concatenate(
                [
                    ref[pl.ds(row0, BLOCK), pl.ds(qlane0, HEAD_SIZE)],
                    ref[pl.ds(row0, BLOCK), pl.ds(qlane1, HEAD_SIZE)],
                ],
                axis=0,
            )

        qs = both(q_ref)
        dos = both(do_ref)
        start = start_ref[0:1, pl.ds(row0, BLOCK)] - row0

        def keys(w):
            return win[pl.ds(pl.multiple_of(row0 + w * BLOCK, BLOCK), BLOCK), pl.ds(lane0, HEAD_SIZE)]

        def values(w):
            return win[pl.ds(pl.multiple_of(row0 + w * BLOCK, BLOCK), BLOCK), pl.ds(vlane0, HEAD_SIZE)]

        peak = jnp.full((8, 2 * BLOCK), NEG_LARGE, jnp.float32)
        for w in range(K_BLOCKS):
            s = dot(keys(w), qs, ((1,), (1,)))
            if w < BACK:
                bound = jnp.where(hit_ref[i, w] > 0, -1, start - w * BLOCK)
                ok = key_iota >= bound
            else:
                ok = (key_iota >= start - w * BLOCK) & (key_iota <= row_iota)
            ok = jnp.concatenate([ok, ok], axis=1)
            s = jnp.where(ok, s * EXP2_SCALE, NEG_LARGE)
            s_scr[w * BLOCK : (w + 1) * BLOCK, :] = s
            peak = jnp.maximum(peak, jnp.max(s.reshape(BLOCK // 8, 8, 2 * BLOCK), axis=0))
        peak = jnp.max(peak, axis=0, keepdims=True)

        total = jnp.zeros((8, 2 * BLOCK), jnp.float32)
        inner = jnp.zeros((8, 2 * BLOCK), jnp.float32)
        for w in range(K_BLOCKS):
            rows = slice(w * BLOCK, (w + 1) * BLOCK)
            dp = dot(values(w), dos, ((1,), (1,)))
            weight = jnp.exp2(s_scr[rows, :] - peak)
            total += jnp.sum(weight.reshape(BLOCK // 8, 8, 2 * BLOCK), axis=0)
            inner += jnp.sum((weight * dp).reshape(BLOCK // 8, 8, 2 * BLOCK), axis=0)
            s_scr[rows, :] = weight
            dp_scr[rows, :] = dp
        total = jnp.sum(total, axis=0, keepdims=True)
        inner = jnp.sum(inner, axis=0, keepdims=True)
        inverse = 1.0 / total
        delta = inner * inverse
        inverse_scaled = inverse * SCORE_SCALE

        for w in range(K_BLOCKS):
            rows = slice(w * BLOCK, (w + 1) * BLOCK)
            weight = s_scr[rows, :]
            p_scr[rows, :] = (weight * inverse).astype(jnp.bfloat16)
            ds_scr[rows, :] = ((weight * inverse_scaled) * (dp_scr[rows, :] - delta)).astype(jnp.bfloat16)
        dq_t = jnp.zeros((HEAD_SIZE, 2 * BLOCK), jnp.float32)
        for w in range(K_BLOCKS):
            rows = slice(w * BLOCK, (w + 1) * BLOCK)
            out_rows = pl.ds(pl.multiple_of(row0 + w * BLOCK, BLOCK), BLOCK)
            ds = ds_scr[rows, :]
            dkv_ref[out_rows, pl.ds(lane0, HEAD_SIZE)] += dot(ds, qs, ((1,), (0,)))
            dkv_ref[out_rows, pl.ds(vlane0, HEAD_SIZE)] += dot(p_scr[rows, :], dos, ((1,), (0,)))
        window_keys = win[pl.ds(row0, K_BLOCKS * BLOCK), pl.ds(lane0, HEAD_SIZE)]
        dq_t = dot(window_keys, ds_scr[...], ((0,), (0,)))
        dq = dq_t.T
        dq_ref[pl.ds(row0, BLOCK), pl.ds(qlane0, HEAD_SIZE)] = dq[:BLOCK]
        dq_ref[pl.ds(row0, BLOCK), pl.ds(qlane1, HEAD_SIZE)] = dq[BLOCK:]
        return carry

    lax.fori_loop(0, LOCAL_HEADS * Q_BLOCKS, step, 0)


def attention(hit, start, q, do, pieces):
    vmem = pl.BlockSpec(memory_space=pltpu.VMEM)
    smem = pl.BlockSpec(memory_space=pltpu.SMEM)
    keys = K_BLOCKS * BLOCK
    return pl.pallas_call(
        attention_kernel,
        out_shape=(
            jax.ShapeDtypeStruct((SLAB, 4 * HEAD_SIZE), jnp.float32),
            jax.ShapeDtypeStruct((WINDOW, 4 * HEAD_SIZE), jnp.float32),
        ),
        in_specs=[smem] + [vmem] * 8,
        out_specs=(vmem, vmem),
        scratch_shapes=[
            pltpu.VMEM((WINDOW, 4 * HEAD_SIZE), jnp.bfloat16),
            pltpu.VMEM((keys, 2 * BLOCK), jnp.float32),
            pltpu.VMEM((keys, 2 * BLOCK), jnp.float32),
            pltpu.VMEM((keys, 2 * BLOCK), jnp.bfloat16),
            pltpu.VMEM((keys, 2 * BLOCK), jnp.bfloat16),
        ],
        compiler_params=pltpu.CompilerParams(vmem_limit_bytes=48 * 1024 * 1024),
        name="attention",
    )(hit, start, q, do, *pieces)


def per_device(queries, output_gradient, key_states, value_inputs, turn_ids, listed):
    slab = lax.axis_index(SLAB_AXES)
    low = lax.axis_index("xl")
    group = lax.axis_index("xh")
    width = LOCAL_HEADS * HEAD_SIZE

    def by_owner(x):
        return x.reshape(-1, 4, 2, width).transpose(2, 1, 0, 3)

    kv = jnp.concatenate([by_owner(key_states), by_owner(value_inputs)], axis=3)
    kv = kv.reshape(8, key_states.shape[0], 2 * width)
    own = lax.all_to_all(kv, MEMBER_AXES, 0, 0, tiled=True).reshape(SLAB, 2 * width)

    q2 = jnp.stack([queries, output_gradient]).reshape(2, SPAN, 2, 2 * width)
    mine = lax.dynamic_index_in_dim(q2, low, 2, keepdims=False)
    other = lax.dynamic_index_in_dim(q2, 1 - low, 2, keepdims=False)
    other = lax.ppermute(other, "xl", [(0, 1), (1, 0)])
    first = low == 0
    q_do = jnp.concatenate([jnp.where(first, mine, other), jnp.where(first, other, mine)], axis=1)

    p1 = slab_shift(own, 1)
    p2 = slab_shift(p1, 1)
    p3 = slab_shift(p2, 1)
    p4 = slab_shift(p3[SPAN:], 1)

    padded = jnp.concatenate([jnp.full((HALO,), -1, turn_ids.dtype), turn_ids])
    window_turns = lax.dynamic_slice_in_dim(padded, slab * SLAB, WINDOW, 0)
    start = jnp.sum((window_turns[None, :] < window_turns[HALO:, None]).astype(jnp.int32), axis=1)[None, :]
    table = lax.dynamic_index_in_dim(listed, group, 0, keepdims=False)
    table = lax.dynamic_slice_in_dim(table, slab * Q_BLOCKS, Q_BLOCKS, 0)[:, ::-1]
    key_block = slab * Q_BLOCKS - BACK + jnp.arange(Q_BLOCKS)[:, None] + jnp.arange(BACK)[None, :]
    hit = jnp.where(key_block >= 0, table, 0)

    dq, dkv = attention(hit, start, q_do[0], q_do[1], (p4, p3, p2, p1, own))

    part = [dkv[:SPAN]] + [dkv[SPAN + SLAB * k : SPAN + SLAB * (k + 1)] for k in range(4)]
    moving = slab_shift(part[0].astype(jnp.bfloat16), -1).astype(jnp.float32)
    moving = jnp.concatenate([part[1][:SPAN], part[1][SPAN:] + moving], axis=0)
    for k in (2, 3, 4):
        moving = part[k] + slab_shift(moving.astype(jnp.bfloat16), -1).astype(jnp.float32)

    out = lax.all_to_all(moving.reshape(8, -1, 2 * width), MEMBER_AXES, 0, 0, tiled=True)
    out = out.reshape(2, 4, -1, 2, width).transpose(3, 2, 1, 0, 4).reshape(2, -1, KEY_VALUE_HEADS * HEAD_SIZE)

    dq = dq.reshape(2, SPAN, 2 * width)
    mine = lax.dynamic_index_in_dim(dq, low, 0, keepdims=False)
    other = lax.dynamic_index_in_dim(dq, 1 - low, 0, keepdims=False)
    other = lax.ppermute(other, "xl", [(0, 1), (1, 0)])
    grad_queries = jnp.concatenate([jnp.where(first, mine, other), jnp.where(first, other, mine)], axis=1)
    return grad_queries, out[0], out[1]


def solution(mesh):
    y, z, xl, xh, core = 4, 8, 2, 2, 2
    fine = Mesh(mesh.devices.reshape(y, z, xl, xh, core), ("y", "z", "xl", "xh", "core"))
    pb, ka = ("y", "z", "xl"), ("xh", "core")
    in_specs = (P(pb, ka), P(pb, ka), P(pb + ka, None), P(pb + ka, None), P(), P())
    out_specs = (P(pb, ka), P(pb + ka, None), P(pb + ka, None))
    return jax.shard_map(per_device, mesh=fine, in_specs=in_specs, out_specs=out_specs, check_vma=False)
```

time: 793 us -> 175 us (0.22)
  the two profiles are of different devices: /device:TPU:24 before, /device:TPU:1 now
where the time goes in v1:
time: 175 us
  waiting for transfers between devices  90.5 us (52%)
  starting transfers between devices  26.8 us (15%)
  Pallas kernels  24.2 us (14%)
  blocking collectives  14.8 us (8%)
  local copies, waits for them, and re-layouts  10.1 us (6%)
  other arithmetic  7.94 us (5%)
    ppermute x8, waiting for transfers between devices, slab_shift(): lax.ppermute(x, SLAB_AXES, [(i, (i + by) % count) for i in range(count)])  78.1 us
    pallas_call x1, Pallas kernels, attention(): pl.pallas_call(attention_kernel, out_shape=(jax.ShapeDtypeStruct((SLAB, 4...  24.2 us
    all_to_all x1, blocking collectives, per_device(): lax.all_to_all(kv, MEMBER_AXES, 0, 0, tiled=True).reshape(SLAB, 2 * width)  14.8 us
    ppermute x8, starting transfers between devices, slab_shift(): lax.ppermute(x, SLAB_AXES, [(i, (i + by) % count) for i in range(count)])  14.2 us
    all_to_all x1, starting transfers between devices, per_device(): lax.all_to_all(moving.reshape(8, -1, 2 * width), MEMBER_AXES, 0, 0, tiled...  12.5 us
    all_to_all x1, waiting for transfers between devices, per_device(): lax.all_to_all(moving.reshape(8, -1, 2 * width), MEMBER_AXES, 0, 0, tiled...  12.4 us
  transfers between devices with their start and end apart: 11, of which 9 were waited for; matrix products, arithmetic and copies ran while one was open for 4% of the time, Pallas kernels for 0%

profile of v1, /device:TPU:1, one launch (start us, length us, event | category | flops | bytes accessed | tf_op | source)
XLA Modules:
  0.0 175.2 jit_solution(16674749616272790290)
XLA Ops:
  0.7 1.2 reshape.45
  1.9 1.1 reshape.46
  3.0 0.5 pad_maximum_fusion.2
  3.5 0.2 copy.17
  3.6 14.8 %all_to_all.10 = bf16[8,64,512]{2,1,0:T(8,128)(2,1)S(1)} all-to-all(bf16[8,64,512]{2,1,0:T(8,128)(2,1)S(1)} %bitcast.31), channel_id=1, replica_groups=mesh['y'=4,'z'=8,'xl'=2,'xh'=2,'core'=2] {'xl','xh','core'}, dimensions={0} | all-to-all | bytes 1048576 | tf_op jit(solution)/shard_map/all_to_all | solution.py:171
  18.5 1.6 collective-permute-start.1
  20.1 1.4 stack.9
  21.5 0.4 stack.10
  21.9 0.1 copy_dynamic-update-slice_fusion.1
  22.0 15.9 %collective-permute-done.1.p1_ref = bf16[512,512]{1,0:T(8,128)(2,1)S(1)} collective-permute-done((bf16[512,512]{1,0:T(8,128)(2,1)S(1)}, bf16[512,512]{1,0:T(8,128)(2,1)S(1)}, u32[]{:S(2)}, u32[]{:S(2)}) %collective-permute-start.1) | collective-permute-done | bytes 524320 | tf_op jit(solution)/shard_map/ppermute | solution.py:36
  37.9 0.8 dynamic-slice_bitcast_fusion.1
  38.8 0.1 pad_dynamic-slice_fusion
  38.9 0.1 constant_dynamic-slice_fusion
  39.0 14.2 %collective-permute-done.2.p2_ref = bf16[512,512]{1,0:T(8,128)(2,1)S(1)} collective-permute-done((bf16[512,512]{1,0:T(8,128)(2,1)S(1)}, bf16[512,512]{1,0:T(8,128)(2,1)S(1)}, u32[]{:S(2)}, u32[]{:S(2)}) %collective-permute-start.2) | collective-permute-done | bytes 524320 | tf_op jit(solution)/shard_map/ppermute | solution.py:36
  53.2 0.1 copy.14
  53.3 0.1 rev.3
  53.4 0.1 pad_dynamic-slice_fusion.1
  53.4 0.7 convert_reduce_fusion
  54.1 0.1 fusion.3.hit_ref
  54.2 13.4 %collective-permute-done.3.p3_ref = bf16[512,512]{1,0:T(8,128)(2,1)S(1)} collective-permute-done((bf16[512,512]{1,0:T(8,128)(2,1)S(1)}, bf16[512,512]{1,0:T(8,128)(2,1)S(1)}, u32[]{:S(2)}, u32[]{:S(2)}) %collective-permute-start.3) | collective-permute-done | bytes 524320 | tf_op jit(solution)/shard_map/ppermute | solution.py:36
  67.6 0.1 collective-permute-start.4
  67.7 1.1 bitcast_select_fusion.2
  68.8 0.1 fusion.2
  68.9 7.3 %collective-permute-done.4.p4_ref = bf16[256,512]{1,0:T(8,128)(2,1)S(1)} collective-permute-done((bf16[256,512]{1,0:T(8,128)(2,1)S(1)}, bf16[256,512]{1,0:T(8,128)(2,1)S(1)}, u32[]{:S(2)}, u32[]{:S(2)}) %collective-permute-start.4) | collective-permute-done | bytes 262176 | tf_op jit(solution)/shard_map/ppermute | solution.py:36
  76.2 24.2 %attention.1 = (f32[512,512]{1,0:T(8,128)S(1)}, f32[2304,512]{1,0:T(8,128)}) custom-call(s32[4,14]{1,0:T(4,128)S(1)} %fusion.3.hit_ref, s32[1,512]{1,0:T(1,128)S(1)} %bitcast.29, bf16[512,512]{1,0:T(8,128)(2,1)S(1)} %get-tuple-element.16.q_ref, bf16[512,512]{1,0:T(8,128)(2,1)S(1)} %get-tuple-element.15.do_ref, ...), custom_call_target="tpu_custom_call" | custom-call | tf_op jit(solution)/shard_map/attention/pallas_call | solution.py:140
  100.4 2.8 %convert.8 = bf16[2304,512]{1,0:T(8,128)(2,1)S(1)} convert(f32[2304,512]{1,0:T(8,128)} %get-tuple-element.6) | non-fusion elementwise | flops 1179648 | bytes 7077888 | tf_op jit(solution)/shard_map/convert.2
  103.2 0.1 collective-permute-start.6
  103.3 5.2 %collective-permute-done.6 = bf16[256,512]{1,0:T(8,128)(2,1)S(1)} collective-permute-done((bf16[256,512]{1,0:T(8,128)(2,1)S(1)}, bf16[256,512]{1,0:T(8,128)(2,1)S(1)}, u32[]{:S(2)}, u32[]{:S(2)}) %collective-permute-start.6) | collective-permute-done | bytes 262176 | tf_op jit(solution)/shard_map/ppermute | solution.py:36
  108.5 0.1 add_convert_fusion.2
  108.6 3.4 %collective-permute-start.7 = (bf16[512,512]{1,0:T(8,128)(2,1)S(1)}, bf16[512,512]{1,0:T(8,128)(2,1)S(1)}, u32[]{:S(2)}, u32[]{:S(2)}) collective-permute-start(bf16[512,512]{1,0:T(8,128)(2,1)S(1)} %pad_maximum_fusion.3), channel_id=1, source_target_pairs={{0,248},{8,0},{16,8},{24,16},{32,24},{40,32},{48,40},{56,48},{64,5... | collective-permute-start | bytes 1572872 | tf_op jit(solution)/shard_map/ppermute | solution.py:36
  112.1 7.0 %collective-permute-done.7 = bf16[512,512]{1,0:T(8,128)(2,1)S(1)} collective-permute-done((bf16[512,512]{1,0:T(8,128)(2,1)S(1)}, bf16[512,512]{1,0:T(8,128)(2,1)S(1)}, u32[]{:S(2)}, u32[]{:S(2)}) %collective-permute-start.7) | collective-permute-done | bytes 524320 | tf_op jit(solution)/shard_map/ppermute | solution.py:36
  119.1 0.2 add_convert_fusion.1
  119.2 4.6 %collective-permute-start.8 = (bf16[512,512]{1,0:T(8,128)(2,1)S(1)}, bf16[512,512]{1,0:T(8,128)(2,1)S(1)}, u32[]{:S(2)}, u32[]{:S(2)}) collective-permute-start(bf16[512,512]{1,0:T(8,128)(2,1)S(1)} %add_convert_fusion.1), channel_id=1, source_target_pairs={{0,248},{8,0},{16,8},{24,16},{32,24},{40,32},{48,40},{56,48},{64,5... | collective-permute-start | bytes 1572872 | tf_op jit(solution)/shard_map/ppermute | solution.py:36
  123.8 7.0 %collective-permute-done.8 = bf16[512,512]{1,0:T(8,128)(2,1)S(1)} collective-permute-done((bf16[512,512]{1,0:T(8,128)(2,1)S(1)}, bf16[512,512]{1,0:T(8,128)(2,1)S(1)}, u32[]{:S(2)}, u32[]{:S(2)}) %collective-permute-start.8) | collective-permute-done | bytes 524320 | tf_op jit(solution)/shard_map/ppermute | solution.py:36
  130.8 0.2 add_convert_fusion
  131.0 4.5 %collective-permute-start.9 = (bf16[512,512]{1,0:T(8,128)(2,1)S(1)}, bf16[512,512]{1,0:T(8,128)(2,1)S(1)}, u32[]{:S(2)}, u32[]{:S(2)}) collective-permute-start(bf16[512,512]{1,0:T(8,128)(2,1)S(1)} %add_convert_fusion), channel_id=1, source_target_pairs={{0,248},{8,0},{16,8},{24,16},{32,24},{40,32},{48,40},{56,48},{64,5... | collective-permute-start | bytes 1572872 | tf_op jit(solution)/shard_map/ppermute | solution.py:36
  135.5 0.1 collective-permute-start.5
  135.6 8.1 %collective-permute-done.9 = bf16[512,512]{1,0:T(8,128)(2,1)S(1)} collective-permute-done((bf16[512,512]{1,0:T(8,128)(2,1)S(1)}, bf16[512,512]{1,0:T(8,128)(2,1)S(1)}, u32[]{:S(2)}, u32[]{:S(2)}) %collective-permute-start.9) | collective-permute-done | bytes 524320 | tf_op jit(solution)/shard_map/ppermute | solution.py:36
  143.6 1.1 convert_add_fusion
  144.8 12.5 %all-to-all-start.1 = ((f32[8,64,512]{2,1,0:T(8,128)}), f32[8,64,512]{2,1,0:T(8,128)S(1)}, u32[]{:S(2)}, u32[]{:S(2)}) async-start(f32[8,64,512]{2,1,0:T(8,128)} %bitcast.13), calls=%async_computation.1 | async-start | bytes 2097152 | tf_op jit(solution)/shard_map/all_to_all | solution.py:201
  157.3 0.1 bitcast_select_fusion.1
  157.4 1.1 pad_maximum_fusion
  158.5 12.4 %all-to-all-done.1 = f32[8,64,512]{2,1,0:T(8,128)S(1)} async-done(((f32[8,64,512]{2,1,0:T(8,128)}), f32[8,64,512]{2,1,0:T(8,128)S(1)}, u32[]{:S(2)}, u32[]{:S(2)}) %all-to-all-start.1) | async-done | bytes 1048608 | tf_op jit(solution)/shard_map/all_to_all | solution.py:201
  170.9 0.7 reshape.51
  171.6 0.8 copy.22
  172.4 0.4 fusion.5
  172.7 1.2 squeeze.35
  174.0 1.2 squeeze.34
  (19 shorter events, 0.2 us)
Async XLA Ops:
  0.6 38.2 %copy-start = (s32[2,128,14]{1,0,2:T(2,128)S(1)}, s32[2,128,14]{1,0,2:T(2,128)}, u32[]{:S(2)}) copy-start(s32[2,128,14]{1,0,2:T(2,128)} %param.11) | copy-start | bytes 43012
  0.6 20.9 %copy-start.2 = (bf16[256,1024]{1,0:T(8,128)(2,1)S(1)}, bf16[256,1024]{1,0:T(8,128)(2,1)}, u32[]{:S(2)}) copy-start(bf16[256,1024]{1,0:T(8,128)(2,1)} %param.7) | copy-start | bytes 1572868
  0.7 38.1 %copy-start.3 = (s32[16384]{0:T(1024)S(1)}, s32[16384]{0:T(1024)}, u32[]{:S(2)}) copy-start(s32[16384]{0:T(1024)} %param.10) | copy-start | bytes 196612
  18.5 19.4 %collective-permute-start.1 = (bf16[512,512]{1,0:T(8,128)(2,1)S(1)}, bf16[512,512]{1,0:T(8,128)(2,1)S(1)}, u32[]{:S(2)}, u32[]{:S(2)}) collective-permute-start(bf16[512,512]{1,0:T(8,128)(2,1)S(1)} %bitcast.25), channel_id=1, source_target_pairs={{0,8},{8,16},{16,24},{24,32},{32,40},{40,48},{48,56},{56,64},{64,7... | collective-permute-start | bytes 1572872 | tf_op jit(solution)/shard_map/ppermute | solution.py:36
  37.9 15.3 %collective-permute-start.2 = (bf16[512,512]{1,0:T(8,128)(2,1)S(1)}, bf16[512,512]{1,0:T(8,128)(2,1)S(1)}, u32[]{:S(2)}, u32[]{:S(2)}) collective-permute-start(bf16[512,512]{1,0:T(8,128)(2,1)S(1)} %collective-permute-done.1.p1_ref), channel_id=1, source_target_pairs={{0,8},{8,16},{16,24},{24,32},{32,40},{40,48},{48,56},{56,64},{64,7... | collective-permute-start | bytes 1572872 | tf_op jit(solution)/shard_map/ppermute | solution.py:36
  38.8 28.9 %collective-permute-start = (bf16[2,256,512]{2,1,0:T(8,128)(2,1)}, bf16[2,256,512]{2,1,0:T(8,128)(2,1)}, u32[]{:S(2)}, u32[]{:S(2)}) collective-permute-start(bf16[2,256,512]{2,1,0:T(8,128)(2,1)} %dynamic-slice_bitcast_fusion.1), channel_id=1, source_target_pairs={{0,4},{4,0},{1,5},{5,1},{2,6},{6,2},{3,7},{7,3},{8,12},{12,8},{9,1... | collective-permute-start | bytes 1572872 | tf_op jit(solution)/shard_map/ppermute | solution.py:176
  53.2 14.4 %collective-permute-start.3 = (bf16[512,512]{1,0:T(8,128)(2,1)S(1)}, bf16[512,512]{1,0:T(8,128)(2,1)S(1)}, u32[]{:S(2)}, u32[]{:S(2)}) collective-permute-start(bf16[512,512]{1,0:T(8,128)(2,1)S(1)} %collective-permute-done.2.p2_ref), channel_id=1, source_target_pairs={{0,8},{8,16},{16,24},{24,32},{32,40},{40,48},{48,56},{56,64},{64,7... | collective-permute-start | bytes 1572872 | tf_op jit(solution)/shard_map/ppermute | solution.py:36
  67.6 8.6 %collective-permute-start.4 = (bf16[256,512]{1,0:T(8,128)(2,1)S(1)}, bf16[256,512]{1,0:T(8,128)(2,1)S(1)}, u32[]{:S(2)}, u32[]{:S(2)}) collective-permute-start(bf16[256,512]{1,0:T(8,128)(2,1)S(1)} %slice.57), channel_id=1, source_target_pairs={{0,8},{8,16},{16,24},{24,32},{32,40},{40,48},{48,56},{56,64},{64,7... | collective-permute-start | bytes 786440 | tf_op jit(solution)/shard_map/ppermute | solution.py:36
  100.4 8.2 %copy-start.1 = (f32[2304,512]{1,0:T(8,128)S(1)}, f32[2304,512]{1,0:T(8,128)}, u32[]{:S(2)}) copy-start(f32[2304,512]{1,0:T(8,128)} %get-tuple-element.6) | copy-start | bytes 14155780
  103.2 5.3 %collective-permute-start.6 = (bf16[256,512]{1,0:T(8,128)(2,1)S(1)}, bf16[256,512]{1,0:T(8,128)(2,1)S(1)}, u32[]{:S(2)}, u32[]{:S(2)}) collective-permute-start(bf16[256,512]{1,0:T(8,128)(2,1)S(1)} %get-tuple-element.8), channel_id=1, source_target_pairs={{0,248},{8,0},{16,8},{24,16},{32,24},{40,32},{48,40},{56,48},{64,5... | collective-permute-start | bytes 786440 | tf_op jit(solution)/shard_map/ppermute | solution.py:36
  108.6 10.4 %collective-permute-start.7 = (bf16[512,512]{1,0:T(8,128)(2,1)S(1)}, bf16[512,512]{1,0:T(8,128)(2,1)S(1)}, u32[]{:S(2)}, u32[]{:S(2)}) collective-permute-start(bf16[512,512]{1,0:T(8,128)(2,1)S(1)} %pad_maximum_fusion.3), channel_id=1, source_target_pairs={{0,248},{8,0},{16,8},{24,16},{32,24},{40,32},{48,40},{56,48},{64,5... | collective-permute-start | bytes 1572872 | tf_op jit(solution)/shard_map/ppermute | solution.py:36
  119.2 11.6 %collective-permute-start.8 = (bf16[512,512]{1,0:T(8,128)(2,1)S(1)}, bf16[512,512]{1,0:T(8,128)(2,1)S(1)}, u32[]{:S(2)}, u32[]{:S(2)}) collective-permute-start(bf16[512,512]{1,0:T(8,128)(2,1)S(1)} %add_convert_fusion.1), channel_id=1, source_target_pairs={{0,248},{8,0},{16,8},{24,16},{32,24},{40,32},{48,40},{56,48},{64,5... | collective-permute-start | bytes 1572872 | tf_op jit(solution)/shard_map/ppermute | solution.py:36
  131.0 12.7 %collective-permute-start.9 = (bf16[512,512]{1,0:T(8,128)(2,1)S(1)}, bf16[512,512]{1,0:T(8,128)(2,1)S(1)}, u32[]{:S(2)}, u32[]{:S(2)}) collective-permute-start(bf16[512,512]{1,0:T(8,128)(2,1)S(1)} %add_convert_fusion), channel_id=1, source_target_pairs={{0,248},{8,0},{16,8},{24,16},{32,24},{40,32},{48,40},{56,48},{64,5... | collective-permute-start | bytes 1572872 | tf_op jit(solution)/shard_map/ppermute | solution.py:36
  135.5 21.8 %collective-permute-start.5 = (f32[256,512]{1,0:T(8,128)S(1)}, f32[256,512]{1,0:T(8,128)S(1)}, u32[]{:S(2)}, u32[]{:S(2)}) collective-permute-start(f32[256,512]{1,0:T(8,128)S(1)} %dynamic-slice_bitcast_fusion), channel_id=1, source_target_pairs={{0,4},{4,0},{1,5},{5,1},{2,6},{6,2},{3,7},{7,3},{8,12},{12,8},{9,1... | collective-permute-start | bytes 1572872 | tf_op jit(solution)/shard_map/ppermute | solution.py:207
  144.8 26.1 %all-to-all-start.1 = ((f32[8,64,512]{2,1,0:T(8,128)}), f32[8,64,512]{2,1,0:T(8,128)S(1)}, u32[]{:S(2)}, u32[]{:S(2)}) async-start(f32[8,64,512]{2,1,0:T(8,128)} %bitcast.13), calls=%async_computation.1 | async-start | bytes 2097152 | tf_op jit(solution)/shard_map/all_to_all | solution.py:201

commit v2 on v1

v2 whole, which is shorter than its diff:
```python
import functools
import math

import jax
import jax.numpy as jnp
from jax import lax
from jax.experimental import pallas as pl
from jax.experimental.pallas import tpu as pltpu
from jax.sharding import Mesh
from jax.sharding import PartitionSpec as P

KEY_VALUE_HEADS = 16
HEAD_SIZE = 128
BLOCK = 128
BACK = 14
SPAN = 256
SLAB = 2 * SPAN
HALO = BACK * BLOCK
WINDOW = HALO + SLAB
LOCAL_HEADS = 2
WIDTH = LOCAL_HEADS * HEAD_SIZE
Q_BLOCKS = SLAB // BLOCK
PAIR = 2 * BLOCK
ROWS = Q_BLOCKS * PAIR

SCORE_SCALE = 1.0 / 12.0
EXP2_SCALE = SCORE_SCALE * math.log2(math.e)
NEG_LARGE = -1e30

SLAB_AXES = ("y", "z")
MEMBER_AXES = ("xl", "xh", "core")

VMEM_SPEC = pl.BlockSpec(memory_space=pltpu.VMEM)
SMEM_SPEC = pl.BlockSpec(memory_space=pltpu.SMEM)


def slab_shift(x, by):
    count = lax.axis_size(SLAB_AXES)
    return lax.ppermute(x, SLAB_AXES, [(i, i + by) for i in range(count) if 0 <= i + by < count])


def low_swap(x):
    return lax.ppermute(x, "xl", [(0, 1), (1, 0)])


def dot(a, b, da, db):
    return lax.dot_general(a, b, (((da,), (db,)), ((), ())), preferred_element_type=jnp.float32)


def call(kernel, name, out_shape, in_specs, scratch=(), aliases=None):
    outs = out_shape if isinstance(out_shape, (tuple, list)) else (out_shape,)
    size = sum(o.size * o.dtype.itemsize for o in outs)
    return pl.pallas_call(
        kernel,
        out_shape=out_shape,
        in_specs=in_specs,
        out_specs=jax.tree.map(lambda _: VMEM_SPEC, out_shape),
        scratch_shapes=scratch,
        input_output_aliases=aliases or {},
        compiler_params=pltpu.CompilerParams(vmem_limit_bytes=32 * 1024 * 1024),
        cost_estimate=pl.CostEstimate(flops=1024, bytes_accessed=size, transcendentals=0),
        name=name,
    )


def f32(*shape):
    return jax.ShapeDtypeStruct(shape, jnp.float32)


def bf16(*shape):
    return jax.ShapeDtypeStruct(shape, jnp.bfloat16)


def owner_columns(d):
    return (d % 4 * 4 + d // 4 * 2) * HEAD_SIZE


def pack_kernel(k_ref, v_ref, out_ref, k_scr, v_scr, sems):
    copies = [pltpu.make_async_copy(k_ref, k_scr, sems.at[0]), pltpu.make_async_copy(v_ref, v_scr, sems.at[1])]
    for copy in copies:
        copy.start()
    for n, (copy, scr) in enumerate(zip(copies, (k_scr, v_scr))):
        copy.wait()
        for d in range(8):
            c = owner_columns(d)
            out_ref[d, :, n * WIDTH : (n + 1) * WIDTH] = scr[:, c : c + WIDTH]


def unpack_kernel(in_ref, dk_ref, dv_ref):
    for d in range(8):
        c = owner_columns(d)
        dk_ref[:, c : c + WIDTH] = in_ref[d, :, :WIDTH].astype(jnp.float32)
        dv_ref[:, c : c + WIDTH] = in_ref[d, :, WIDTH:].astype(jnp.float32)


def rows_kernel(low_ref, q_ref, do_ref, other_ref, qr_ref, dor_ref):
    low = low_ref[0]
    for x, (src, dst) in enumerate(((q_ref, qr_ref), (do_ref, dor_ref))):
        for h in range(LOCAL_HEADS):
            for b in range(2):
                for n in range(2):
                    c = h * PAIR + n * BLOCK
                    rows = slice(b * BLOCK, (b + 1) * BLOCK)
                    here = pl.multiple_of((2 * low + b) * PAIR + n * BLOCK, BLOCK)
                    there = pl.multiple_of((2 * (1 - low) + b) * PAIR + n * BLOCK, BLOCK)
                    lane = pl.multiple_of(low * 2 * WIDTH + c, BLOCK)
                    dst[h, pl.ds(here, BLOCK), :] = src[rows, pl.ds(lane, BLOCK)]
                    dst[h, pl.ds(there, BLOCK), :] = other_ref[x, rows, c : c + BLOCK]


def columns_kernel(low_ref, mine_ref, other_ref, out_ref):
    low = low_ref[0]
    out_ref[:, pl.ds(pl.multiple_of(low * 2 * WIDTH, BLOCK), 2 * WIDTH)] = mine_ref[...]
    out_ref[:, pl.ds(pl.multiple_of((1 - low) * 2 * WIDTH, BLOCK), 2 * WIDTH)] = other_ref[...]


def visible(i, w):
    return i <= w <= i + BACK


def mask_of(hit_ref, start_ref, i, w):
    key_iota = lax.broadcasted_iota(jnp.int32, (BLOCK, BLOCK), 0)
    bound = start_ref[0:1, i * BLOCK : (i + 1) * BLOCK] - w * BLOCK
    if w < i + BACK:
        ok = key_iota >= jnp.where(hit_ref[i, w - i] > 0, -1, bound)
    else:
        ok = (key_iota >= bound) & (key_iota <= lax.broadcasted_iota(jnp.int32, (BLOCK, BLOCK), 1))
    return jnp.concatenate([ok, ok], axis=1)


def fold(x, op):
    return op(x.reshape(BLOCK // 8, 8, PAIR), axis=0)


def stats_kernel(first_blocks, opening, closing, *refs):
    count = len(first_blocks)
    hit_ref, start_ref, q_ref, do_ref = refs[:4]
    pieces = refs[4 : 4 + count]
    rest = refs[4 + count :]
    if opening:
        state_in, rest = None, rest
    else:
        state_in, rest = rest[0], rest[1:]
    out_ref, s_scr = rest
    for h in range(LOCAL_HEADS):
        for i in range(Q_BLOCKS):
            lanes = slice(i * PAIR, (i + 1) * PAIR)
            qs = q_ref[h, lanes, :]
            dos = do_ref[h, lanes, :]
            if opening:
                top = jnp.full((8, PAIR), NEG_LARGE, jnp.float32)
                total = jnp.zeros((8, PAIR), jnp.float32)
                inner = jnp.zeros((8, PAIR), jnp.float32)
            else:
                top, total, inner = (state_in[h, n, :, lanes] for n in range(3))
            todo = []
            for ref, first in zip(pieces, first_blocks):
                seen = [w for w in (first, first + 1) if visible(i, w)]
                if seen:
                    todo.append((ref, seen, (seen[0] - first) * BLOCK))
            peak = top
            at = 0
            for ref, seen, row in todo:
                s = dot(ref[row : row + len(seen) * BLOCK, h * HEAD_SIZE : (h + 1) * HEAD_SIZE], qs, 1, 1)
                for n, w in enumerate(seen):
                    x = jnp.where(
                        mask_of(hit_ref, start_ref, i, w), s[n * BLOCK : (n + 1) * BLOCK] * EXP2_SCALE, NEG_LARGE
                    )
                    s_scr[h * Q_BLOCKS + i, at : at + BLOCK, :] = x
                    peak = jnp.maximum(peak, fold(x, jnp.max))
                    at += BLOCK
            if todo and not opening:
                factor = jnp.exp2(top - peak)
                total = total * factor
                inner = inner * factor
            at = 0
            for ref, seen, row in todo:
                dp = dot(
                    ref[row : row + len(seen) * BLOCK, WIDTH + h * HEAD_SIZE : WIDTH + (h + 1) * HEAD_SIZE], dos, 1, 1
                )
                for n, w in enumerate(seen):
                    x = s_scr[h * Q_BLOCKS + i, at : at + BLOCK, :].reshape(BLOCK // 8, 8, PAIR)
                    weight = jnp.exp2(x - peak[None])
                    total = total + jnp.sum(weight, axis=0)
                    inner = inner + jnp.sum(weight * dp[n * BLOCK : (n + 1) * BLOCK].reshape(BLOCK // 8, 8, PAIR), axis=0)
                    at += BLOCK
            if closing:
                top = jnp.max(peak, axis=0, keepdims=True)
                factor = jnp.exp2(peak - top)
                total = jnp.sum(total * factor, axis=0, keepdims=True)
                inner = jnp.sum(inner * factor, axis=0, keepdims=True)
                out_ref[h, 0:1, lanes] = top + jnp.log2(total)
                out_ref[h, 1:2, lanes] = inner / total
            else:
                out_ref[h, 0, :, lanes] = peak
                out_ref[h, 1, :, lanes] = total
                out_ref[h, 2, :, lanes] = inner


def stats(first_blocks, tables, pieces, state, closing):
    opening = state is None
    shape = f32(LOCAL_HEADS, 8, ROWS) if closing else f32(LOCAL_HEADS, 3, 8, ROWS)
    return call(
        functools.partial(stats_kernel, first_blocks, opening, closing),
        "stats",
        shape,
        [SMEM_SPEC] + [VMEM_SPEC] * (3 + len(pieces) + (not opening)),
        scratch=[pltpu.VMEM((LOCAL_HEADS * Q_BLOCKS, 2 * BLOCK * len(pieces), PAIR), jnp.float32)],
    )(*tables, *pieces, *(() if opening else (state,)))


def grads_kernel(first_blocks, opening, closing, *refs):
    count = len(first_blocks)
    span = 2 * BLOCK
    if closing:
        low_ref, refs = refs[0], refs[1:]
    hit_ref, start_ref, q_ref, do_ref, norm_ref = refs[:5]
    pieces = refs[5 : 5 + count]
    rest = refs[5 + count :]
    if not opening:
        dqt_in, rest = rest[0], rest[1:]
    joined = first_blocks[-1] == BACK + 2
    if joined:
        out_refs, rest = [rest[0].at[n * span : (n + 1) * span] for n in range(count)], rest[1:]
    else:
        out_refs, rest = rest[:count], rest[count:]
    if closing:
        mine_ref, send_ref, p_scr, ds_scr, dq_scr = rest
    else:
        dqt_out, p_scr, ds_scr = rest
    for h in range(LOCAL_HEADS):
        kcols = slice(h * HEAD_SIZE, (h + 1) * HEAD_SIZE)
        vcols = slice(WIDTH + h * HEAD_SIZE, WIDTH + (h + 1) * HEAD_SIZE)
        last_row = 0
        for i in range(Q_BLOCKS):
            lanes = slice(i * PAIR, (i + 1) * PAIR)
            qs = q_ref[h, lanes, :]
            dos = do_ref[h, lanes, :]
            norm = norm_ref[h, 0:1, lanes]
            delta = norm_ref[h, 1:2, lanes]
            for m, (ref, first) in enumerate(zip(pieces, first_blocks)):
                seen = [w for w in (first, first + 1) if visible(i, w)]
                for w in (first, first + 1):
                    if w not in seen:
                        at = slice(m * span + (w - first) * BLOCK, m * span + (w - first + 1) * BLOCK)
                        p_scr[h, at, lanes] = jnp.zeros((BLOCK, PAIR), jnp.bfloat16)
                        ds_scr[h, at, lanes] = jnp.zeros((BLOCK, PAIR), jnp.bfloat16)
                if not seen:
                    continue
                row = (seen[0] - first) * BLOCK
                rows = slice(row, row + len(seen) * BLOCK)
                s = dot(ref[rows, kcols], qs, 1, 1)
                dp = dot(ref[rows, vcols], dos, 1, 1)
                for n, w in enumerate(seen):
                    part = slice(n * BLOCK, (n + 1) * BLOCK)
                    x = jnp.where(mask_of(hit_ref, start_ref, i, w), s[part] * EXP2_SCALE - norm, NEG_LARGE)
                    prob = jnp.exp2(x)
                    at = slice(m * span + (w - first) * BLOCK, m * span + (w - first + 1) * BLOCK)
                    p_scr[h, at, lanes] = prob.astype(jnp.bfloat16)
                    ds_scr[h, at, lanes] = ((prob * SCORE_SCALE) * (dp[part] - delta)).astype(jnp.bfloat16)
        keys = [ref[:, kcols] for ref in pieces]
        keys = keys[0] if count == 1 else jnp.concatenate(keys, axis=0)
        ds = ds_scr[h]
        dv = dot(p_scr[h], do_ref[h], 1, 0)
        dk = dot(ds, q_ref[h], 1, 0)
        dqt = dot(keys, ds, 0, 0)
        if not opening:
            dqt = dqt + dqt_in[h]
        for m, out in enumerate(out_refs):
            out[:, kcols] = dk[m * span : (m + 1) * span].astype(out.dtype)
            out[:, vcols] = dv[m * span : (m + 1) * span].astype(out.dtype)
        if closing:
            for b in range(2 * Q_BLOCKS):
                c = h * PAIR + (b % 2) * BLOCK
                dq_scr[b // 2 * BLOCK : (b // 2 + 1) * BLOCK, c : c + BLOCK] = dqt[:, b * BLOCK : (b + 1) * BLOCK].T
        else:
            dqt_out[h] = dqt
    if closing:
        low = low_ref[0]
        mine_ref[...] = dq_scr[pl.ds(pl.multiple_of(low * SPAN, SPAN), SPAN), :]
        send_ref[...] = dq_scr[pl.ds(pl.multiple_of((1 - low) * SPAN, SPAN), SPAN), :]


def grads(first_blocks, tables, norm, pieces, dqt, dtypes, low=None):
    opening, closing = dqt is None, low is not None
    count = len(pieces)
    rows = SPAN * count // len(dtypes)
    outs = [jax.ShapeDtypeStruct((rows, 2 * WIDTH), d) for d in dtypes]
    outs += [f32(SPAN, 2 * WIDTH)] * 2 if closing else [f32(LOCAL_HEADS, HEAD_SIZE, ROWS)]
    scratch = [pltpu.VMEM((LOCAL_HEADS, SPAN * count, ROWS), jnp.bfloat16)] * 2
    if closing:
        scratch.append(pltpu.VMEM((SLAB, 2 * WIDTH), jnp.float32))
    operands = tables + (norm,) + tuple(pieces) + (() if opening else (dqt,))
    specs = [SMEM_SPEC] + [VMEM_SPEC] * (len(operands) - 1)
    if closing:
        operands, specs = (low,) + operands, [SMEM_SPEC] + specs
    aliases = {} if opening or closing else {len(operands) - 1: len(dtypes)}
    return call(
        functools.partial(grads_kernel, first_blocks, opening, closing),
        "grads",
        tuple(outs),
        specs,
        scratch=scratch,
        aliases=aliases,
    )(*operands)


def per_device(queries, output_gradient, key_states, value_inputs, turn_ids, listed):
    slab = lax.axis_index(SLAB_AXES)
    low = lax.axis_index("xl")
    group = lax.axis_index("xh")
    low_ref = low.reshape(1)

    kv = pl.pallas_call(
        pack_kernel,
        out_shape=bf16(8, SPAN // 4, 2 * WIDTH),
        in_specs=[pl.BlockSpec(memory_space=pl.ANY)] * 2,
        out_specs=VMEM_SPEC,
        scratch_shapes=[pltpu.VMEM((SPAN // 4, KEY_VALUE_HEADS * HEAD_SIZE), jnp.bfloat16)] * 2
        + [pltpu.SemaphoreType.DMA((2,))],
        name="pack",
    )(key_states, value_inputs)
    own = lax.all_to_all(kv, MEMBER_AXES, 0, 0, tiled=True)
    b0 = own[4:].reshape(SPAN, 2 * WIDTH)
    a0 = own[:4].reshape(SPAN, 2 * WIDTH)

    b1 = slab_shift(b0, 1)
    a1 = slab_shift(a0, 1)
    b2 = slab_shift(b1, 1)
    a2 = slab_shift(a1, 1)
    send = jnp.stack(
        [lax.dynamic_slice_in_dim(x, (1 - low) * 2 * WIDTH, 2 * WIDTH, 1) for x in (queries, output_gradient)]
    )
    other = low_swap(send)
    q, do = call(
        rows_kernel, "rows", (bf16(LOCAL_HEADS, ROWS, HEAD_SIZE),) * 2, [SMEM_SPEC] + [VMEM_SPEC] * 3
    )(low_ref, queries, output_gradient, other)

    padded = jnp.concatenate([jnp.full((HALO,), -1, turn_ids.dtype), turn_ids])
    window_turns = lax.dynamic_slice_in_dim(padded, slab * SLAB, WINDOW, 0)
    start = jnp.sum((window_turns[None, :] < window_turns[HALO:, None]).astype(jnp.int32), axis=1)[None, :]
    table = lax.dynamic_index_in_dim(listed, group, 0, keepdims=False)
    table = lax.dynamic_slice_in_dim(table, slab * Q_BLOCKS, Q_BLOCKS, 0)[:, ::-1]
    key_block = slab * Q_BLOCKS - BACK + jnp.arange(Q_BLOCKS)[:, None] + jnp.arange(BACK)[None, :]
    hit = jnp.where(key_block >= 0, table, 0)
    tables = (hit, start, q, do)

    state = stats((14, 16, 10, 12), tables, (a0, b0, a1, b1), None, False)
    b2, state = lax.optimization_barrier((b2, state))
    b3 = slab_shift(b2, 1)
    a3 = slab_shift(a2, 1)
    state = stats((6, 8), tables, (a2, b2), state, False)
    b3, state = lax.optimization_barrier((b3, state))
    b4 = slab_shift(b3, 1)
    state = stats((2, 4), tables, (a3, b3), state, False)
    b4, state = lax.optimization_barrier((b4, state))
    norm = stats((0,), tables, (b4,), state, True)

    low16, full = jnp.bfloat16, jnp.float32
    def after(arrived, *values):
        return lax.optimization_barrier((arrived,) + values)[1:]

    def to_owners(x):
        return lax.all_to_all(x.reshape(8, SPAN // 4, 2 * WIDTH), MEMBER_AXES, 0, 0, tiled=True)

    def summed(part, arrived):
        return (part + arrived.astype(full)).astype(low16)

    def summed(part, arrived):
        return (part + arrived.astype(full)).astype(low16)

    gb4, dqt = grads((0,), tables, norm, (b4,), None, (low16,))
    rb = slab_shift(gb4, -1)
    ga3, gb3, dqt = grads((2, 4), tables, norm, (a3, b3), dqt, (low16, full))
    ra = slab_shift(ga3, -1)
    (dqt,) = after(rb, dqt)
    rb = slab_shift(summed(gb3, rb), -1)
    ga2, gb2, dqt = grads((6, 8), tables, norm, (a2, b2), dqt, (full, full))
    dqt, ra = lax.optimization_barrier((dqt, ra))
    ra = slab_shift(summed(ga2, ra), -1)
    g0, dqt = grads((14, 16), tables, norm, (a0, b0), dqt, (full,))
    dqt, rb = lax.optimization_barrier((dqt, rb))
    rb = slab_shift(summed(gb2, rb), -1)
    ga1, gb1, mine, send = grads((10, 12), tables, norm, (a1, b1), dqt, (full, full), low_ref)
    ra = slab_shift(summed(ga1, ra), -1)
    other = low_swap(send)
    rb = slab_shift(summed(gb1, rb), -1)
    other, rb = lax.optimization_barrier((other, rb))
    total = to_owners(g0 + jnp.concatenate([ra, rb], axis=0).astype(full))
    grad_keys, grad_values = call(
        unpack_kernel, "unpack", (f32(SPAN // 4, KEY_VALUE_HEADS * HEAD_SIZE),) * 2, [VMEM_SPEC]
    )(total)

    grad_queries = call(
        columns_kernel, "columns", f32(SPAN, 4 * WIDTH), [SMEM_SPEC] + [VMEM_SPEC] * 2
    )(low_ref, mine, other)
    return grad_queries, grad_keys, grad_values


def solution(mesh):
    fine = Mesh(mesh.devices.reshape(4, 8, 2, 2, 2), ("y", "z", "xl", "xh", "core"))
    pb, ka = ("y", "z", "xl"), ("xh", "core")
    in_specs = (P(pb, ka), P(pb, ka), P(pb + ka, None), P(pb + ka, None), P(), P())
    out_specs = (P(pb, ka), P(pb + ka, None), P(pb + ka, None))
    return jax.shard_map(per_device, mesh=fine, in_specs=in_specs, out_specs=out_specs, check_vma=False)
```

time: 175 us -> 135 us (0.77)
  the two profiles are of different devices: /device:TPU:1 before, /device:TPU:24 now
where the time goes in v2:
time: 135 us
  starting transfers between devices  53.3 us (39%)
  waiting for transfers between devices  48.5 us (36%)
  Pallas kernels  28.3 us (21%)
  other arithmetic  3.1 us (2%)
    ppermute x14, starting transfers between devices, slab_shift(): lax.ppermute(x, SLAB_AXES, [(i, i + by) for i in range(count) if 0 <= i +...  43.1 us
    ppermute x14, waiting for transfers between devices, slab_shift(): lax.ppermute(x, SLAB_AXES, [(i, i + by) for i in range(count) if 0 <= i +...  27 us
    pallas_call x5, Pallas kernels, grads(): call(functools.partial(grads_kernel, first_blocks, opening, closing), 'gr...  15 us
    all_to_all x1, waiting for transfers between devices, to_owners(): lax.all_to_all(x.reshape(8, SPAN // 4, 2 * WIDTH), MEMBER_AXES, 0, 0, til...  14.6 us
    pallas_call x4, Pallas kernels, stats(): call(functools.partial(stats_kernel, first_blocks, opening, closing), 'st...  9.08 us
    all_to_all x1, waiting for transfers between devices, per_device(): own = lax.all_to_all(kv, MEMBER_AXES, 0, 0, tiled=True)  6.94 us
    all_to_all x1, starting transfers between devices, per_device(): own = lax.all_to_all(kv, MEMBER_AXES, 0, 0, tiled=True)  4.31 us
    all_to_all x1, starting transfers between devices, to_owners(): lax.all_to_all(x.reshape(8, SPAN // 4, 2 * WIDTH), MEMBER_AXES, 0, 0, til...  3.56 us
  transfers between devices with their start and end apart: 18, of which 15 were waited for; matrix products, arithmetic and copies ran while one was open for 2% of the time, Pallas kernels for 17%

profile of v2, /device:TPU:24, one launch (start us, length us, event | category | flops | bytes accessed | tf_op | source)
XLA Modules:
  0.0 134.7 jit_solution(3766607994117408965)
XLA Ops:
  0.7 1.9 %pack.1 = bf16[8,64,512]{2,1,0:T(8,128)(2,1)} custom-call(bf16[64,2048]{1,0:T(8,128)(2,1)} %k_ref.1, bf16[64,2048]{1,0:T(8,128)(2,1)} %v_ref.1), custom_call_target="tpu_custom_call" | custom-call | tf_op jit(solution)/shard_map/pack/pallas_call | solution.py:314
  2.6 4.3 %all-to-all-start = ((bf16[8,64,512]{2,1,0:T(8,128)(2,1)}), bf16[8,64,512]{2,1,0:T(8,128)(2,1)S(1)}, u32[]{:S(2)}, u32[]{:S(2)}) async-start(bf16[8,64,512]{2,1,0:T(8,128)(2,1)} %pack.1), calls=%async_computation | async-start | bytes 1048576 | tf_op jit(solution)/shard_map/all_to_all | solution.py:323
  7.0 0.8 pad_maximum_fusion
  7.9 2.0 %collective-permute-start = (bf16[2,256,512]{2,1,0:T(8,128)(2,1)}, bf16[2,256,512]{2,1,0:T(8,128)(2,1)S(1)}, u32[]{:S(2)}, u32[]{:S(2)}) collective-permute-start(bf16[2,256,512]{2,1,0:T(8,128)(2,1)} %pad_maximum_fusion), channel_id=1, source_target_pairs={{0,4},{4,0},{1,5},{5,1},{2,6},{6,2},{3,7},{7,3},{8,12},{12,8},{9,1... | collective-permute-start | bytes 1572872 | tf_op jit(solution)/shard_map/ppermute | solution.py:43
  10.0 6.9 %all-to-all-done = bf16[8,64,512]{2,1,0:T(8,128)(2,1)S(1)} async-done(((bf16[8,64,512]{2,1,0:T(8,128)(2,1)}), bf16[8,64,512]{2,1,0:T(8,128)(2,1)S(1)}, u32[]{:S(2)}, u32[]{:S(2)}) %all-to-all-start) | async-done | bytes 524320 | tf_op jit(solution)/shard_map/all_to_all | solution.py:323
  17.0 3.8 %collective-permute-start.1 = (bf16[256,512]{1,0:T(8,128)(2,1)S(1)}, bf16[256,512]{1,0:T(8,128)(2,1)S(1)}, u32[]{:S(2)}, u32[]{:S(2)}) collective-permute-start(bf16[256,512]{1,0:T(8,128)(2,1)S(1)} %bitcast.13), channel_id=1, source_target_pairs={{0,8},{8,16},{16,24},{24,32},{32,40},{40,48},{48,56},{56,64},{64,7... | collective-permute-start | bytes 786440 | tf_op jit(solution)/shard_map/ppermute | solution.py:39
  20.9 0.7 convert_reduce_fusion
  21.6 3.8 %collective-permute-start.3 = (bf16[256,512]{1,0:T(8,128)(2,1)S(1)}, bf16[256,512]{1,0:T(8,128)(2,1)S(1)}, u32[]{:S(2)}, u32[]{:S(2)}) collective-permute-start(bf16[256,512]{1,0:T(8,128)(2,1)S(1)} %bitcast.10), channel_id=1, source_target_pairs={{0,8},{8,16},{16,24},{24,32},{32,40},{40,48},{48,56},{56,64},{64,7... | collective-permute-start | bytes 786440 | tf_op jit(solution)/shard_map/ppermute | solution.py:39
  25.4 6.8 %collective-permute-done.1.refs_7_ = bf16[256,512]{1,0:T(8,128)(2,1)S(1)} collective-permute-done((bf16[256,512]{1,0:T(8,128)(2,1)S(1)}, bf16[256,512]{1,0:T(8,128)(2,1)S(1)}, u32[]{:S(2)}, u32[]{:S(2)}) %collective-permute-start.1) | collective-permute-done | bytes 262176 | tf_op jit(solution)/shard_map/ppermute | solution.py:39
  32.2 1.9 %collective-permute-start.2 = (bf16[256,512]{1,0:T(8,128)(2,1)S(1)}, bf16[256,512]{1,0:T(8,128)(2,1)S(1)}, u32[]{:S(2)}, u32[]{:S(2)}) collective-permute-start(bf16[256,512]{1,0:T(8,128)(2,1)S(1)} %collective-permute-done.1.refs_7_), channel_id=1, source_target_pairs={{0,8},{8,16},{16,24},{24,32},{32,40},{40,48},{48,56},{56,64},{64,7... | collective-permute-start | bytes 786440 | tf_op jit(solution)/shard_map/ppermute | solution.py:39
  34.4 0.2 rows.1
  34.6 2.1 %collective-permute-done.3.refs_6_ = bf16[256,512]{1,0:T(8,128)(2,1)S(1)} collective-permute-done((bf16[256,512]{1,0:T(8,128)(2,1)S(1)}, bf16[256,512]{1,0:T(8,128)(2,1)S(1)}, u32[]{:S(2)}, u32[]{:S(2)}) %collective-permute-start.3) | collective-permute-done | bytes 262176 | tf_op jit(solution)/shard_map/ppermute | solution.py:39
  36.7 1.9 %collective-permute-start.5 = (bf16[256,512]{1,0:T(8,128)(2,1)S(1)}, bf16[256,512]{1,0:T(8,128)(2,1)S(1)}, u32[]{:S(2)}, u32[]{:S(2)}) collective-permute-start(bf16[256,512]{1,0:T(8,128)(2,1)S(1)} %collective-permute-done.3.refs_6_), channel_id=1, source_target_pairs={{0,8},{8,16},{16,24},{24,32},{32,40},{40,48},{48,56},{56,64},{64,7... | collective-permute-start | bytes 786440 | tf_op jit(solution)/shard_map/ppermute | solution.py:39
  38.6 3.4 %stats.4.refs_6_ = f32[2,3,8,1024]{3,2,1,0:T(8,128)S(1)} custom-call(s32[4,14]{1,0:T(4,128)S(1)} %fusion.refs_0_.refs_1_, s32[1,512]{1,0:T(1,128)S(1)} %bitcast.16, bf16[2,1024,128]{2,1,0:T(8,128)(2,1)S(1)} %get-tuple-element.34.refs_2_.refs_3_, bf16[2,1024,128]{2,1,0:T(8,128)(2,1)S(1)} %get-tuple-element.35.refs_3_.refs_4_, bf16[256,512]{1,0:T(8,128)(2,1)S(1)} %bitcast.11, ...), custom_call_target="tpu_custom_call" | custom-call | flops 1024 | bytes 196608 | tf_op jit(solution)/shard_map/stats/pallas_call | solution.py:203
  41.9 1.7 %collective-permute-done.2.refs_5_.refs_6_ = bf16[256,512]{1,0:T(8,128)(2,1)S(1)} collective-permute-done((bf16[256,512]{1,0:T(8,128)(2,1)S(1)}, bf16[256,512]{1,0:T(8,128)(2,1)S(1)}, u32[]{:S(2)}, u32[]{:S(2)}) %collective-permute-start.2) | collective-permute-done | bytes 262176 | tf_op jit(solution)/shard_map/ppermute | solution.py:39
  43.7 1.9 %collective-permute-start.4 = (bf16[256,512]{1,0:T(8,128)(2,1)S(1)}, bf16[256,512]{1,0:T(8,128)(2,1)S(1)}, u32[]{:S(2)}, u32[]{:S(2)}) collective-permute-start(bf16[256,512]{1,0:T(8,128)(2,1)S(1)} %collective-permute-done.2.refs_5_.refs_6_), channel_id=1, source_target_pairs={{0,8},{8,16},{16,24},{24,32},{32,40},{40,48},{48,56},{56,64},{64,7... | collective-permute-start | bytes 786440 | tf_op jit(solution)/shard_map/ppermute | solution.py:39
  45.6 4.0 %collective-permute-done.5.refs_4_.refs_5_ = bf16[256,512]{1,0:T(8,128)(2,1)S(1)} collective-permute-done((bf16[256,512]{1,0:T(8,128)(2,1)S(1)}, bf16[256,512]{1,0:T(8,128)(2,1)S(1)}, u32[]{:S(2)}, u32[]{:S(2)}) %collective-permute-start.5) | collective-permute-done | bytes 262176 | tf_op jit(solution)/shard_map/ppermute | solution.py:39
  49.6 1.9 %collective-permute-start.7 = (bf16[256,512]{1,0:T(8,128)(2,1)S(1)}, bf16[256,512]{1,0:T(8,128)(2,1)S(1)}, u32[]{:S(2)}, u32[]{:S(2)}) collective-permute-start(bf16[256,512]{1,0:T(8,128)(2,1)S(1)} %collective-permute-done.5.refs_4_.refs_5_), channel_id=1, source_target_pairs={{0,8},{8,16},{16,24},{24,32},{32,40},{40,48},{48,56},{56,64},{64,7... | collective-permute-start | bytes 786440 | tf_op jit(solution)/shard_map/ppermute | solution.py:39
  51.5 2.3 %stats.5.refs_6_ = f32[2,3,8,1024]{3,2,1,0:T(8,128)S(1)} custom-call(s32[4,14]{1,0:T(4,128)S(1)} %fusion.refs_0_.refs_1_, s32[1,512]{1,0:T(1,128)S(1)} %bitcast.17, bf16[2,1024,128]{2,1,0:T(8,128)(2,1)S(1)} %get-tuple-element.34.refs_2_.refs_3_, bf16[2,1024,128]{2,1,0:T(8,128)(2,1)S(1)} %get-tuple-element.35.refs_3_.refs_4_, ...), custom_call_target="tpu_custom_call" | custom-call | flops 1024 | bytes 196608 | tf_op jit(solution)/shard_map/stats/pallas_call | solution.py:203
  53.9 1.0 collective-permute-done.4.refs_5_.refs_6_
  54.9 2.2 %collective-permute-start.6 = (bf16[256,512]{1,0:T(8,128)(2,1)S(1)}, bf16[256,512]{1,0:T(8,128)(2,1)S(1)}, u32[]{:S(2)}, u32[]{:S(2)}) collective-permute-start(bf16[256,512]{1,0:T(8,128)(2,1)S(1)} %collective-permute-done.4.refs_5_.refs_6_), channel_id=1, source_target_pairs={{0,8},{8,16},{16,24},{24,32},{32,40},{40,48},{48,56},{56,64},{64,7... | collective-permute-start | bytes 786440 | tf_op jit(solution)/shard_map/ppermute | solution.py:39
  57.1 5.4 %collective-permute-done.7.refs_4_.refs_5_ = bf16[256,512]{1,0:T(8,128)(2,1)S(1)} collective-permute-done((bf16[256,512]{1,0:T(8,128)(2,1)S(1)}, bf16[256,512]{1,0:T(8,128)(2,1)S(1)}, u32[]{:S(2)}, u32[]{:S(2)}) %collective-permute-start.7) | collective-permute-done | bytes 262176 | tf_op jit(solution)/shard_map/ppermute | solution.py:39
  62.5 2.3 %stats.6.refs_5_ = f32[2,3,8,1024]{3,2,1,0:T(8,128)S(1)} custom-call(s32[4,14]{1,0:T(4,128)S(1)} %fusion.refs_0_.refs_1_, s32[1,512]{1,0:T(1,128)S(1)} %bitcast.18, bf16[2,1024,128]{2,1,0:T(8,128)(2,1)S(1)} %get-tuple-element.34.refs_2_.refs_3_, bf16[2,1024,128]{2,1,0:T(8,128)(2,1)S(1)} %get-tuple-element.35.refs_3_.refs_4_, ...), custom_call_target="tpu_custom_call" | custom-call | flops 1024 | bytes 196608 | tf_op jit(solution)/shard_map/stats/pallas_call | solution.py:203
  64.8 0.8 collective-permute-done.6.refs_4_.refs_5_
  65.6 1.1 stats.7.refs_4_.refs_5_
  66.7 1.7 %grads.5 = (bf16[256,512]{1,0:T(8,128)(2,1)S(1)}, f32[2,128,1024]{2,1,0:T(8,128)S(1)}) custom-call(s32[4,14]{1,0:T(4,128)S(1)} %fusion.refs_0_.refs_1_, s32[1,512]{1,0:T(1,128)S(1)} %bitcast.20, bf16[2,1024,128]{2,1,0:T(8,128)(2,1)S(1)} %get-tuple-element.34.refs_2_.refs_3_, bf16[2,1024,128]{2,1,0:T(8,128)(2,1)S(1)} %get-tuple-element.35.refs_3_.refs_4_, ...), custom_call_target="tpu_custom_call" | custom-call | flops 1024 | bytes 1310720 | tf_op jit(solution)/shard_map/grads/pallas_call | solution.py:298
  68.4 2.8 %collective-permute-start.8 = (bf16[256,512]{1,0:T(8,128)(2,1)S(1)}, bf16[256,512]{1,0:T(8,128)(2,1)S(1)}, u32[]{:S(2)}, u32[]{:S(2)}) collective-permute-start(bf16[256,512]{1,0:T(8,128)(2,1)S(1)} %get-tuple-element.42), channel_id=1, source_target_pairs={{8,0},{16,8},{24,16},{32,24},{40,32},{48,40},{56,48},{64,56},{72,6... | collective-permute-start | bytes 786440 | tf_op jit(solution)/shard_map/ppermute | solution.py:39
  71.2 3.3 %grads.6 = (bf16[256,512]{1,0:T(8,128)(2,1)S(1)}, f32[256,512]{1,0:T(8,128)S(1)}, f32[2,128,1024]{2,1,0:T(8,128)S(1)}) custom-call(s32[4,14]{1,0:T(4,128)S(1)} %fusion.refs_0_.refs_1_, s32[1,512]{1,0:T(1,128)S(1)} %bitcast.21, bf16[2,1024,128]{2,1,0:T(8,128)(2,1)S(1)} %get-tuple-element.34.refs_2_.refs_3_, ...), custom_call_target="tpu_custom_call", output_to_operand_aliasing={{2}: (7, {})} | custom-call | flops 1024 | bytes 1835008 | tf_op jit(solution)/shard_map/grads/pallas_call | solution.py:298
  74.5 2.7 %collective-permute-start.9 = (bf16[256,512]{1,0:T(8,128)(2,1)S(1)}, bf16[256,512]{1,0:T(8,128)(2,1)S(1)}, u32[]{:S(2)}, u32[]{:S(2)}) collective-permute-start(bf16[256,512]{1,0:T(8,128)(2,1)S(1)} %get-tuple-element.47), channel_id=1, source_target_pairs={{8,0},{16,8},{24,16},{32,24},{40,32},{48,40},{56,48},{64,56},{72,6... | collective-permute-start | bytes 786440 | tf_op jit(solution)/shard_map/ppermute | solution.py:39
  77.4 4.1 %collective-permute-start.10 = (bf16[256,512]{1,0:T(8,128)(2,1)S(1)}, bf16[256,512]{1,0:T(8,128)(2,1)S(1)}, u32[]{:S(2)}, u32[]{:S(2)}) collective-permute-start(bf16[256,512]{1,0:T(8,128)(2,1)S(1)} %add_convert_fusion.4), channel_id=1, source_target_pairs={{8,0},{16,8},{24,16},{32,24},{40,32},{48,40},{56,48},{64,56},{72,6... | collective-permute-start | bytes 786440 | tf_op jit(solution)/shard_map/ppermute | solution.py:39
  81.6 3.4 %grads.7 = (f32[256,512]{1,0:T(8,128)S(1)}, f32[256,512]{1,0:T(8,128)S(1)}, f32[2,128,1024]{2,1,0:T(8,128)S(1)}) custom-call(s32[4,14]{1,0:T(4,128)S(1)} %fusion.refs_0_.refs_1_, s32[1,512]{1,0:T(1,128)S(1)} %bitcast.22, bf16[2,1024,128]{2,1,0:T(8,128)(2,1)S(1)} %get-tuple-element.34.refs_2_.refs_3_, ...), custom_call_target="tpu_custom_call", output_to_operand_aliasing={{2}: (7, {})} | custom-call | flops 1024 | bytes 2097152 | tf_op jit(solution)/shard_map/grads/pallas_call | solution.py:298
  85.0 0.1 collective-permute-done.9
  85.1 3.0 %grads.8 = (f32[512,512]{1,0:T(8,128)S(1)}, f32[2,128,1024]{2,1,0:T(8,128)S(1)}) custom-call(s32[4,14]{1,0:T(4,128)S(1)} %fusion.refs_0_.refs_1_, s32[1,512]{1,0:T(1,128)S(1)} %bitcast.23, bf16[2,1024,128]{2,1,0:T(8,128)(2,1)S(1)} %get-tuple-element.34.refs_2_.refs_3_, ...), custom_call_target="tpu_custom_call", output_to_operand_aliasing={{1}: (7, {})} | custom-call | flops 1024 | bytes 2097152 | tf_op jit(solution)/shard_map/grads/pallas_call | solution.py:298
  88.2 4.7 %collective-permute-start.12 = (bf16[256,512]{1,0:T(8,128)(2,1)S(1)}, bf16[256,512]{1,0:T(8,128)(2,1)S(1)}, u32[]{:S(2)}, u32[]{:S(2)}) collective-permute-start(bf16[256,512]{1,0:T(8,128)(2,1)S(1)} %add_convert_fusion.3), channel_id=1, source_target_pairs={{8,0},{16,8},{24,16},{32,24},{40,32},{48,40},{56,48},{64,56},{72,6... | collective-permute-start | bytes 786440 | tf_op jit(solution)/shard_map/ppermute | solution.py:39
  93.0 1.9 %collective-permute-start.14 = (bf16[256,512]{1,0:T(8,128)(2,1)S(1)}, bf16[256,512]{1,0:T(8,128)(2,1)S(1)}, u32[]{:S(2)}, u32[]{:S(2)}) collective-permute-start(bf16[256,512]{1,0:T(8,128)(2,1)S(1)} %add_convert_fusion.1), channel_id=1, source_target_pairs={{8,0},{16,8},{24,16},{32,24},{40,32},{48,40},{56,48},{64,56},{72,6... | collective-permute-start | bytes 786440 | tf_op jit(solution)/shard_map/ppermute | solution.py:39
  94.9 3.5 %grads.9 = (f32[256,512]{1,0:T(8,128)S(1)}, f32[256,512]{1,0:T(8,128)S(1)}, f32[256,512]{1,0:T(8,128)S(1)}, f32[256,512]{1,0:T(8,128)S(1)}) custom-call(s32[1]{0:T(128)} %bitcast.low_ref.refs_0_, s32[4,14]{1,0:T(4,128)S(1)} %fusion.refs_0_.refs_1_, s32[1,512]{1,0:T(1,128)S(1)} %bitcast.24, bf16[2,1024,128]{2,1,0:T(8,128)(2,1)S(1)} %get-tuple-element.34.refs_2_.refs_3_, ...), custom_call_target="tpu_custom_call" | custom-call | flops 1024 | bytes 2097152 | tf_op jit(solution)/shard_map/grads/pallas_call | solution.py:298
  98.5 0.3 collective-permute-start.11
  98.8 0.4 collective-permute-done.12
  99.3 5.1 %collective-permute-start.13 = (bf16[256,512]{1,0:T(8,128)(2,1)S(1)}, bf16[256,512]{1,0:T(8,128)(2,1)S(1)}, u32[]{:S(2)}, u32[]{:S(2)}) collective-permute-start(bf16[256,512]{1,0:T(8,128)(2,1)S(1)} %add_convert_fusion.2), channel_id=1, source_target_pairs={{8,0},{16,8},{24,16},{32,24},{40,32},{48,40},{56,48},{64,56},{72,6... | collective-permute-start | bytes 786440 | tf_op jit(solution)/shard_map/ppermute | solution.py:39
  104.4 0.3 collective-permute-done.14
  104.8 4.3 %collective-permute-start.15 = (bf16[256,512]{1,0:T(8,128)(2,1)S(1)}, bf16[256,512]{1,0:T(8,128)(2,1)S(1)}, u32[]{:S(2)}, u32[]{:S(2)}) collective-permute-start(bf16[256,512]{1,0:T(8,128)(2,1)S(1)} %add_convert_fusion), channel_id=1, source_target_pairs={{8,0},{16,8},{24,16},{32,24},{40,32},{48,40},{56,48},{64,56},{72,6... | collective-permute-start | bytes 786440 | tf_op jit(solution)/shard_map/ppermute | solution.py:39
  109.1 1.3 collective-permute-done.13
  110.5 2.8 %collective-permute-done.15 = bf16[256,512]{1,0:T(8,128)(2,1)S(1)} collective-permute-done((bf16[256,512]{1,0:T(8,128)(2,1)S(1)}, bf16[256,512]{1,0:T(8,128)(2,1)S(1)}, u32[]{:S(2)}, u32[]{:S(2)}) %collective-permute-start.15) | collective-permute-done | bytes 262176 | tf_op jit(solution)/shard_map/ppermute | solution.py:39
  113.3 1.2 convert_add_fusion
  114.4 3.6 %all-to-all-start.1 = ((f32[8,64,512]{2,1,0:T(8,128)}), f32[8,64,512]{2,1,0:T(8,128)S(1)}, u32[]{:S(2)}, u32[]{:S(2)}) async-start(f32[8,64,512]{2,1,0:T(8,128)} %bitcast.25), calls=%async_computation.1 | async-start | bytes 2097152 | tf_op jit(solution)/shard_map/all_to_all | solution.py:364
  118.0 1.0 columns.1
  119.1 14.6 %all-to-all-done.1.in_ref = f32[8,64,512]{2,1,0:T(8,128)S(1)} async-done(((f32[8,64,512]{2,1,0:T(8,128)}), f32[8,64,512]{2,1,0:T(8,128)S(1)}, u32[]{:S(2)}, u32[]{:S(2)}) %all-to-all-start.1) | async-done | bytes 1048608 | tf_op jit(solution)/shard_map/all_to_all | solution.py:364
  133.6 1.0 unpack.1
  (26 shorter events, 1.1 us)
Async XLA Ops:
  0.6 9.2 %copy-start = (s32[2,128,14]{1,0,2:T(2,128)S(1)}, s32[2,128,14]{1,0,2:T(2,128)}, u32[]{:S(2)}) copy-start(s32[2,128,14]{1,0,2:T(2,128)} %param.11) | copy-start | bytes 43012
  0.6 6.3 %copy-start.2 = (bf16[256,1024]{1,0:T(8,128)(2,1)S(1)}, bf16[256,1024]{1,0:T(8,128)(2,1)}, u32[]{:S(2)}) copy-start(bf16[256,1024]{1,0:T(8,128)(2,1)} %do_ref.1) | copy-start | bytes 1572868
  0.7 6.3 %copy-start.1 = (bf16[256,1024]{1,0:T(8,128)(2,1)S(1)}, bf16[256,1024]{1,0:T(8,128)(2,1)}, u32[]{:S(2)}) copy-start(bf16[256,1024]{1,0:T(8,128)(2,1)} %q_ref.1) | copy-start | bytes 1572868
  2.6 14.4 %all-to-all-start = ((bf16[8,64,512]{2,1,0:T(8,128)(2,1)}), bf16[8,64,512]{2,1,0:T(8,128)(2,1)S(1)}, u32[]{:S(2)}, u32[]{:S(2)}) async-start(bf16[8,64,512]{2,1,0:T(8,128)(2,1)} %pack.1), calls=%async_computation | async-start | bytes 1048576 | tf_op jit(solution)/shard_map/all_to_all | solution.py:323
  6.9 3.0 %copy-start.3 = (s32[16384]{0:T(1024)S(1)}, s32[16384]{0:T(1024)}, u32[]{:S(2)}) copy-start(s32[16384]{0:T(1024)} %param.10) | copy-start | bytes 196612
  7.9 26.5 %collective-permute-start = (bf16[2,256,512]{2,1,0:T(8,128)(2,1)}, bf16[2,256,512]{2,1,0:T(8,128)(2,1)S(1)}, u32[]{:S(2)}, u32[]{:S(2)}) collective-permute-start(bf16[2,256,512]{2,1,0:T(8,128)(2,1)} %pad_maximum_fusion), channel_id=1, source_target_pairs={{0,4},{4,0},{1,5},{5,1},{2,6},{6,2},{3,7},{7,3},{8,12},{12,8},{9,1... | collective-permute-start | bytes 1572872 | tf_op jit(solution)/shard_map/ppermute | solution.py:43
  17.0 15.2 %collective-permute-start.1 = (bf16[256,512]{1,0:T(8,128)(2,1)S(1)}, bf16[256,512]{1,0:T(8,128)(2,1)S(1)}, u32[]{:S(2)}, u32[]{:S(2)}) collective-permute-start(bf16[256,512]{1,0:T(8,128)(2,1)S(1)} %bitcast.13), channel_id=1, source_target_pairs={{0,8},{8,16},{16,24},{24,32},{32,40},{40,48},{48,56},{56,64},{64,7... | collective-permute-start | bytes 786440 | tf_op jit(solution)/shard_map/ppermute | solution.py:39
  21.6 15.1 %collective-permute-start.3 = (bf16[256,512]{1,0:T(8,128)(2,1)S(1)}, bf16[256,512]{1,0:T(8,128)(2,1)S(1)}, u32[]{:S(2)}, u32[]{:S(2)}) collective-permute-start(bf16[256,512]{1,0:T(8,128)(2,1)S(1)} %bitcast.10), channel_id=1, source_target_pairs={{0,8},{8,16},{16,24},{24,32},{32,40},{40,48},{48,56},{56,64},{64,7... | collective-permute-start | bytes 786440 | tf_op jit(solution)/shard_map/ppermute | solution.py:39
  32.2 11.5 %collective-permute-start.2 = (bf16[256,512]{1,0:T(8,128)(2,1)S(1)}, bf16[256,512]{1,0:T(8,128)(2,1)S(1)}, u32[]{:S(2)}, u32[]{:S(2)}) collective-permute-start(bf16[256,512]{1,0:T(8,128)(2,1)S(1)} %collective-permute-done.1.refs_7_), channel_id=1, source_target_pairs={{0,8},{8,16},{16,24},{24,32},{32,40},{40,48},{48,56},{56,64},{64,7... | collective-permute-start | bytes 786440 | tf_op jit(solution)/shard_map/ppermute | solution.py:39
  36.7 12.9 %collective-permute-start.5 = (bf16[256,512]{1,0:T(8,128)(2,1)S(1)}, bf16[256,512]{1,0:T(8,128)(2,1)S(1)}, u32[]{:S(2)}, u32[]{:S(2)}) collective-permute-start(bf16[256,512]{1,0:T(8,128)(2,1)S(1)} %collective-permute-done.3.refs_6_), channel_id=1, source_target_pairs={{0,8},{8,16},{16,24},{24,32},{32,40},{40,48},{48,56},{56,64},{64,7... | collective-permute-start | bytes 786440 | tf_op jit(solution)/shard_map/ppermute | solution.py:39
  43.7 11.2 %collective-permute-start.4 = (bf16[256,512]{1,0:T(8,128)(2,1)S(1)}, bf16[256,512]{1,0:T(8,128)(2,1)S(1)}, u32[]{:S(2)}, u32[]{:S(2)}) collective-permute-start(bf16[256,512]{1,0:T(8,128)(2,1)S(1)} %collective-permute-done.2.refs_5_.refs_6_), channel_id=1, source_target_pairs={{0,8},{8,16},{16,24},{24,32},{32,40},{40,48},{48,56},{56,64},{64,7... | collective-permute-start | bytes 786440 | tf_op jit(solution)/shard_map/ppermute | solution.py:39
  49.6 12.9 %collective-permute-start.7 = (bf16[256,512]{1,0:T(8,128)(2,1)S(1)}, bf16[256,512]{1,0:T(8,128)(2,1)S(1)}, u32[]{:S(2)}, u32[]{:S(2)}) collective-permute-start(bf16[256,512]{1,0:T(8,128)(2,1)S(1)} %collective-permute-done.5.refs_4_.refs_5_), channel_id=1, source_target_pairs={{0,8},{8,16},{16,24},{24,32},{32,40},{40,48},{48,56},{56,64},{64,7... | collective-permute-start | bytes 786440 | tf_op jit(solution)/shard_map/ppermute | solution.py:39
  54.9 10.7 %collective-permute-start.6 = (bf16[256,512]{1,0:T(8,128)(2,1)S(1)}, bf16[256,512]{1,0:T(8,128)(2,1)S(1)}, u32[]{:S(2)}, u32[]{:S(2)}) collective-permute-start(bf16[256,512]{1,0:T(8,128)(2,1)S(1)} %collective-permute-done.4.refs_5_.refs_6_), channel_id=1, source_target_pairs={{0,8},{8,16},{16,24},{24,32},{32,40},{40,48},{48,56},{56,64},{64,7... | collective-permute-start | bytes 786440 | tf_op jit(solution)/shard_map/ppermute | solution.py:39
  68.4 8.9 %collective-permute-start.8 = (bf16[256,512]{1,0:T(8,128)(2,1)S(1)}, bf16[256,512]{1,0:T(8,128)(2,1)S(1)}, u32[]{:S(2)}, u32[]{:S(2)}) collective-permute-start(bf16[256,512]{1,0:T(8,128)(2,1)S(1)} %get-tuple-element.42), channel_id=1, source_target_pairs={{8,0},{16,8},{24,16},{32,24},{40,32},{48,40},{56,48},{64,56},{72,6... | collective-permute-start | bytes 786440 | tf_op jit(solution)/shard_map/ppermute | solution.py:39
  74.5 10.6 %collective-permute-start.9 = (bf16[256,512]{1,0:T(8,128)(2,1)S(1)}, bf16[256,512]{1,0:T(8,128)(2,1)S(1)}, u32[]{:S(2)}, u32[]{:S(2)}) collective-permute-start(bf16[256,512]{1,0:T(8,128)(2,1)S(1)} %get-tuple-element.47), channel_id=1, source_target_pairs={{8,0},{16,8},{24,16},{32,24},{40,32},{48,40},{56,48},{64,56},{72,6... | collective-permute-start | bytes 786440 | tf_op jit(solution)/shard_map/ppermute | solution.py:39
  77.4 10.7 %collective-permute-start.10 = (bf16[256,512]{1,0:T(8,128)(2,1)S(1)}, bf16[256,512]{1,0:T(8,128)(2,1)S(1)}, u32[]{:S(2)}, u32[]{:S(2)}) collective-permute-start(bf16[256,512]{1,0:T(8,128)(2,1)S(1)} %add_convert_fusion.4), channel_id=1, source_target_pairs={{8,0},{16,8},{24,16},{32,24},{40,32},{48,40},{56,48},{64,56},{72,6... | collective-permute-start | bytes 786440 | tf_op jit(solution)/shard_map/ppermute | solution.py:39
  88.2 11.0 %collective-permute-start.12 = (bf16[256,512]{1,0:T(8,128)(2,1)S(1)}, bf16[256,512]{1,0:T(8,128)(2,1)S(1)}, u32[]{:S(2)}, u32[]{:S(2)}) collective-permute-start(bf16[256,512]{1,0:T(8,128)(2,1)S(1)} %add_convert_fusion.3), channel_id=1, source_target_pairs={{8,0},{16,8},{24,16},{32,24},{40,32},{48,40},{56,48},{64,56},{72,6... | collective-permute-start | bytes 786440 | tf_op jit(solution)/shard_map/ppermute | solution.py:39
  93.0 11.7 %collective-permute-start.14 = (bf16[256,512]{1,0:T(8,128)(2,1)S(1)}, bf16[256,512]{1,0:T(8,128)(2,1)S(1)}, u32[]{:S(2)}, u32[]{:S(2)}) collective-permute-start(bf16[256,512]{1,0:T(8,128)(2,1)S(1)} %add_convert_fusion.1), channel_id=1, source_target_pairs={{8,0},{16,8},{24,16},{32,24},{40,32},{48,40},{56,48},{64,56},{72,6... | collective-permute-start | bytes 786440 | tf_op jit(solution)/shard_map/ppermute | solution.py:39
  98.5 12.0 %collective-permute-start.11 = (f32[256,512]{1,0:T(8,128)S(1)}, f32[256,512]{1,0:T(8,128)S(1)}, u32[]{:S(2)}, u32[]{:S(2)}) collective-permute-start(f32[256,512]{1,0:T(8,128)S(1)} %get-tuple-element.53), channel_id=1, source_target_pairs={{0,4},{4,0},{1,5},{5,1},{2,6},{6,2},{3,7},{7,3},{8,12},{12,8},{9,1... | collective-permute-start | bytes 1572872 | tf_op jit(solution)/shard_map/ppermute | solution.py:43
  99.3 11.1 %collective-permute-start.13 = (bf16[256,512]{1,0:T(8,128)(2,1)S(1)}, bf16[256,512]{1,0:T(8,128)(2,1)S(1)}, u32[]{:S(2)}, u32[]{:S(2)}) collective-permute-start(bf16[256,512]{1,0:T(8,128)(2,1)S(1)} %add_convert_fusion.2), channel_id=1, source_target_pairs={{8,0},{16,8},{24,16},{32,24},{40,32},{48,40},{56,48},{64,56},{72,6... | collective-permute-start | bytes 786440 | tf_op jit(solution)/shard_map/ppermute | solution.py:39
  104.8 8.5 %collective-permute-start.15 = (bf16[256,512]{1,0:T(8,128)(2,1)S(1)}, bf16[256,512]{1,0:T(8,128)(2,1)S(1)}, u32[]{:S(2)}, u32[]{:S(2)}) collective-permute-start(bf16[256,512]{1,0:T(8,128)(2,1)S(1)} %add_convert_fusion), channel_id=1, source_target_pairs={{8,0},{16,8},{24,16},{32,24},{40,32},{48,40},{56,48},{64,56},{72,6... | collective-permute-start | bytes 786440 | tf_op jit(solution)/shard_map/ppermute | solution.py:39
  114.4 19.2 %all-to-all-start.1 = ((f32[8,64,512]{2,1,0:T(8,128)}), f32[8,64,512]{2,1,0:T(8,128)S(1)}, u32[]{:S(2)}, u32[]{:S(2)}) async-start(f32[8,64,512]{2,1,0:T(8,128)} %bitcast.25), calls=%async_computation.1 | async-start | bytes 2097152 | tf_op jit(solution)/shard_map/all_to_all | solution.py:364

commit v3 on v2

--- a/solution.py
+++ b/solution.py
@@ -111,7 +111,7 @@
 def columns_kernel(low_ref, mine_ref, other_ref, out_ref):
     low = low_ref[0]
     out_ref[:, pl.ds(pl.multiple_of(low * 2 * WIDTH, BLOCK), 2 * WIDTH)] = mine_ref[...]
-    out_ref[:, pl.ds(pl.multiple_of((1 - low) * 2 * WIDTH, BLOCK), 2 * WIDTH)] = other_ref[...]
+    out_ref[:, pl.ds(pl.multiple_of((1 - low) * 2 * WIDTH, BLOCK), 2 * WIDTH)] = other_ref[...].astype(jnp.float32)
 
 
 def visible(i, w):
@@ -125,7 +125,13 @@
         ok = key_iota >= jnp.where(hit_ref[i, w - i] > 0, -1, bound)
     else:
         ok = (key_iota >= bound) & (key_iota <= lax.broadcasted_iota(jnp.int32, (BLOCK, BLOCK), 1))
-    return jnp.concatenate([ok, ok], axis=1)
+    return ok
+
+
+def masked(ok, x):
+    return jnp.concatenate(
+        [jnp.where(ok, x[:, :BLOCK], NEG_LARGE), jnp.where(ok, x[:, BLOCK:], NEG_LARGE)], axis=1
+    )
 
 
 def fold(x, op):
@@ -141,7 +147,7 @@
         state_in, rest = None, rest
     else:
         state_in, rest = rest[0], rest[1:]
-    out_ref, s_scr = rest
+    (out_ref,) = rest
     for h in range(LOCAL_HEADS):
         for i in range(Q_BLOCKS):
             lanes = slice(i * PAIR, (i + 1) * PAIR)
@@ -159,31 +165,19 @@
                 if seen:
                     todo.append((ref, seen, (seen[0] - first) * BLOCK))
             peak = top
-            at = 0
             for ref, seen, row in todo:
-                s = dot(ref[row : row + len(seen) * BLOCK, h * HEAD_SIZE : (h + 1) * HEAD_SIZE], qs, 1, 1)
+                rows = slice(row, row + len(seen) * BLOCK)
+                s = dot(ref[rows, h * HEAD_SIZE : (h + 1) * HEAD_SIZE], qs, 1, 1)
+                dp = dot(ref[rows, WIDTH + h * HEAD_SIZE : WIDTH + (h + 1) * HEAD_SIZE], dos, 1, 1)
                 for n, w in enumerate(seen):
-                    x = jnp.where(
-                        mask_of(hit_ref, start_ref, i, w), s[n * BLOCK : (n + 1) * BLOCK] * EXP2_SCALE, NEG_LARGE
-                    )
-                    s_scr[h * Q_BLOCKS + i, at : at + BLOCK, :] = x
-                    peak = jnp.maximum(peak, fold(x, jnp.max))
-                    at += BLOCK
-            if todo and not opening:
-                factor = jnp.exp2(top - peak)
-                total = total * factor
-                inner = inner * factor
-            at = 0
-            for ref, seen, row in todo:
-                dp = dot(
-                    ref[row : row + len(seen) * BLOCK, WIDTH + h * HEAD_SIZE : WIDTH + (h + 1) * HEAD_SIZE], dos, 1, 1
-                )
-                for n, w in enumerate(seen):
-                    x = s_scr[h * Q_BLOCKS + i, at : at + BLOCK, :].reshape(BLOCK // 8, 8, PAIR)
-                    weight = jnp.exp2(x - peak[None])
-                    total = total + jnp.sum(weight, axis=0)
-                    inner = inner + jnp.sum(weight * dp[n * BLOCK : (n + 1) * BLOCK].reshape(BLOCK // 8, 8, PAIR), axis=0)
-                    at += BLOCK
+                    part = slice(n * BLOCK, (n + 1) * BLOCK)
+                    x = masked(mask_of(hit_ref, start_ref, i, w), s[part] * EXP2_SCALE)
+                    higher = jnp.maximum(peak, fold(x, jnp.max))
+                    weight = jnp.exp2(x.reshape(BLOCK // 8, 8, PAIR) - higher[None])
+                    factor = jnp.exp2(peak - higher)
+                    total = total * factor + jnp.sum(weight, axis=0)
+                    inner = inner * factor + jnp.sum(weight * dp[part].reshape(BLOCK // 8, 8, PAIR), axis=0)
+                    peak = higher
             if closing:
                 top = jnp.max(peak, axis=0, keepdims=True)
                 factor = jnp.exp2(peak - top)
@@ -205,7 +199,6 @@
         "stats",
         shape,
         [SMEM_SPEC] + [VMEM_SPEC] * (3 + len(pieces) + (not opening)),
-        scratch=[pltpu.VMEM((LOCAL_HEADS * Q_BLOCKS, 2 * BLOCK * len(pieces), PAIR), jnp.float32)],
     )(*tables, *pieces, *(() if opening else (state,)))
 
 
@@ -253,7 +246,7 @@
                 dp = dot(ref[rows, vcols], dos, 1, 1)
                 for n, w in enumerate(seen):
                     part = slice(n * BLOCK, (n + 1) * BLOCK)
-                    x = jnp.where(mask_of(hit_ref, start_ref, i, w), s[part] * EXP2_SCALE - norm, NEG_LARGE)
+                    x = masked(mask_of(hit_ref, start_ref, i, w), s[part] * EXP2_SCALE - norm)
                     prob = jnp.exp2(x)
                     at = slice(m * span + (w - first) * BLOCK, m * span + (w - first + 1) * BLOCK)
                     p_scr[h, at, lanes] = prob.astype(jnp.bfloat16)
@@ -278,7 +271,7 @@
     if closing:
         low = low_ref[0]
         mine_ref[...] = dq_scr[pl.ds(pl.multiple_of(low * SPAN, SPAN), SPAN), :]
-        send_ref[...] = dq_scr[pl.ds(pl.multiple_of((1 - low) * SPAN, SPAN), SPAN), :]
+        send_ref[...] = dq_scr[pl.ds(pl.multiple_of((1 - low) * SPAN, SPAN), SPAN), :].astype(jnp.bfloat16)
 
 
 def grads(first_blocks, tables, norm, pieces, dqt, dtypes, low=None):
@@ -286,7 +279,7 @@
     count = len(pieces)
     rows = SPAN * count // len(dtypes)
     outs = [jax.ShapeDtypeStruct((rows, 2 * WIDTH), d) for d in dtypes]
-    outs += [f32(SPAN, 2 * WIDTH)] * 2 if closing else [f32(LOCAL_HEADS, HEAD_SIZE, ROWS)]
+    outs += [f32(SPAN, 2 * WIDTH), bf16(SPAN, 2 * WIDTH)] if closing else [f32(LOCAL_HEADS, HEAD_SIZE, ROWS)]
     scratch = [pltpu.VMEM((LOCAL_HEADS, SPAN * count, ROWS), jnp.bfloat16)] * 2
     if closing:
         scratch.append(pltpu.VMEM((SLAB, 2 * WIDTH), jnp.float32))
@@ -376,17 +369,18 @@
     (dqt,) = after(rb, dqt)
     rb = slab_shift(summed(gb3, rb), -1)
     ga2, gb2, dqt = grads((6, 8), tables, norm, (a2, b2), dqt, (full, full))
-    dqt, ra = lax.optimization_barrier((dqt, ra))
     ra = slab_shift(summed(ga2, ra), -1)
-    g0, dqt = grads((14, 16), tables, norm, (a0, b0), dqt, (full,))
-    dqt, rb = lax.optimization_barrier((dqt, rb))
+    (dqt,) = after(rb, dqt)
     rb = slab_shift(summed(gb2, rb), -1)
-    ga1, gb1, mine, send = grads((10, 12), tables, norm, (a1, b1), dqt, (full, full), low_ref)
-    ra = slab_shift(summed(ga1, ra), -1)
+    ga1, gb1, dqt = grads((10, 12), tables, norm, (a1, b1), dqt, (full, full))
+    dqt, ra = lax.optimization_barrier((dqt, summed(ga1, ra)))
+    ra = slab_shift(ra, -1)
+    g0, mine, send = grads((14, 16), tables, norm, (a0, b0), dqt, (full,), low_ref)
+    send, rb = lax.optimization_barrier((send, rb))
+    rb = slab_shift(summed(gb1, rb), -1)
     other = low_swap(send)
-    rb = slab_shift(summed(gb1, rb), -1)
     other, rb = lax.optimization_barrier((other, rb))
-    total = to_owners(g0 + jnp.concatenate([ra, rb], axis=0).astype(full))
+    total = to_owners((g0 + jnp.concatenate([ra, rb], axis=0).astype(full)).astype(low16))
     grad_keys, grad_values = call(
         unpack_kernel, "unpack", (f32(SPAN // 4, KEY_VALUE_HEADS * HEAD_SIZE),) * 2, [VMEM_SPEC]
     )(total)

time: 135 us -> 130 us (0.963)
  starting transfers between devices: 53.3 us -> 51.1 us
  waiting for transfers between devices: 48.5 us -> 46.7 us
    all_to_all x1, waiting for transfers between devices: 14.6 us -> 9.02 us  [to_owners(): lax.all_to_all(x.reshape(8, SPAN // 4, 2 * WIDTH), MEMBER_AXES, 0, 0, til...]
    ppermute x14, waiting for transfers between devices: 27 us -> 29.6 us  [slab_shift(): lax.ppermute(x, SLAB_AXES, [(i, i + by) for i in range(count) if 0 <= i +...]
    ppermute x14, starting transfers between devices: 43.1 us -> 40.5 us  [slab_shift(): lax.ppermute(x, SLAB_AXES, [(i, i + by) for i in range(count) if 0 <= i +...]
  transfers between devices with their start and end apart: 18 -> 18, of which waited for: 15 -> 15; matrix products, arithmetic and copies ran while one was open for 2% -> 1% of each run, Pallas kernels for 17% -> 17%
where the time goes in v3:
time: 130 us; the launch traced here: 129 us
  starting transfers between devices  51.1 us (39%)
  waiting for transfers between devices  46.7 us (36%)
  Pallas kernels  28 us (22%)
  other arithmetic  2.15 us (2%)
    ppermute x14, starting transfers between devices, slab_shift(): lax.ppermute(x, SLAB_AXES, [(i, i + by) for i in range(count) if 0 <= i +...  40.5 us
    ppermute x14, waiting for transfers between devices, slab_shift(): lax.ppermute(x, SLAB_AXES, [(i, i + by) for i in range(count) if 0 <= i +...  29.6 us
    pallas_call x5, Pallas kernels, grads(): call(functools.partial(grads_kernel, first_blocks, opening, closing), 'gr...  15 us
    all_to_all x1, waiting for transfers between devices, to_owners(): lax.all_to_all(x.reshape(8, SPAN // 4, 2 * WIDTH), MEMBER_AXES, 0, 0, til...  9.02 us
    pallas_call x4, Pallas kernels, stats(): call(functools.partial(stats_kernel, first_blocks, opening, closing), 'st...  8.83 us
    all_to_all x1, waiting for transfers between devices, per_device(): own = lax.all_to_all(kv, MEMBER_AXES, 0, 0, tiled=True)  7.64 us
    all_to_all x1, starting transfers between devices, per_device(): own = lax.all_to_all(kv, MEMBER_AXES, 0, 0, tiled=True)  4.31 us
    all_to_all x1, starting transfers between devices, to_owners(): lax.all_to_all(x.reshape(8, SPAN // 4, 2 * WIDTH), MEMBER_AXES, 0, 0, til...  3.85 us
  transfers between devices with their start and end apart: 18, of which 15 were waited for; matrix products, arithmetic and copies ran while one was open for 1% of the time, Pallas kernels for 17%

profile of v3, /device:TPU:24, one launch (start us, length us, event | category | flops | bytes accessed | tf_op | source)
XLA Modules:
  0.0 129.5 jit_solution(16672985548257706680)
XLA Ops:
  0.7 1.9 %pack.1 = bf16[8,64,512]{2,1,0:T(8,128)(2,1)} custom-call(bf16[64,2048]{1,0:T(8,128)(2,1)} %k_ref.1, bf16[64,2048]{1,0:T(8,128)(2,1)} %v_ref.1), custom_call_target="tpu_custom_call" | custom-call | tf_op jit(solution)/shard_map/pack/pallas_call | solution.py:307
  2.6 4.3 %all-to-all-start = ((bf16[8,64,512]{2,1,0:T(8,128)(2,1)}), bf16[8,64,512]{2,1,0:T(8,128)(2,1)S(1)}, u32[]{:S(2)}, u32[]{:S(2)}) async-start(bf16[8,64,512]{2,1,0:T(8,128)(2,1)} %pack.1), calls=%async_computation | async-start | bytes 1048576 | tf_op jit(solution)/shard_map/all_to_all | solution.py:316
  7.1 2.1 %collective-permute-start = (bf16[2,256,512]{2,1,0:T(8,128)(2,1)S(1)}, bf16[2,256,512]{2,1,0:T(8,128)(2,1)S(1)}, u32[]{:S(2)}, u32[]{:S(2)}) collective-permute-start(bf16[2,256,512]{2,1,0:T(8,128)(2,1)S(1)} %pad_maximum_fusion), channel_id=1, source_target_pairs={{0,4},{4,0},{1,5},{5,1},{2,6},{6,2},{3,7},{7,3},{8,12},{12,8},{9,1... | collective-permute-start | bytes 1572872 | tf_op jit(solution)/shard_map/ppermute | solution.py:43
  9.3 7.6 %all-to-all-done = bf16[8,64,512]{2,1,0:T(8,128)(2,1)S(1)} async-done(((bf16[8,64,512]{2,1,0:T(8,128)(2,1)}), bf16[8,64,512]{2,1,0:T(8,128)(2,1)S(1)}, u32[]{:S(2)}, u32[]{:S(2)}) %all-to-all-start) | async-done | bytes 524320 | tf_op jit(solution)/shard_map/all_to_all | solution.py:316
  17.0 3.8 %collective-permute-start.1 = (bf16[256,512]{1,0:T(8,128)(2,1)S(1)}, bf16[256,512]{1,0:T(8,128)(2,1)S(1)}, u32[]{:S(2)}, u32[]{:S(2)}) collective-permute-start(bf16[256,512]{1,0:T(8,128)(2,1)S(1)} %bitcast.13), channel_id=1, source_target_pairs={{0,8},{8,16},{16,24},{24,32},{32,40},{40,48},{48,56},{56,64},{64,7... | collective-permute-start | bytes 786440 | tf_op jit(solution)/shard_map/ppermute | solution.py:39
  20.9 0.7 convert_reduce_fusion
  21.6 3.8 %collective-permute-start.3 = (bf16[256,512]{1,0:T(8,128)(2,1)S(1)}, bf16[256,512]{1,0:T(8,128)(2,1)S(1)}, u32[]{:S(2)}, u32[]{:S(2)}) collective-permute-start(bf16[256,512]{1,0:T(8,128)(2,1)S(1)} %bitcast.10), channel_id=1, source_target_pairs={{0,8},{8,16},{16,24},{24,32},{32,40},{40,48},{48,56},{56,64},{64,7... | collective-permute-start | bytes 786440 | tf_op jit(solution)/shard_map/ppermute | solution.py:39
  25.4 6.8 %collective-permute-done.1.refs_7_.refs_6_ = bf16[256,512]{1,0:T(8,128)(2,1)S(1)} collective-permute-done((bf16[256,512]{1,0:T(8,128)(2,1)S(1)}, bf16[256,512]{1,0:T(8,128)(2,1)S(1)}, u32[]{:S(2)}, u32[]{:S(2)}) %collective-permute-start.1) | collective-permute-done | bytes 262176 | tf_op jit(solution)/shard_map/ppermute | solution.py:39
  32.2 1.9 %collective-permute-start.2 = (bf16[256,512]{1,0:T(8,128)(2,1)S(1)}, bf16[256,512]{1,0:T(8,128)(2,1)S(1)}, u32[]{:S(2)}, u32[]{:S(2)}) collective-permute-start(bf16[256,512]{1,0:T(8,128)(2,1)S(1)} %collective-permute-done.1.refs_7_.refs_6_), channel_id=1, source_target_pairs={{0,8},{8,16},{16,24},{24,32},{32,40},{40,48},{48,56},{56,64},{64,7... | collective-permute-start | bytes 786440 | tf_op jit(solution)/shard_map/ppermute | solution.py:39
  34.4 0.2 rows.1
  34.6 2.1 %collective-permute-done.3.refs_6_.refs_5_ = bf16[256,512]{1,0:T(8,128)(2,1)S(1)} collective-permute-done((bf16[256,512]{1,0:T(8,128)(2,1)S(1)}, bf16[256,512]{1,0:T(8,128)(2,1)S(1)}, u32[]{:S(2)}, u32[]{:S(2)}) %collective-permute-start.3) | collective-permute-done | bytes 262176 | tf_op jit(solution)/shard_map/ppermute | solution.py:39
  36.7 1.9 %collective-permute-start.5 = (bf16[256,512]{1,0:T(8,128)(2,1)S(1)}, bf16[256,512]{1,0:T(8,128)(2,1)S(1)}, u32[]{:S(2)}, u32[]{:S(2)}) collective-permute-start(bf16[256,512]{1,0:T(8,128)(2,1)S(1)} %collective-permute-done.3.refs_6_.refs_5_), channel_id=1, source_target_pairs={{0,8},{8,16},{16,24},{24,32},{32,40},{40,48},{48,56},{56,64},{64,7... | collective-permute-start | bytes 786440 | tf_op jit(solution)/shard_map/ppermute | solution.py:39
  38.6 3.3 %stats.4.refs_6_ = f32[2,3,8,1024]{3,2,1,0:T(8,128)S(1)} custom-call(s32[4,14]{1,0:T(4,128)S(1)} %fusion.refs_0_.refs_1_, s32[1,512]{1,0:T(1,128)S(1)} %bitcast.16, bf16[2,1024,128]{2,1,0:T(8,128)(2,1)S(1)} %get-tuple-element.35.refs_2_.refs_3_, bf16[2,1024,128]{2,1,0:T(8,128)(2,1)S(1)} %get-tuple-element.36.refs_3_.refs_4_, bf16[256,512]{1,0:T(8,128)(2,1)S(1)} %bitcast.11, ...), custom_call_target="tpu_custom_call" | custom-call | flops 1024 | bytes 196608 | tf_op jit(solution)/shard_map/stats/pallas_call | solution.py:197
  41.9 1.8 %collective-permute-done.2.refs_5_.refs_6_ = bf16[256,512]{1,0:T(8,128)(2,1)S(1)} collective-permute-done((bf16[256,512]{1,0:T(8,128)(2,1)S(1)}, bf16[256,512]{1,0:T(8,128)(2,1)S(1)}, u32[]{:S(2)}, u32[]{:S(2)}) %collective-permute-start.2) | collective-permute-done | bytes 262176 | tf_op jit(solution)/shard_map/ppermute | solution.py:39
  43.7 1.9 %collective-permute-start.4 = (bf16[256,512]{1,0:T(8,128)(2,1)S(1)}, bf16[256,512]{1,0:T(8,128)(2,1)S(1)}, u32[]{:S(2)}, u32[]{:S(2)}) collective-permute-start(bf16[256,512]{1,0:T(8,128)(2,1)S(1)} %collective-permute-done.2.refs_5_.refs_6_), channel_id=1, source_target_pairs={{0,8},{8,16},{16,24},{24,32},{32,40},{40,48},{48,56},{56,64},{64,7... | collective-permute-start | bytes 786440 | tf_op jit(solution)/shard_map/ppermute | solution.py:39
  45.6 4.1 %collective-permute-done.5.refs_4_.refs_5_ = bf16[256,512]{1,0:T(8,128)(2,1)S(1)} collective-permute-done((bf16[256,512]{1,0:T(8,128)(2,1)S(1)}, bf16[256,512]{1,0:T(8,128)(2,1)S(1)}, u32[]{:S(2)}, u32[]{:S(2)}) %collective-permute-start.5) | collective-permute-done | bytes 262176 | tf_op jit(solution)/shard_map/ppermute | solution.py:39
  49.7 1.9 %collective-permute-start.7 = (bf16[256,512]{1,0:T(8,128)(2,1)S(1)}, bf16[256,512]{1,0:T(8,128)(2,1)S(1)}, u32[]{:S(2)}, u32[]{:S(2)}) collective-permute-start(bf16[256,512]{1,0:T(8,128)(2,1)S(1)} %collective-permute-done.5.refs_4_.refs_5_), channel_id=1, source_target_pairs={{0,8},{8,16},{16,24},{24,32},{32,40},{40,48},{48,56},{56,64},{64,7... | collective-permute-start | bytes 786440 | tf_op jit(solution)/shard_map/ppermute | solution.py:39
  51.6 2.3 %stats.5.refs_6_ = f32[2,3,8,1024]{3,2,1,0:T(8,128)S(1)} custom-call(s32[4,14]{1,0:T(4,128)S(1)} %fusion.refs_0_.refs_1_, s32[1,512]{1,0:T(1,128)S(1)} %bitcast.17, bf16[2,1024,128]{2,1,0:T(8,128)(2,1)S(1)} %get-tuple-element.35.refs_2_.refs_3_, bf16[2,1024,128]{2,1,0:T(8,128)(2,1)S(1)} %get-tuple-element.36.refs_3_.refs_4_, ...), custom_call_target="tpu_custom_call" | custom-call | flops 1024 | bytes 196608 | tf_op jit(solution)/shard_map/stats/pallas_call | solution.py:197
  53.9 1.0 collective-permute-done.4.refs_5_.refs_6_
  54.9 2.0 %collective-permute-start.6 = (bf16[256,512]{1,0:T(8,128)(2,1)S(1)}, bf16[256,512]{1,0:T(8,128)(2,1)S(1)}, u32[]{:S(2)}, u32[]{:S(2)}) collective-permute-start(bf16[256,512]{1,0:T(8,128)(2,1)S(1)} %collective-permute-done.4.refs_5_.refs_6_), channel_id=1, source_target_pairs={{0,8},{8,16},{16,24},{24,32},{32,40},{40,48},{48,56},{56,64},{64,7... | collective-permute-start | bytes 786440 | tf_op jit(solution)/shard_map/ppermute | solution.py:39
  56.9 5.8 %collective-permute-done.7.refs_4_.refs_5_ = bf16[256,512]{1,0:T(8,128)(2,1)S(1)} collective-permute-done((bf16[256,512]{1,0:T(8,128)(2,1)S(1)}, bf16[256,512]{1,0:T(8,128)(2,1)S(1)}, u32[]{:S(2)}, u32[]{:S(2)}) %collective-permute-start.7) | collective-permute-done | bytes 262176 | tf_op jit(solution)/shard_map/ppermute | solution.py:39
  62.7 2.2 %stats.6.refs_5_ = f32[2,3,8,1024]{3,2,1,0:T(8,128)S(1)} custom-call(s32[4,14]{1,0:T(4,128)S(1)} %fusion.refs_0_.refs_1_, s32[1,512]{1,0:T(1,128)S(1)} %bitcast.18, bf16[2,1024,128]{2,1,0:T(8,128)(2,1)S(1)} %get-tuple-element.35.refs_2_.refs_3_, bf16[2,1024,128]{2,1,0:T(8,128)(2,1)S(1)} %get-tuple-element.36.refs_3_.refs_4_, ...), custom_call_target="tpu_custom_call" | custom-call | flops 1024 | bytes 196608 | tf_op jit(solution)/shard_map/stats/pallas_call | solution.py:197
  64.9 0.8 collective-permute-done.6.refs_4_.refs_5_
  65.7 1.1 stats.7.refs_4_.refs_5_
  66.7 1.7 %grads.5 = (bf16[256,512]{1,0:T(8,128)(2,1)S(1)}, f32[2,128,1024]{2,1,0:T(8,128)S(1)}) custom-call(s32[4,14]{1,0:T(4,128)S(1)} %fusion.refs_0_.refs_1_, s32[1,512]{1,0:T(1,128)S(1)} %bitcast.20, bf16[2,1024,128]{2,1,0:T(8,128)(2,1)S(1)} %get-tuple-element.35.refs_2_.refs_3_, bf16[2,1024,128]{2,1,0:T(8,128)(2,1)S(1)} %get-tuple-element.36.refs_3_.refs_4_, ...), custom_call_target="tpu_custom_call" | custom-call | flops 1024 | bytes 1310720 | tf_op jit(solution)/shard_map/grads/pallas_call | solution.py:291
  68.5 2.7 %collective-permute-start.8 = (bf16[256,512]{1,0:T(8,128)(2,1)S(1)}, bf16[256,512]{1,0:T(8,128)(2,1)S(1)}, u32[]{:S(2)}, u32[]{:S(2)}) collective-permute-start(bf16[256,512]{1,0:T(8,128)(2,1)S(1)} %get-tuple-element.45), channel_id=1, source_target_pairs={{8,0},{16,8},{24,16},{32,24},{40,32},{48,40},{56,48},{64,56},{72,6... | collective-permute-start | bytes 786440 | tf_op jit(solution)/shard_map/ppermute | solution.py:39
  71.2 3.3 %grads.6 = (bf16[256,512]{1,0:T(8,128)(2,1)S(1)}, f32[256,512]{1,0:T(8,128)S(1)}, f32[2,128,1024]{2,1,0:T(8,128)S(1)}) custom-call(s32[4,14]{1,0:T(4,128)S(1)} %fusion.refs_0_.refs_1_, s32[1,512]{1,0:T(1,128)S(1)} %bitcast.21, bf16[2,1024,128]{2,1,0:T(8,128)(2,1)S(1)} %get-tuple-element.35.refs_2_.refs_3_, ...), custom_call_target="tpu_custom_call", output_to_operand_aliasing={{2}: (7, {})} | custom-call | flops 1024 | bytes 1835008 | tf_op jit(solution)/shard_map/grads/pallas_call | solution.py:291
  74.5 2.7 %collective-permute-start.10 = (bf16[256,512]{1,0:T(8,128)(2,1)S(1)}, bf16[256,512]{1,0:T(8,128)(2,1)S(1)}, u32[]{:S(2)}, u32[]{:S(2)}) collective-permute-start(bf16[256,512]{1,0:T(8,128)(2,1)S(1)} %get-tuple-element.53), channel_id=1, source_target_pairs={{8,0},{16,8},{24,16},{32,24},{40,32},{48,40},{56,48},{64,56},{72,6... | collective-permute-start | bytes 786440 | tf_op jit(solution)/shard_map/ppermute | solution.py:39
  77.2 0.3 collective-permute-done.8
  77.6 3.8 %collective-permute-start.9 = (bf16[256,512]{1,0:T(8,128)(2,1)S(1)}, bf16[256,512]{1,0:T(8,128)(2,1)S(1)}, u32[]{:S(2)}, u32[]{:S(2)}) collective-permute-start(bf16[256,512]{1,0:T(8,128)(2,1)S(1)} %add_convert_fusion.5), channel_id=1, source_target_pairs={{8,0},{16,8},{24,16},{32,24},{40,32},{48,40},{56,48},{64,56},{72,6... | collective-permute-start | bytes 786440 | tf_op jit(solution)/shard_map/ppermute | solution.py:39
  81.5 3.4 %grads.7 = (f32[256,512]{1,0:T(8,128)S(1)}, f32[256,512]{1,0:T(8,128)S(1)}, f32[2,128,1024]{2,1,0:T(8,128)S(1)}) custom-call(s32[4,14]{1,0:T(4,128)S(1)} %fusion.refs_0_.refs_1_, s32[1,512]{1,0:T(1,128)S(1)} %bitcast.22, bf16[2,1024,128]{2,1,0:T(8,128)(2,1)S(1)} %get-tuple-element.35.refs_2_.refs_3_, ...), custom_call_target="tpu_custom_call", output_to_operand_aliasing={{2}: (7, {})} | custom-call | flops 1024 | bytes 2097152 | tf_op jit(solution)/shard_map/grads/pallas_call | solution.py:291
  84.9 0.3 collective-permute-done.10
  85.2 4.6 %collective-permute-start.11 = (bf16[256,512]{1,0:T(8,128)(2,1)S(1)}, bf16[256,512]{1,0:T(8,128)(2,1)S(1)}, u32[]{:S(2)}, u32[]{:S(2)}) collective-permute-start(bf16[256,512]{1,0:T(8,128)(2,1)S(1)} %add_convert_fusion.4), channel_id=1, source_target_pairs={{8,0},{16,8},{24,16},{32,24},{40,32},{48,40},{56,48},{64,56},{72,6... | collective-permute-start | bytes 786440 | tf_op jit(solution)/shard_map/ppermute | solution.py:39
  89.9 0.8 collective-permute-done.9
  90.8 3.7 %collective-permute-start.12 = (bf16[256,512]{1,0:T(8,128)(2,1)S(1)}, bf16[256,512]{1,0:T(8,128)(2,1)S(1)}, u32[]{:S(2)}, u32[]{:S(2)}) collective-permute-start(bf16[256,512]{1,0:T(8,128)(2,1)S(1)} %add_convert_fusion.2), channel_id=1, source_target_pairs={{8,0},{16,8},{24,16},{32,24},{40,32},{48,40},{56,48},{64,56},{72,6... | collective-permute-start | bytes 786440 | tf_op jit(solution)/shard_map/ppermute | solution.py:39
  94.6 3.4 %grads.8 = (f32[256,512]{1,0:T(8,128)S(1)}, f32[256,512]{1,0:T(8,128)S(1)}, f32[2,128,1024]{2,1,0:T(8,128)S(1)}) custom-call(s32[4,14]{1,0:T(4,128)S(1)} %fusion.refs_0_.refs_1_, s32[1,512]{1,0:T(1,128)S(1)} %bitcast.23, bf16[2,1024,128]{2,1,0:T(8,128)(2,1)S(1)} %get-tuple-element.35.refs_2_.refs_3_, ...), custom_call_target="tpu_custom_call", output_to_operand_aliasing={{2}: (7, {})} | custom-call | flops 1024 | bytes 2097152 | tf_op jit(solution)/shard_map/grads/pallas_call | solution.py:291
  98.1 3.1 %grads.9 = (f32[512,512]{1,0:T(8,128)S(1)}, f32[256,512]{1,0:T(8,128)S(1)}, bf16[256,512]{1,0:T(8,128)(2,1)S(1)}) custom-call(s32[1]{0:T(128)} %bitcast.low_ref.refs_0_, s32[4,14]{1,0:T(4,128)S(1)} %fusion.refs_0_.refs_1_, s32[1,512]{1,0:T(1,128)S(1)} %bitcast.24, bf16[2,1024,128]{2,1,0:T(8,128)(2,1)S(1)} %get-tuple-element.35.refs_2_.refs_3_, ...), custom_call_target="tpu_custom_call" | custom-call | flops 1024 | bytes 1835008 | tf_op jit(solution)/shard_map/grads/pallas_call | solution.py:291
  101.2 0.3 collective-permute-start.13
  101.6 3.6 %collective-permute-start.14 = (bf16[256,512]{1,0:T(8,128)(2,1)S(1)}, bf16[256,512]{1,0:T(8,128)(2,1)S(1)}, u32[]{:S(2)}, u32[]{:S(2)}) collective-permute-start(bf16[256,512]{1,0:T(8,128)(2,1)S(1)} %add_convert_fusion.1), channel_id=1, source_target_pairs={{8,0},{16,8},{24,16},{32,24},{40,32},{48,40},{56,48},{64,56},{72,6... | collective-permute-start | bytes 786440 | tf_op jit(solution)/shard_map/ppermute | solution.py:39
  105.3 1.9 %collective-permute-start.15 = (bf16[256,512]{1,0:T(8,128)(2,1)S(1)}, bf16[256,512]{1,0:T(8,128)(2,1)S(1)}, u32[]{:S(2)}, u32[]{:S(2)}) collective-permute-start(bf16[256,512]{1,0:T(8,128)(2,1)S(1)} %add_convert_fusion.3), channel_id=1, source_target_pairs={{8,0},{16,8},{24,16},{32,24},{40,32},{48,40},{56,48},{64,56},{72,6... | collective-permute-start | bytes 786440 | tf_op jit(solution)/shard_map/ppermute | solution.py:39
  107.2 0.5 collective-permute-done.13.other_ref
  107.7 2.3 %collective-permute-done.14 = bf16[256,512]{1,0:T(8,128)(2,1)S(1)} collective-permute-done((bf16[256,512]{1,0:T(8,128)(2,1)S(1)}, bf16[256,512]{1,0:T(8,128)(2,1)S(1)}, u32[]{:S(2)}, u32[]{:S(2)}) %collective-permute-start.14) | collective-permute-done | bytes 262176 | tf_op jit(solution)/shard_map/ppermute | solution.py:39
  110.0 3.6 %collective-permute-done.15 = bf16[256,512]{1,0:T(8,128)(2,1)S(1)} collective-permute-done((bf16[256,512]{1,0:T(8,128)(2,1)S(1)}, bf16[256,512]{1,0:T(8,128)(2,1)S(1)}, u32[]{:S(2)}, u32[]{:S(2)}) %collective-permute-start.15) | collective-permute-done | bytes 262176 | tf_op jit(solution)/shard_map/ppermute | solution.py:39
  113.5 1.0 add_convert_fusion
  114.5 3.8 %all-to-all-start.1 = ((bf16[8,64,512]{2,1,0:T(8,128)(2,1)}), bf16[8,64,512]{2,1,0:T(8,128)(2,1)S(1)}, u32[]{:S(2)}, u32[]{:S(2)}) async-start(bf16[8,64,512]{2,1,0:T(8,128)(2,1)} %bitcast.7), calls=%async_computation.1 | async-start | bytes 1048576 | tf_op jit(solution)/shard_map/all_to_all | solution.py:357
  118.4 1.0 columns.1
  119.4 9.0 %all-to-all-done.1.in_ref = bf16[8,64,512]{2,1,0:T(8,128)(2,1)S(1)} async-done(((bf16[8,64,512]{2,1,0:T(8,128)(2,1)}), bf16[8,64,512]{2,1,0:T(8,128)(2,1)S(1)}, u32[]{:S(2)}, u32[]{:S(2)}) %all-to-all-start.1) | async-done | bytes 524320 | tf_op jit(solution)/shard_map/all_to_all | solution.py:357
  128.4 1.0 unpack.1
  (26 shorter events, 1.1 us)
Async XLA Ops:
  0.6 8.5 %copy-start = (s32[2,128,14]{1,0,2:T(2,128)S(1)}, s32[2,128,14]{1,0,2:T(2,128)}, u32[]{:S(2)}) copy-start(s32[2,128,14]{1,0,2:T(2,128)} %param.11) | copy-start | bytes 43012
  0.6 6.3 %copy-start.2 = (bf16[256,1024]{1,0:T(8,128)(2,1)S(1)}, bf16[256,1024]{1,0:T(8,128)(2,1)}, u32[]{:S(2)}) copy-start(bf16[256,1024]{1,0:T(8,128)(2,1)} %do_ref.1) | copy-start | bytes 1572868
  0.7 6.3 %copy-start.1 = (bf16[256,1024]{1,0:T(8,128)(2,1)S(1)}, bf16[256,1024]{1,0:T(8,128)(2,1)}, u32[]{:S(2)}) copy-start(bf16[256,1024]{1,0:T(8,128)(2,1)} %q_ref.1) | copy-start | bytes 1572868
  2.6 14.4 %all-to-all-start = ((bf16[8,64,512]{2,1,0:T(8,128)(2,1)}), bf16[8,64,512]{2,1,0:T(8,128)(2,1)S(1)}, u32[]{:S(2)}, u32[]{:S(2)}) async-start(bf16[8,64,512]{2,1,0:T(8,128)(2,1)} %pack.1), calls=%async_computation | async-start | bytes 1048576 | tf_op jit(solution)/shard_map/all_to_all | solution.py:316
  6.9 2.3 %copy-start.3 = (s32[16384]{0:T(1024)S(1)}, s32[16384]{0:T(1024)}, u32[]{:S(2)}) copy-start(s32[16384]{0:T(1024)} %param.10) | copy-start | bytes 196612
  7.1 27.3 %collective-permute-start = (bf16[2,256,512]{2,1,0:T(8,128)(2,1)S(1)}, bf16[2,256,512]{2,1,0:T(8,128)(2,1)S(1)}, u32[]{:S(2)}, u32[]{:S(2)}) collective-permute-start(bf16[2,256,512]{2,1,0:T(8,128)(2,1)S(1)} %pad_maximum_fusion), channel_id=1, source_target_pairs={{0,4},{4,0},{1,5},{5,1},{2,6},{6,2},{3,7},{7,3},{8,12},{12,8},{9,1... | collective-permute-start | bytes 1572872 | tf_op jit(solution)/shard_map/ppermute | solution.py:43
  17.0 15.2 %collective-permute-start.1 = (bf16[256,512]{1,0:T(8,128)(2,1)S(1)}, bf16[256,512]{1,0:T(8,128)(2,1)S(1)}, u32[]{:S(2)}, u32[]{:S(2)}) collective-permute-start(bf16[256,512]{1,0:T(8,128)(2,1)S(1)} %bitcast.13), channel_id=1, source_target_pairs={{0,8},{8,16},{16,24},{24,32},{32,40},{40,48},{48,56},{56,64},{64,7... | collective-permute-start | bytes 786440 | tf_op jit(solution)/shard_map/ppermute | solution.py:39
  21.6 15.1 %collective-permute-start.3 = (bf16[256,512]{1,0:T(8,128)(2,1)S(1)}, bf16[256,512]{1,0:T(8,128)(2,1)S(1)}, u32[]{:S(2)}, u32[]{:S(2)}) collective-permute-start(bf16[256,512]{1,0:T(8,128)(2,1)S(1)} %bitcast.10), channel_id=1, source_target_pairs={{0,8},{8,16},{16,24},{24,32},{32,40},{40,48},{48,56},{56,64},{64,7... | collective-permute-start | bytes 786440 | tf_op jit(solution)/shard_map/ppermute | solution.py:39
  32.2 11.5 %collective-permute-start.2 = (bf16[256,512]{1,0:T(8,128)(2,1)S(1)}, bf16[256,512]{1,0:T(8,128)(2,1)S(1)}, u32[]{:S(2)}, u32[]{:S(2)}) collective-permute-start(bf16[256,512]{1,0:T(8,128)(2,1)S(1)} %collective-permute-done.1.refs_7_.refs_6_), channel_id=1, source_target_pairs={{0,8},{8,16},{16,24},{24,32},{32,40},{40,48},{48,56},{56,64},{64,7... | collective-permute-start | bytes 786440 | tf_op jit(solution)/shard_map/ppermute | solution.py:39
  36.7 13.0 %collective-permute-start.5 = (bf16[256,512]{1,0:T(8,128)(2,1)S(1)}, bf16[256,512]{1,0:T(8,128)(2,1)S(1)}, u32[]{:S(2)}, u32[]{:S(2)}) collective-permute-start(bf16[256,512]{1,0:T(8,128)(2,1)S(1)} %collective-permute-done.3.refs_6_.refs_5_), channel_id=1, source_target_pairs={{0,8},{8,16},{16,24},{24,32},{32,40},{40,48},{48,56},{56,64},{64,7... | collective-permute-start | bytes 786440 | tf_op jit(solution)/shard_map/ppermute | solution.py:39
  43.7 11.2 %collective-permute-start.4 = (bf16[256,512]{1,0:T(8,128)(2,1)S(1)}, bf16[256,512]{1,0:T(8,128)(2,1)S(1)}, u32[]{:S(2)}, u32[]{:S(2)}) collective-permute-start(bf16[256,512]{1,0:T(8,128)(2,1)S(1)} %collective-permute-done.2.refs_5_.refs_6_), channel_id=1, source_target_pairs={{0,8},{8,16},{16,24},{24,32},{32,40},{40,48},{48,56},{56,64},{64,7... | collective-permute-start | bytes 786440 | tf_op jit(solution)/shard_map/ppermute | solution.py:39
  49.7 13.0 %collective-permute-start.7 = (bf16[256,512]{1,0:T(8,128)(2,1)S(1)}, bf16[256,512]{1,0:T(8,128)(2,1)S(1)}, u32[]{:S(2)}, u32[]{:S(2)}) collective-permute-start(bf16[256,512]{1,0:T(8,128)(2,1)S(1)} %collective-permute-done.5.refs_4_.refs_5_), channel_id=1, source_target_pairs={{0,8},{8,16},{16,24},{24,32},{32,40},{40,48},{48,56},{56,64},{64,7... | collective-permute-start | bytes 786440 | tf_op jit(solution)/shard_map/ppermute | solution.py:39
  54.9 10.8 %collective-permute-start.6 = (bf16[256,512]{1,0:T(8,128)(2,1)S(1)}, bf16[256,512]{1,0:T(8,128)(2,1)S(1)}, u32[]{:S(2)}, u32[]{:S(2)}) collective-permute-start(bf16[256,512]{1,0:T(8,128)(2,1)S(1)} %collective-permute-done.4.refs_5_.refs_6_), channel_id=1, source_target_pairs={{0,8},{8,16},{16,24},{24,32},{32,40},{40,48},{48,56},{56,64},{64,7... | collective-permute-start | bytes 786440 | tf_op jit(solution)/shard_map/ppermute | solution.py:39
  68.5 9.1 %collective-permute-start.8 = (bf16[256,512]{1,0:T(8,128)(2,1)S(1)}, bf16[256,512]{1,0:T(8,128)(2,1)S(1)}, u32[]{:S(2)}, u32[]{:S(2)}) collective-permute-start(bf16[256,512]{1,0:T(8,128)(2,1)S(1)} %get-tuple-element.45), channel_id=1, source_target_pairs={{8,0},{16,8},{24,16},{32,24},{40,32},{48,40},{56,48},{64,56},{72,6... | collective-permute-start | bytes 786440 | tf_op jit(solution)/shard_map/ppermute | solution.py:39
  74.5 10.6 %collective-permute-start.10 = (bf16[256,512]{1,0:T(8,128)(2,1)S(1)}, bf16[256,512]{1,0:T(8,128)(2,1)S(1)}, u32[]{:S(2)}, u32[]{:S(2)}) collective-permute-start(bf16[256,512]{1,0:T(8,128)(2,1)S(1)} %get-tuple-element.53), channel_id=1, source_target_pairs={{8,0},{16,8},{24,16},{32,24},{40,32},{48,40},{56,48},{64,56},{72,6... | collective-permute-start | bytes 786440 | tf_op jit(solution)/shard_map/ppermute | solution.py:39
  77.6 13.1 %collective-permute-start.9 = (bf16[256,512]{1,0:T(8,128)(2,1)S(1)}, bf16[256,512]{1,0:T(8,128)(2,1)S(1)}, u32[]{:S(2)}, u32[]{:S(2)}) collective-permute-start(bf16[256,512]{1,0:T(8,128)(2,1)S(1)} %add_convert_fusion.5), channel_id=1, source_target_pairs={{8,0},{16,8},{24,16},{32,24},{40,32},{48,40},{56,48},{64,56},{72,6... | collective-permute-start | bytes 786440 | tf_op jit(solution)/shard_map/ppermute | solution.py:39
  85.2 12.7 %collective-permute-start.11 = (bf16[256,512]{1,0:T(8,128)(2,1)S(1)}, bf16[256,512]{1,0:T(8,128)(2,1)S(1)}, u32[]{:S(2)}, u32[]{:S(2)}) collective-permute-start(bf16[256,512]{1,0:T(8,128)(2,1)S(1)} %add_convert_fusion.4), channel_id=1, source_target_pairs={{8,0},{16,8},{24,16},{32,24},{40,32},{48,40},{56,48},{64,56},{72,6... | collective-permute-start | bytes 786440 | tf_op jit(solution)/shard_map/ppermute | solution.py:39
  90.8 10.4 %collective-permute-start.12 = (bf16[256,512]{1,0:T(8,128)(2,1)S(1)}, bf16[256,512]{1,0:T(8,128)(2,1)S(1)}, u32[]{:S(2)}, u32[]{:S(2)}) collective-permute-start(bf16[256,512]{1,0:T(8,128)(2,1)S(1)} %add_convert_fusion.2), channel_id=1, source_target_pairs={{8,0},{16,8},{24,16},{32,24},{40,32},{48,40},{56,48},{64,56},{72,6... | collective-permute-start | bytes 786440 | tf_op jit(solution)/shard_map/ppermute | solution.py:39
  101.2 6.5 %collective-permute-start.13 = (bf16[256,512]{1,0:T(8,128)(2,1)S(1)}, bf16[256,512]{1,0:T(8,128)(2,1)S(1)}, u32[]{:S(2)}, u32[]{:S(2)}) collective-permute-start(bf16[256,512]{1,0:T(8,128)(2,1)S(1)} %get-tuple-element.58), channel_id=1, source_target_pairs={{0,4},{4,0},{1,5},{5,1},{2,6},{6,2},{3,7},{7,3},{8,12},{12,8},{9,1... | collective-permute-start | bytes 786440 | tf_op jit(solution)/shard_map/ppermute | solution.py:43
  101.6 8.3 %collective-permute-start.14 = (bf16[256,512]{1,0:T(8,128)(2,1)S(1)}, bf16[256,512]{1,0:T(8,128)(2,1)S(1)}, u32[]{:S(2)}, u32[]{:S(2)}) collective-permute-start(bf16[256,512]{1,0:T(8,128)(2,1)S(1)} %add_convert_fusion.1), channel_id=1, source_target_pairs={{8,0},{16,8},{24,16},{32,24},{40,32},{48,40},{56,48},{64,56},{72,6... | collective-permute-start | bytes 786440 | tf_op jit(solution)/shard_map/ppermute | solution.py:39
  105.3 8.3 %collective-permute-start.15 = (bf16[256,512]{1,0:T(8,128)(2,1)S(1)}, bf16[256,512]{1,0:T(8,128)(2,1)S(1)}, u32[]{:S(2)}, u32[]{:S(2)}) collective-permute-start(bf16[256,512]{1,0:T(8,128)(2,1)S(1)} %add_convert_fusion.3), channel_id=1, source_target_pairs={{8,0},{16,8},{24,16},{32,24},{40,32},{48,40},{56,48},{64,56},{72,6... | collective-permute-start | bytes 786440 | tf_op jit(solution)/shard_map/ppermute | solution.py:39
  114.5 13.9 %all-to-all-start.1 = ((bf16[8,64,512]{2,1,0:T(8,128)(2,1)}), bf16[8,64,512]{2,1,0:T(8,128)(2,1)S(1)}, u32[]{:S(2)}, u32[]{:S(2)}) async-start(bf16[8,64,512]{2,1,0:T(8,128)(2,1)} %bitcast.7), calls=%async_computation.1 | async-start | bytes 1048576 | tf_op jit(solution)/shard_map/all_to_all | solution.py:357

commit v4 on v3

--- a/solution.py
+++ b/solution.py
@@ -47,7 +47,7 @@
     return lax.dot_general(a, b, (((da,), (db,)), ((), ())), preferred_element_type=jnp.float32)
 
 
-def call(kernel, name, out_shape, in_specs, scratch=(), aliases=None):
+def call(kernel, name, out_shape, in_specs, scratch=(), aliases=None, light=False):
     outs = out_shape if isinstance(out_shape, (tuple, list)) else (out_shape,)
     size = sum(o.size * o.dtype.itemsize for o in outs)
     return pl.pallas_call(
@@ -58,7 +58,7 @@
         scratch_shapes=scratch,
         input_output_aliases=aliases or {},
         compiler_params=pltpu.CompilerParams(vmem_limit_bytes=32 * 1024 * 1024),
-        cost_estimate=pl.CostEstimate(flops=1024, bytes_accessed=size, transcendentals=0),
+        cost_estimate=pl.CostEstimate(flops=1024, bytes_accessed=1 if light else size, transcendentals=0),
         name=name,
     )
 
@@ -205,6 +205,8 @@
 def grads_kernel(first_blocks, opening, closing, *refs):
     count = len(first_blocks)
     span = 2 * BLOCK
+    query_blocks = min(Q_BLOCKS, first_blocks[-1] + 2)
+    rows_used = query_blocks * PAIR
     if closing:
         low_ref, refs = refs[0], refs[1:]
     hit_ref, start_ref, q_ref, do_ref, norm_ref = refs[:5]
@@ -224,8 +226,7 @@
     for h in range(LOCAL_HEADS):
         kcols = slice(h * HEAD_SIZE, (h + 1) * HEAD_SIZE)
         vcols = slice(WIDTH + h * HEAD_SIZE, WIDTH + (h + 1) * HEAD_SIZE)
-        last_row = 0
-        for i in range(Q_BLOCKS):
+        for i in range(query_blocks):
             lanes = slice(i * PAIR, (i + 1) * PAIR)
             qs = q_ref[h, lanes, :]
             dos = do_ref[h, lanes, :]
@@ -253,9 +254,10 @@
                     ds_scr[h, at, lanes] = ((prob * SCORE_SCALE) * (dp[part] - delta)).astype(jnp.bfloat16)
         keys = [ref[:, kcols] for ref in pieces]
         keys = keys[0] if count == 1 else jnp.concatenate(keys, axis=0)
-        ds = ds_scr[h]
-        dv = dot(p_scr[h], do_ref[h], 1, 0)
-        dk = dot(ds, q_ref[h], 1, 0)
+        used = slice(0, rows_used)
+        ds = ds_scr[h, :, used]
+        dv = dot(p_scr[h, :, used], do_ref[h, used, :], 1, 0)
+        dk = dot(ds, q_ref[h, used, :], 1, 0)
         dqt = dot(keys, ds, 0, 0)
         if not opening:
             dqt = dqt + dqt_in[h]
@@ -267,14 +269,16 @@
                 c = h * PAIR + (b % 2) * BLOCK
                 dq_scr[b // 2 * BLOCK : (b // 2 + 1) * BLOCK, c : c + BLOCK] = dqt[:, b * BLOCK : (b + 1) * BLOCK].T
         else:
-            dqt_out[h] = dqt
+            dqt_out[h, :, used] = dqt
+            if rows_used < ROWS:
+                dqt_out[h, :, rows_used:] = jnp.zeros((HEAD_SIZE, ROWS - rows_used), jnp.float32)
     if closing:
         low = low_ref[0]
         mine_ref[...] = dq_scr[pl.ds(pl.multiple_of(low * SPAN, SPAN), SPAN), :]
         send_ref[...] = dq_scr[pl.ds(pl.multiple_of((1 - low) * SPAN, SPAN), SPAN), :].astype(jnp.bfloat16)
 
 
-def grads(first_blocks, tables, norm, pieces, dqt, dtypes, low=None):
+def grads(first_blocks, tables, norm, pieces, dqt, dtypes, low=None, light=False):
     opening, closing = dqt is None, low is not None
     count = len(pieces)
     rows = SPAN * count // len(dtypes)
@@ -295,7 +299,24 @@
         specs,
         scratch=scratch,
         aliases=aliases,
+        light=light,
     )(*operands)
+
+
+def finish_kernel(hit_ref, start_ref, q_ref, do_ref, piece, state, norm_ref, far_ref, dqt_ref, p_scr, ds_scr):
+    tables = (hit_ref, start_ref, q_ref, do_ref)
+    stats_kernel((0,), False, True, *tables, piece, state, norm_ref)
+    grads_kernel((0,), True, False, *tables, norm_ref, piece, far_ref, dqt_ref, p_scr, ds_scr)
+
+
+def finish(tables, piece, state):
+    return call(
+        finish_kernel,
+        "finish",
+        (f32(LOCAL_HEADS, 8, ROWS), bf16(SPAN, 2 * WIDTH), f32(LOCAL_HEADS, HEAD_SIZE, ROWS)),
+        [SMEM_SPEC] + [VMEM_SPEC] * 5,
+        scratch=[pltpu.VMEM((LOCAL_HEADS, SPAN, 2 * PAIR), jnp.bfloat16)] * 2,
+    )(*tables, piece, state)
 
 
 def per_device(queries, output_gradient, key_states, value_inputs, turn_ids, listed):
@@ -347,12 +368,9 @@
     b4 = slab_shift(b3, 1)
     state = stats((2, 4), tables, (a3, b3), state, False)
     b4, state = lax.optimization_barrier((b4, state))
-    norm = stats((0,), tables, (b4,), state, True)
+    norm, gb4, dqt = finish(tables, b4, state)
 
     low16, full = jnp.bfloat16, jnp.float32
-    def after(arrived, *values):
-        return lax.optimization_barrier((arrived,) + values)[1:]
-
     def to_owners(x):
         return lax.all_to_all(x.reshape(8, SPAN // 4, 2 * WIDTH), MEMBER_AXES, 0, 0, tiled=True)
 
@@ -362,25 +380,25 @@
     def summed(part, arrived):
         return (part + arrived.astype(full)).astype(low16)
 
-    gb4, dqt = grads((0,), tables, norm, (b4,), None, (low16,))
     rb = slab_shift(gb4, -1)
-    ga3, gb3, dqt = grads((2, 4), tables, norm, (a3, b3), dqt, (low16, full))
+    ga3, gb3, dqt = grads((2, 4), tables, norm, (a3, b3), dqt, (low16, full), light=True)
     ra = slab_shift(ga3, -1)
-    (dqt,) = after(rb, dqt)
+    g0, dqt = grads((14, 16), tables, norm, (a0, b0), dqt, (full,), light=True)
+    dqt, rb = lax.optimization_barrier((dqt, rb))
     rb = slab_shift(summed(gb3, rb), -1)
+    dqt, ra = lax.optimization_barrier((dqt, ra))
     ga2, gb2, dqt = grads((6, 8), tables, norm, (a2, b2), dqt, (full, full))
     ra = slab_shift(summed(ga2, ra), -1)
-    (dqt,) = after(rb, dqt)
+    dqt, rb = lax.optimization_barrier((dqt, rb))
     rb = slab_shift(summed(gb2, rb), -1)
-    ga1, gb1, dqt = grads((10, 12), tables, norm, (a1, b1), dqt, (full, full))
-    dqt, ra = lax.optimization_barrier((dqt, summed(ga1, ra)))
-    ra = slab_shift(ra, -1)
-    g0, mine, send = grads((14, 16), tables, norm, (a0, b0), dqt, (full,), low_ref)
-    send, rb = lax.optimization_barrier((send, rb))
+    ga1, gb1, mine, send = grads((10, 12), tables, norm, (a1, b1), dqt, (full, full), low_ref)
+    ra = slab_shift(summed(ga1, ra), -1)
     rb = slab_shift(summed(gb1, rb), -1)
     other = low_swap(send)
     other, rb = lax.optimization_barrier((other, rb))
-    total = to_owners((g0 + jnp.concatenate([ra, rb], axis=0).astype(full)).astype(low16))
+    total = lax.dynamic_update_slice(jnp.zeros((SLAB, 2 * WIDTH), low16), summed(g0[:SPAN], ra), (0, 0))
+    total, rb = lax.optimization_barrier((total, rb))
+    total = to_owners(lax.dynamic_update_slice(total, summed(g0[SPAN:], rb), (SPAN, 0)))
     grad_keys, grad_values = call(
         unpack_kernel, "unpack", (f32(SPAN // 4, KEY_VALUE_HEADS * HEAD_SIZE),) * 2, [VMEM_SPEC]
     )(total)

time: 130 us -> 127 us (0.977)
  waiting for transfers between devices: 46.7 us -> 42.1 us
  starting transfers between devices: 51.1 us -> 53 us
    ppermute x14, waiting for transfers between devices: 29.6 us -> 25.4 us  [slab_shift(): lax.ppermute(x, SLAB_AXES, [(i, i + by) for i in range(count) if 0 <= i +...]
    ppermute x14, starting transfers between devices: 40.5 us -> 42.4 us  [slab_shift(): lax.ppermute(x, SLAB_AXES, [(i, i + by) for i in range(count) if 0 <= i +...]
    pallas_call x0 -> x1, Pallas kernels: none -> 1.72 us  [finish(): call(finish_kernel, 'finish', (f32(LOCAL_HEADS, 8, ROWS), bf16(SPAN, 2 *...]
    pallas_call x5 -> x4, Pallas kernels: 15 us -> 13.3 us  [grads(): call(functools.partial(grads_kernel, first_blocks, opening, closing), 'gr...]
    pallas_call x4 -> x3, Pallas kernels: 8.83 us -> 7.78 us  [stats(): call(functools.partial(stats_kernel, first_blocks, opening, closing), 'st...]
  transfers between devices with their start and end apart: 18 -> 18, of which waited for: 15 -> 11; matrix products, arithmetic and copies ran while one was open for 1% -> 2% of each run, Pallas kernels for 17% -> 18%
where the time goes in v4:
time: 127 us; the launch traced here: 126 us
  starting transfers between devices  53 us (42%)
  waiting for transfers between devices  42.1 us (33%)
  Pallas kernels  27 us (21%)
  other arithmetic  2 us (2%)
  local copies, waits for them, and re-layouts  1.37 us (1%)
    ppermute x14, starting transfers between devices, slab_shift(): lax.ppermute(x, SLAB_AXES, [(i, i + by) for i in range(count) if 0 <= i +...  42.4 us
    ppermute x14, waiting for transfers between devices, slab_shift(): lax.ppermute(x, SLAB_AXES, [(i, i + by) for i in range(count) if 0 <= i +...  25.4 us
    pallas_call x4, Pallas kernels, grads(): call(functools.partial(grads_kernel, first_blocks, opening, closing), 'gr...  13.3 us
    all_to_all x1, waiting for transfers between devices, to_owners(): lax.all_to_all(x.reshape(8, SPAN // 4, 2 * WIDTH), MEMBER_AXES, 0, 0, til...  9.02 us
    pallas_call x3, Pallas kernels, stats(): call(functools.partial(stats_kernel, first_blocks, opening, closing), 'st...  7.78 us
    all_to_all x1, waiting for transfers between devices, per_device(): own = lax.all_to_all(kv, MEMBER_AXES, 0, 0, tiled=True)  7.64 us
    all_to_all x1, starting transfers between devices, per_device(): own = lax.all_to_all(kv, MEMBER_AXES, 0, 0, tiled=True)  4.31 us
    all_to_all x1, starting transfers between devices, to_owners(): lax.all_to_all(x.reshape(8, SPAN // 4, 2 * WIDTH), MEMBER_AXES, 0, 0, til...  3.88 us
  transfers between devices with their start and end apart: 18, of which 11 were waited for; matrix products, arithmetic and copies ran while one was open for 2% of the time, Pallas kernels for 18%

profile of v4, /device:TPU:24, one launch (start us, length us, event | category | flops | bytes accessed | tf_op | source)
XLA Modules:
  0.0 126.4 jit_solution(5076352742830173401)
XLA Ops:
  0.7 1.9 %pack.1 = bf16[8,64,512]{2,1,0:T(8,128)(2,1)} custom-call(bf16[64,2048]{1,0:T(8,128)(2,1)} %k_ref.1, bf16[64,2048]{1,0:T(8,128)(2,1)} %v_ref.1), custom_call_target="tpu_custom_call" | custom-call | tf_op jit(solution)/shard_map/pack/pallas_call | solution.py:328
  2.6 4.3 %all-to-all-start = ((bf16[8,64,512]{2,1,0:T(8,128)(2,1)}), bf16[8,64,512]{2,1,0:T(8,128)(2,1)S(1)}, u32[]{:S(2)}, u32[]{:S(2)}) async-start(bf16[8,64,512]{2,1,0:T(8,128)(2,1)} %pack.1), calls=%async_computation | async-start | bytes 1048576 | tf_op jit(solution)/shard_map/all_to_all | solution.py:337
  7.1 2.1 %collective-permute-start = (bf16[2,256,512]{2,1,0:T(8,128)(2,1)S(1)}, bf16[2,256,512]{2,1,0:T(8,128)(2,1)S(1)}, u32[]{:S(2)}, u32[]{:S(2)}) collective-permute-start(bf16[2,256,512]{2,1,0:T(8,128)(2,1)S(1)} %pad_maximum_fusion), channel_id=1, source_target_pairs={{0,4},{4,0},{1,5},{5,1},{2,6},{6,2},{3,7},{7,3},{8,12},{12,8},{9,1... | collective-permute-start | bytes 1572872 | tf_op jit(solution)/shard_map/ppermute | solution.py:43
  9.3 0.1 pad_dynamic-slice_fusion.1
  9.3 7.6 %all-to-all-done = bf16[8,64,512]{2,1,0:T(8,128)(2,1)S(1)} async-done(((bf16[8,64,512]{2,1,0:T(8,128)(2,1)}), bf16[8,64,512]{2,1,0:T(8,128)(2,1)S(1)}, u32[]{:S(2)}, u32[]{:S(2)}) %all-to-all-start) | async-done | bytes 524320 | tf_op jit(solution)/shard_map/all_to_all | solution.py:337
  17.0 3.8 %collective-permute-start.1 = (bf16[256,512]{1,0:T(8,128)(2,1)S(1)}, bf16[256,512]{1,0:T(8,128)(2,1)S(1)}, u32[]{:S(2)}, u32[]{:S(2)}) collective-permute-start(bf16[256,512]{1,0:T(8,128)(2,1)S(1)} %bitcast.13), channel_id=1, source_target_pairs={{0,8},{8,16},{16,24},{24,32},{32,40},{40,48},{48,56},{56,64},{64,7... | collective-permute-start | bytes 786440 | tf_op jit(solution)/shard_map/ppermute | solution.py:39
  20.9 0.1 pad_dynamic-slice_fusion
  20.9 0.7 convert_reduce_fusion
  21.6 3.8 %collective-permute-start.3 = (bf16[256,512]{1,0:T(8,128)(2,1)S(1)}, bf16[256,512]{1,0:T(8,128)(2,1)S(1)}, u32[]{:S(2)}, u32[]{:S(2)}) collective-permute-start(bf16[256,512]{1,0:T(8,128)(2,1)S(1)} %bitcast.10), channel_id=1, source_target_pairs={{0,8},{8,16},{16,24},{24,32},{32,40},{40,48},{48,56},{56,64},{64,7... | collective-permute-start | bytes 786440 | tf_op jit(solution)/shard_map/ppermute | solution.py:39
  25.4 6.8 %collective-permute-done.1.refs_7_ = bf16[256,512]{1,0:T(8,128)(2,1)S(1)} collective-permute-done((bf16[256,512]{1,0:T(8,128)(2,1)S(1)}, bf16[256,512]{1,0:T(8,128)(2,1)S(1)}, u32[]{:S(2)}, u32[]{:S(2)}) %collective-permute-start.1) | collective-permute-done | bytes 262176 | tf_op jit(solution)/shard_map/ppermute | solution.py:39
  32.2 1.9 %collective-permute-start.2 = (bf16[256,512]{1,0:T(8,128)(2,1)S(1)}, bf16[256,512]{1,0:T(8,128)(2,1)S(1)}, u32[]{:S(2)}, u32[]{:S(2)}) collective-permute-start(bf16[256,512]{1,0:T(8,128)(2,1)S(1)} %collective-permute-done.1.refs_7_), channel_id=1, source_target_pairs={{0,8},{8,16},{16,24},{24,32},{32,40},{40,48},{48,56},{56,64},{64,7... | collective-permute-start | bytes 786440 | tf_op jit(solution)/shard_map/ppermute | solution.py:39
  34.1 0.1 copy.13
  34.2 0.1 rev.3
  34.4 0.2 rows.1
  34.6 2.1 %collective-permute-done.3.refs_6_ = bf16[256,512]{1,0:T(8,128)(2,1)S(1)} collective-permute-done((bf16[256,512]{1,0:T(8,128)(2,1)S(1)}, bf16[256,512]{1,0:T(8,128)(2,1)S(1)}, u32[]{:S(2)}, u32[]{:S(2)}) %collective-permute-start.3) | collective-permute-done | bytes 262176 | tf_op jit(solution)/shard_map/ppermute | solution.py:39
  36.7 1.9 %collective-permute-start.5 = (bf16[256,512]{1,0:T(8,128)(2,1)S(1)}, bf16[256,512]{1,0:T(8,128)(2,1)S(1)}, u32[]{:S(2)}, u32[]{:S(2)}) collective-permute-start(bf16[256,512]{1,0:T(8,128)(2,1)S(1)} %collective-permute-done.3.refs_6_), channel_id=1, source_target_pairs={{0,8},{8,16},{16,24},{24,32},{32,40},{40,48},{48,56},{56,64},{64,7... | collective-permute-start | bytes 786440 | tf_op jit(solution)/shard_map/ppermute | solution.py:39
  38.6 3.3 %stats.3.refs_6_ = f32[2,3,8,1024]{3,2,1,0:T(8,128)S(1)} custom-call(s32[4,14]{1,0:T(4,128)S(1)} %fusion.1.refs_0_.hit_ref.refs_1_, s32[1,512]{1,0:T(1,128)S(1)} %bitcast.16, bf16[2,1024,128]{2,1,0:T(8,128)(2,1)S(1)} %get-tuple-element.38.refs_2_.q_ref.refs_3_, bf16[2,1024,128]{2,1,0:T(8,128)(2,1)S(1)} %get-tuple-element.39.refs_3_.do_ref.refs_4_, ...), custom_call_target="tpu_custom_call" | custom-call | flops 1024 | bytes 196608 | tf_op jit(solution)/shard_map/stats/pallas_call | solution.py:197
  41.9 1.8 %collective-permute-done.2.refs_5_.refs_6_ = bf16[256,512]{1,0:T(8,128)(2,1)S(1)} collective-permute-done((bf16[256,512]{1,0:T(8,128)(2,1)S(1)}, bf16[256,512]{1,0:T(8,128)(2,1)S(1)}, u32[]{:S(2)}, u32[]{:S(2)}) %collective-permute-start.2) | collective-permute-done | bytes 262176 | tf_op jit(solution)/shard_map/ppermute | solution.py:39
  43.7 1.9 %collective-permute-start.4 = (bf16[256,512]{1,0:T(8,128)(2,1)S(1)}, bf16[256,512]{1,0:T(8,128)(2,1)S(1)}, u32[]{:S(2)}, u32[]{:S(2)}) collective-permute-start(bf16[256,512]{1,0:T(8,128)(2,1)S(1)} %collective-permute-done.2.refs_5_.refs_6_), channel_id=1, source_target_pairs={{0,8},{8,16},{16,24},{24,32},{32,40},{40,48},{48,56},{56,64},{64,7... | collective-permute-start | bytes 786440 | tf_op jit(solution)/shard_map/ppermute | solution.py:39
  45.6 4.1 %collective-permute-done.5.refs_4_.refs_5_ = bf16[256,512]{1,0:T(8,128)(2,1)S(1)} collective-permute-done((bf16[256,512]{1,0:T(8,128)(2,1)S(1)}, bf16[256,512]{1,0:T(8,128)(2,1)S(1)}, u32[]{:S(2)}, u32[]{:S(2)}) %collective-permute-start.5) | collective-permute-done | bytes 262176 | tf_op jit(solution)/shard_map/ppermute | solution.py:39
  49.7 1.9 %collective-permute-start.7 = (bf16[256,512]{1,0:T(8,128)(2,1)S(1)}, bf16[256,512]{1,0:T(8,128)(2,1)S(1)}, u32[]{:S(2)}, u32[]{:S(2)}) collective-permute-start(bf16[256,512]{1,0:T(8,128)(2,1)S(1)} %collective-permute-done.5.refs_4_.refs_5_), channel_id=1, source_target_pairs={{0,8},{8,16},{16,24},{24,32},{32,40},{40,48},{48,56},{56,64},{64,7... | collective-permute-start | bytes 786440 | tf_op jit(solution)/shard_map/ppermute | solution.py:39
  51.6 2.3 %stats.4.refs_6_ = f32[2,3,8,1024]{3,2,1,0:T(8,128)S(1)} custom-call(s32[4,14]{1,0:T(4,128)S(1)} %fusion.1.refs_0_.hit_ref.refs_1_, s32[1,512]{1,0:T(1,128)S(1)} %bitcast.17, bf16[2,1024,128]{2,1,0:T(8,128)(2,1)S(1)} %get-tuple-element.38.refs_2_.q_ref.refs_3_, bf16[2,1024,128]{2,1,0:T(8,128)(2,1)S(1)} %get-tuple-element.39.refs_3_.do_ref.refs_4_, ...), custom_call_target="tpu_custom_call" | custom-call | flops 1024 | bytes 196608 | tf_op jit(solution)/shard_map/stats/pallas_call | solution.py:197
  53.9 1.0 collective-permute-done.4.refs_5_.refs_6_
  54.9 2.1 %collective-permute-start.6 = (bf16[256,512]{1,0:T(8,128)(2,1)S(1)}, bf16[256,512]{1,0:T(8,128)(2,1)S(1)}, u32[]{:S(2)}, u32[]{:S(2)}) collective-permute-start(bf16[256,512]{1,0:T(8,128)(2,1)S(1)} %collective-permute-done.4.refs_5_.refs_6_), channel_id=1, source_target_pairs={{0,8},{8,16},{16,24},{24,32},{32,40},{40,48},{48,56},{56,64},{64,7... | collective-permute-start | bytes 786440 | tf_op jit(solution)/shard_map/ppermute | solution.py:39
  56.9 5.7 %collective-permute-done.7.refs_4_.refs_5_ = bf16[256,512]{1,0:T(8,128)(2,1)S(1)} collective-permute-done((bf16[256,512]{1,0:T(8,128)(2,1)S(1)}, bf16[256,512]{1,0:T(8,128)(2,1)S(1)}, u32[]{:S(2)}, u32[]{:S(2)}) %collective-permute-start.7) | collective-permute-done | bytes 262176 | tf_op jit(solution)/shard_map/ppermute | solution.py:39
  62.6 2.2 %stats.5.state = f32[2,3,8,1024]{3,2,1,0:T(8,128)S(1)} custom-call(s32[4,14]{1,0:T(4,128)S(1)} %fusion.1.refs_0_.hit_ref.refs_1_, s32[1,512]{1,0:T(1,128)S(1)} %bitcast.18, bf16[2,1024,128]{2,1,0:T(8,128)(2,1)S(1)} %get-tuple-element.38.refs_2_.q_ref.refs_3_, bf16[2,1024,128]{2,1,0:T(8,128)(2,1)S(1)} %get-tuple-element.39.refs_3_.do_ref.refs_4_, ...), custom_call_target="tpu_custom_call" | custom-call | flops 1024 | bytes 196608 | tf_op jit(solution)/shard_map/stats/pallas_call | solution.py:197
  64.8 0.8 collective-permute-done.6.piece
  65.6 1.7 %finish.1 = (f32[2,8,1024]{2,1,0:T(8,128)S(1)}, bf16[256,512]{1,0:T(8,128)(2,1)S(1)}, f32[2,128,1024]{2,1,0:T(8,128)S(1)}) custom-call(s32[4,14]{1,0:T(4,128)S(1)} %fusion.1.refs_0_.hit_ref.refs_1_, s32[1,512]{1,0:T(1,128)S(1)} %bitcast.19, bf16[2,1024,128]{2,1,0:T(8,128)(2,1)S(1)} %get-tuple-element.38.refs_2_.q_ref.refs_3_, ...), custom_call_target="tpu_custom_call" | custom-call | flops 1024 | bytes 1376256 | tf_op jit(solution)/shard_map/finish/pallas_call | solution.py:313
  67.4 2.5 %collective-permute-start.8 = (bf16[256,512]{1,0:T(8,128)(2,1)S(1)}, bf16[256,512]{1,0:T(8,128)(2,1)S(1)}, u32[]{:S(2)}, u32[]{:S(2)}) collective-permute-start(bf16[256,512]{1,0:T(8,128)(2,1)S(1)} %get-tuple-element.50), channel_id=1, source_target_pairs={{8,0},{16,8},{24,16},{32,24},{40,32},{48,40},{56,48},{64,56},{72,6... | collective-permute-start | bytes 786440 | tf_op jit(solution)/shard_map/ppermute | solution.py:39
  69.9 3.3 %grads.4 = (bf16[256,512]{1,0:T(8,128)(2,1)S(1)}, f32[256,512]{1,0:T(8,128)S(1)}, f32[2,128,1024]{2,1,0:T(8,128)S(1)}) custom-call(s32[4,14]{1,0:T(4,128)S(1)} %fusion.1.refs_0_.hit_ref.refs_1_, s32[1,512]{1,0:T(1,128)S(1)} %bitcast.20, bf16[2,1024,128]{2,1,0:T(8,128)(2,1)S(1)} %get-tuple-element.38.refs_2_.q_ref.refs_3_, ...), custom_call_target="tpu_custom_call", output_to_operand_aliasing={{2}: (7, {})} | custom-call | flops 1024 | bytes 1 | tf_op jit(solution)/shard_map/grads/pallas_call | solution.py:295
  73.2 2.9 %collective-permute-start.9 = (bf16[256,512]{1,0:T(8,128)(2,1)S(1)}, bf16[256,512]{1,0:T(8,128)(2,1)S(1)}, u32[]{:S(2)}, u32[]{:S(2)}) collective-permute-start(bf16[256,512]{1,0:T(8,128)(2,1)S(1)} %get-tuple-element.52), channel_id=1, source_target_pairs={{8,0},{16,8},{24,16},{32,24},{40,32},{48,40},{56,48},{64,56},{72,6... | collective-permute-start | bytes 786440 | tf_op jit(solution)/shard_map/ppermute | solution.py:39
  76.1 3.0 %grads.5 = (f32[512,512]{1,0:T(8,128)S(1)}, f32[2,128,1024]{2,1,0:T(8,128)S(1)}) custom-call(s32[4,14]{1,0:T(4,128)S(1)} %fusion.1.refs_0_.hit_ref.refs_1_, s32[1,512]{1,0:T(1,128)S(1)} %bitcast.21, bf16[2,1024,128]{2,1,0:T(8,128)(2,1)S(1)} %get-tuple-element.38.refs_2_.q_ref.refs_3_, ...), custom_call_target="tpu_custom_call", output_to_operand_aliasing={{1}: (7, {})} | custom-call | flops 1024 | bytes 1 | tf_op jit(solution)/shard_map/grads/pallas_call | solution.py:295
  79.3 2.9 %collective-permute-start.10 = (bf16[256,512]{1,0:T(8,128)(2,1)S(1)}, bf16[256,512]{1,0:T(8,128)(2,1)S(1)}, u32[]{:S(2)}, u32[]{:S(2)}) collective-permute-start(bf16[256,512]{1,0:T(8,128)(2,1)S(1)} %add_convert_fusion.6), channel_id=1, source_target_pairs={{8,0},{16,8},{24,16},{32,24},{40,32},{48,40},{56,48},{64,56},{72,6... | collective-permute-start | bytes 786440 | tf_op jit(solution)/shard_map/ppermute | solution.py:39
  82.2 3.4 %grads.6 = (f32[256,512]{1,0:T(8,128)S(1)}, f32[256,512]{1,0:T(8,128)S(1)}, f32[2,128,1024]{2,1,0:T(8,128)S(1)}) custom-call(s32[4,14]{1,0:T(4,128)S(1)} %fusion.1.refs_0_.hit_ref.refs_1_, s32[1,512]{1,0:T(1,128)S(1)} %bitcast.22, bf16[2,1024,128]{2,1,0:T(8,128)(2,1)S(1)} %get-tuple-element.38.refs_2_.q_ref.refs_3_, ...), custom_call_target="tpu_custom_call", output_to_operand_aliasing={{2}: (7, {})} | custom-call | flops 1024 | bytes 2097152 | tf_op jit(solution)/shard_map/grads/pallas_call | solution.py:295
  85.7 5.0 %collective-permute-start.14 = (bf16[256,512]{1,0:T(8,128)(2,1)S(1)}, bf16[256,512]{1,0:T(8,128)(2,1)S(1)}, u32[]{:S(2)}, u32[]{:S(2)}) collective-permute-start(bf16[256,512]{1,0:T(8,128)(2,1)S(1)} %add_convert_fusion.3), channel_id=1, source_target_pairs={{8,0},{16,8},{24,16},{32,24},{40,32},{48,40},{56,48},{64,56},{72,6... | collective-permute-start | bytes 786440 | tf_op jit(solution)/shard_map/ppermute | solution.py:39
  90.8 3.2 %collective-permute-start.12 = (bf16[256,512]{1,0:T(8,128)(2,1)S(1)}, bf16[256,512]{1,0:T(8,128)(2,1)S(1)}, u32[]{:S(2)}, u32[]{:S(2)}) collective-permute-start(bf16[256,512]{1,0:T(8,128)(2,1)S(1)} %add_convert_fusion.5), channel_id=1, source_target_pairs={{8,0},{16,8},{24,16},{32,24},{40,32},{48,40},{56,48},{64,56},{72,6... | collective-permute-start | bytes 786440 | tf_op jit(solution)/shard_map/ppermute | solution.py:39
  94.0 3.5 %grads.7 = (f32[256,512]{1,0:T(8,128)S(1)}, f32[256,512]{1,0:T(8,128)S(1)}, f32[256,512]{1,0:T(8,128)S(1)}, bf16[256,512]{1,0:T(8,128)(2,1)S(1)}) custom-call(s32[1]{0:T(128)} %bitcast.low_ref.refs_0_, s32[4,14]{1,0:T(4,128)S(1)} %fusion.1.refs_0_.hit_ref.refs_1_, s32[1,512]{1,0:T(1,128)S(1)} %bitcast.23, ...), custom_call_target="tpu_custom_call" | custom-call | flops 1024 | bytes 1835008 | tf_op jit(solution)/shard_map/grads/pallas_call | solution.py:295
  97.6 4.4 %collective-permute-start.15 = (bf16[256,512]{1,0:T(8,128)(2,1)S(1)}, bf16[256,512]{1,0:T(8,128)(2,1)S(1)}, u32[]{:S(2)}, u32[]{:S(2)}) collective-permute-start(bf16[256,512]{1,0:T(8,128)(2,1)S(1)} %add_convert_fusion.2), channel_id=1, source_target_pairs={{8,0},{16,8},{24,16},{32,24},{40,32},{48,40},{56,48},{64,56},{72,6... | collective-permute-start | bytes 786440 | tf_op jit(solution)/shard_map/ppermute | solution.py:39
  102.0 0.3 collective-permute-start.11
  102.4 4.1 %collective-permute-start.13 = (bf16[256,512]{1,0:T(8,128)(2,1)S(1)}, bf16[256,512]{1,0:T(8,128)(2,1)S(1)}, u32[]{:S(2)}, u32[]{:S(2)}) collective-permute-start(bf16[256,512]{1,0:T(8,128)(2,1)S(1)} %add_convert_fusion.4), channel_id=1, source_target_pairs={{8,0},{16,8},{24,16},{32,24},{40,32},{48,40},{56,48},{64,56},{72,6... | collective-permute-start | bytes 786440 | tf_op jit(solution)/shard_map/ppermute | solution.py:39
  106.6 1.0 collective-permute-done.15
  107.6 0.8 dynamic_update_slice.6
  108.5 2.2 %collective-permute-done.13 = bf16[256,512]{1,0:T(8,128)(2,1)S(1)} collective-permute-done((bf16[256,512]{1,0:T(8,128)(2,1)S(1)}, bf16[256,512]{1,0:T(8,128)(2,1)S(1)}, u32[]{:S(2)}, u32[]{:S(2)}) %collective-permute-start.13) | collective-permute-done | bytes 262176 | tf_op jit(solution)/shard_map/ppermute | solution.py:39
  110.7 0.8 fusion
  111.5 3.9 %all-to-all-start.1 = ((bf16[8,64,512]{2,1,0:T(8,128)(2,1)}), bf16[8,64,512]{2,1,0:T(8,128)(2,1)S(1)}, u32[]{:S(2)}, u32[]{:S(2)}) async-start(bf16[8,64,512]{2,1,0:T(8,128)(2,1)} %bitcast.7), calls=%async_computation.1 | async-start | bytes 1048576 | tf_op jit(solution)/shard_map/all_to_all | solution.py:375
  115.3 1.0 columns.1
  116.4 9.0 %all-to-all-done.1.in_ref = bf16[8,64,512]{2,1,0:T(8,128)(2,1)S(1)} async-done(((bf16[8,64,512]{2,1,0:T(8,128)(2,1)}), bf16[8,64,512]{2,1,0:T(8,128)(2,1)S(1)}, u32[]{:S(2)}, u32[]{:S(2)}) %all-to-all-start.1) | async-done | bytes 524320 | tf_op jit(solution)/shard_map/all_to_all | solution.py:375
  125.4 1.0 unpack.1
  (27 shorter events, 0.8 us)
Async XLA Ops:
  0.6 8.5 %copy-start = (s32[2,128,14]{1,0,2:T(2,128)S(1)}, s32[2,128,14]{1,0,2:T(2,128)}, u32[]{:S(2)}) copy-start(s32[2,128,14]{1,0,2:T(2,128)} %param.11) | copy-start | bytes 43012
  0.6 6.3 %copy-start.2 = (bf16[256,1024]{1,0:T(8,128)(2,1)S(1)}, bf16[256,1024]{1,0:T(8,128)(2,1)}, u32[]{:S(2)}) copy-start(bf16[256,1024]{1,0:T(8,128)(2,1)} %do_ref.1) | copy-start | bytes 1572868
  0.7 6.3 %copy-start.1 = (bf16[256,1024]{1,0:T(8,128)(2,1)S(1)}, bf16[256,1024]{1,0:T(8,128)(2,1)}, u32[]{:S(2)}) copy-start(bf16[256,1024]{1,0:T(8,128)(2,1)} %q_ref.1) | copy-start | bytes 1572868
  2.6 14.4 %all-to-all-start = ((bf16[8,64,512]{2,1,0:T(8,128)(2,1)}), bf16[8,64,512]{2,1,0:T(8,128)(2,1)S(1)}, u32[]{:S(2)}, u32[]{:S(2)}) async-start(bf16[8,64,512]{2,1,0:T(8,128)(2,1)} %pack.1), calls=%async_computation | async-start | bytes 1048576 | tf_op jit(solution)/shard_map/all_to_all | solution.py:337
  6.9 2.3 %copy-start.3 = (s32[16384]{0:T(1024)S(1)}, s32[16384]{0:T(1024)}, u32[]{:S(2)}) copy-start(s32[16384]{0:T(1024)} %param.10) | copy-start | bytes 196612
  7.1 27.3 %collective-permute-start = (bf16[2,256,512]{2,1,0:T(8,128)(2,1)S(1)}, bf16[2,256,512]{2,1,0:T(8,128)(2,1)S(1)}, u32[]{:S(2)}, u32[]{:S(2)}) collective-permute-start(bf16[2,256,512]{2,1,0:T(8,128)(2,1)S(1)} %pad_maximum_fusion), channel_id=1, source_target_pairs={{0,4},{4,0},{1,5},{5,1},{2,6},{6,2},{3,7},{7,3},{8,12},{12,8},{9,1... | collective-permute-start | bytes 1572872 | tf_op jit(solution)/shard_map/ppermute | solution.py:43
  17.0 15.2 %collective-permute-start.1 = (bf16[256,512]{1,0:T(8,128)(2,1)S(1)}, bf16[256,512]{1,0:T(8,128)(2,1)S(1)}, u32[]{:S(2)}, u32[]{:S(2)}) collective-permute-start(bf16[256,512]{1,0:T(8,128)(2,1)S(1)} %bitcast.13), channel_id=1, source_target_pairs={{0,8},{8,16},{16,24},{24,32},{32,40},{40,48},{48,56},{56,64},{64,7... | collective-permute-start | bytes 786440 | tf_op jit(solution)/shard_map/ppermute | solution.py:39
  21.6 15.1 %collective-permute-start.3 = (bf16[256,512]{1,0:T(8,128)(2,1)S(1)}, bf16[256,512]{1,0:T(8,128)(2,1)S(1)}, u32[]{:S(2)}, u32[]{:S(2)}) collective-permute-start(bf16[256,512]{1,0:T(8,128)(2,1)S(1)} %bitcast.10), channel_id=1, source_target_pairs={{0,8},{8,16},{16,24},{24,32},{32,40},{40,48},{48,56},{56,64},{64,7... | collective-permute-start | bytes 786440 | tf_op jit(solution)/shard_map/ppermute | solution.py:39
  32.2 11.5 %collective-permute-start.2 = (bf16[256,512]{1,0:T(8,128)(2,1)S(1)}, bf16[256,512]{1,0:T(8,128)(2,1)S(1)}, u32[]{:S(2)}, u32[]{:S(2)}) collective-permute-start(bf16[256,512]{1,0:T(8,128)(2,1)S(1)} %collective-permute-done.1.refs_7_), channel_id=1, source_target_pairs={{0,8},{8,16},{16,24},{24,32},{32,40},{40,48},{48,56},{56,64},{64,7... | collective-permute-start | bytes 786440 | tf_op jit(solution)/shard_map/ppermute | solution.py:39
  36.7 13.0 %collective-permute-start.5 = (bf16[256,512]{1,0:T(8,128)(2,1)S(1)}, bf16[256,512]{1,0:T(8,128)(2,1)S(1)}, u32[]{:S(2)}, u32[]{:S(2)}) collective-permute-start(bf16[256,512]{1,0:T(8,128)(2,1)S(1)} %collective-permute-done.3.refs_6_), channel_id=1, source_target_pairs={{0,8},{8,16},{16,24},{24,32},{32,40},{40,48},{48,56},{56,64},{64,7... | collective-permute-start | bytes 786440 | tf_op jit(solution)/shard_map/ppermute | solution.py:39
  43.7 11.2 %collective-permute-start.4 = (bf16[256,512]{1,0:T(8,128)(2,1)S(1)}, bf16[256,512]{1,0:T(8,128)(2,1)S(1)}, u32[]{:S(2)}, u32[]{:S(2)}) collective-permute-start(bf16[256,512]{1,0:T(8,128)(2,1)S(1)} %collective-permute-done.2.refs_5_.refs_6_), channel_id=1, source_target_pairs={{0,8},{8,16},{16,24},{24,32},{32,40},{40,48},{48,56},{56,64},{64,7... | collective-permute-start | bytes 786440 | tf_op jit(solution)/shard_map/ppermute | solution.py:39
  49.7 13.0 %collective-permute-start.7 = (bf16[256,512]{1,0:T(8,128)(2,1)S(1)}, bf16[256,512]{1,0:T(8,128)(2,1)S(1)}, u32[]{:S(2)}, u32[]{:S(2)}) collective-permute-start(bf16[256,512]{1,0:T(8,128)(2,1)S(1)} %collective-permute-done.5.refs_4_.refs_5_), channel_id=1, source_target_pairs={{0,8},{8,16},{16,24},{24,32},{32,40},{40,48},{48,56},{56,64},{64,7... | collective-permute-start | bytes 786440 | tf_op jit(solution)/shard_map/ppermute | solution.py:39
  54.9 10.8 %collective-permute-start.6 = (bf16[256,512]{1,0:T(8,128)(2,1)S(1)}, bf16[256,512]{1,0:T(8,128)(2,1)S(1)}, u32[]{:S(2)}, u32[]{:S(2)}) collective-permute-start(bf16[256,512]{1,0:T(8,128)(2,1)S(1)} %collective-permute-done.4.refs_5_.refs_6_), channel_id=1, source_target_pairs={{0,8},{8,16},{16,24},{24,32},{32,40},{40,48},{48,56},{56,64},{64,7... | collective-permute-start | bytes 786440 | tf_op jit(solution)/shard_map/ppermute | solution.py:39
  67.4 11.8 %collective-permute-start.8 = (bf16[256,512]{1,0:T(8,128)(2,1)S(1)}, bf16[256,512]{1,0:T(8,128)(2,1)S(1)}, u32[]{:S(2)}, u32[]{:S(2)}) collective-permute-start(bf16[256,512]{1,0:T(8,128)(2,1)S(1)} %get-tuple-element.50), channel_id=1, source_target_pairs={{8,0},{16,8},{24,16},{32,24},{40,32},{48,40},{56,48},{64,56},{72,6... | collective-permute-start | bytes 786440 | tf_op jit(solution)/shard_map/ppermute | solution.py:39
  73.2 9.0 %collective-permute-start.9 = (bf16[256,512]{1,0:T(8,128)(2,1)S(1)}, bf16[256,512]{1,0:T(8,128)(2,1)S(1)}, u32[]{:S(2)}, u32[]{:S(2)}) collective-permute-start(bf16[256,512]{1,0:T(8,128)(2,1)S(1)} %get-tuple-element.52), channel_id=1, source_target_pairs={{8,0},{16,8},{24,16},{32,24},{40,32},{48,40},{56,48},{64,56},{72,6... | collective-permute-start | bytes 786440 | tf_op jit(solution)/shard_map/ppermute | solution.py:39
  79.3 11.4 %collective-permute-start.10 = (bf16[256,512]{1,0:T(8,128)(2,1)S(1)}, bf16[256,512]{1,0:T(8,128)(2,1)S(1)}, u32[]{:S(2)}, u32[]{:S(2)}) collective-permute-start(bf16[256,512]{1,0:T(8,128)(2,1)S(1)} %add_convert_fusion.6), channel_id=1, source_target_pairs={{8,0},{16,8},{24,16},{32,24},{40,32},{48,40},{56,48},{64,56},{72,6... | collective-permute-start | bytes 786440 | tf_op jit(solution)/shard_map/ppermute | solution.py:39
  85.7 11.8 %collective-permute-start.14 = (bf16[256,512]{1,0:T(8,128)(2,1)S(1)}, bf16[256,512]{1,0:T(8,128)(2,1)S(1)}, u32[]{:S(2)}, u32[]{:S(2)}) collective-permute-start(bf16[256,512]{1,0:T(8,128)(2,1)S(1)} %add_convert_fusion.3), channel_id=1, source_target_pairs={{8,0},{16,8},{24,16},{32,24},{40,32},{48,40},{56,48},{64,56},{72,6... | collective-permute-start | bytes 786440 | tf_op jit(solution)/shard_map/ppermute | solution.py:39
  90.8 11.6 %collective-permute-start.12 = (bf16[256,512]{1,0:T(8,128)(2,1)S(1)}, bf16[256,512]{1,0:T(8,128)(2,1)S(1)}, u32[]{:S(2)}, u32[]{:S(2)}) collective-permute-start(bf16[256,512]{1,0:T(8,128)(2,1)S(1)} %add_convert_fusion.5), channel_id=1, source_target_pairs={{8,0},{16,8},{24,16},{32,24},{40,32},{48,40},{56,48},{64,56},{72,6... | collective-permute-start | bytes 786440 | tf_op jit(solution)/shard_map/ppermute | solution.py:39
  97.6 9.9 %collective-permute-start.15 = (bf16[256,512]{1,0:T(8,128)(2,1)S(1)}, bf16[256,512]{1,0:T(8,128)(2,1)S(1)}, u32[]{:S(2)}, u32[]{:S(2)}) collective-permute-start(bf16[256,512]{1,0:T(8,128)(2,1)S(1)} %add_convert_fusion.2), channel_id=1, source_target_pairs={{8,0},{16,8},{24,16},{32,24},{40,32},{48,40},{56,48},{64,56},{72,6... | collective-permute-start | bytes 786440 | tf_op jit(solution)/shard_map/ppermute | solution.py:39
  102.0 6.5 %collective-permute-start.11 = (bf16[256,512]{1,0:T(8,128)(2,1)S(1)}, bf16[256,512]{1,0:T(8,128)(2,1)S(1)}, u32[]{:S(2)}, u32[]{:S(2)}) collective-permute-start(bf16[256,512]{1,0:T(8,128)(2,1)S(1)} %get-tuple-element.59), channel_id=1, source_target_pairs={{0,4},{4,0},{1,5},{5,1},{2,6},{6,2},{3,7},{7,3},{8,12},{12,8},{9,1... | collective-permute-start | bytes 786440 | tf_op jit(solution)/shard_map/ppermute | solution.py:43
  102.4 8.3 %collective-permute-start.13 = (bf16[256,512]{1,0:T(8,128)(2,1)S(1)}, bf16[256,512]{1,0:T(8,128)(2,1)S(1)}, u32[]{:S(2)}, u32[]{:S(2)}) collective-permute-start(bf16[256,512]{1,0:T(8,128)(2,1)S(1)} %add_convert_fusion.4), channel_id=1, source_target_pairs={{8,0},{16,8},{24,16},{32,24},{40,32},{48,40},{56,48},{64,56},{72,6... | collective-permute-start | bytes 786440 | tf_op jit(solution)/shard_map/ppermute | solution.py:39
  111.5 13.9 %all-to-all-start.1 = ((bf16[8,64,512]{2,1,0:T(8,128)(2,1)}), bf16[8,64,512]{2,1,0:T(8,128)(2,1)S(1)}, u32[]{:S(2)}, u32[]{:S(2)}) async-start(bf16[8,64,512]{2,1,0:T(8,128)(2,1)} %bitcast.7), calls=%async_computation.1 | async-start | bytes 1048576 | tf_op jit(solution)/shard_map/all_to_all | solution.py:375

commit v5 on v4

--- a/solution.py
+++ b/solution.py
@@ -235,7 +235,7 @@
             for m, (ref, first) in enumerate(zip(pieces, first_blocks)):
                 seen = [w for w in (first, first + 1) if visible(i, w)]
                 for w in (first, first + 1):
-                    if w not in seen:
+                    if w not in seen and not joined:
                         at = slice(m * span + (w - first) * BLOCK, m * span + (w - first + 1) * BLOCK)
                         p_scr[h, at, lanes] = jnp.zeros((BLOCK, PAIR), jnp.bfloat16)
                         ds_scr[h, at, lanes] = jnp.zeros((BLOCK, PAIR), jnp.bfloat16)
@@ -255,10 +255,21 @@
         keys = [ref[:, kcols] for ref in pieces]
         keys = keys[0] if count == 1 else jnp.concatenate(keys, axis=0)
         used = slice(0, rows_used)
-        ds = ds_scr[h, :, used]
-        dv = dot(p_scr[h, :, used], do_ref[h, used, :], 1, 0)
-        dk = dot(ds, q_ref[h, used, :], 1, 0)
-        dqt = dot(keys, ds, 0, 0)
+        if joined:
+            dv, dk, dqt = [], [], []
+            for r in range(Q_BLOCKS):
+                rows, later = slice(r * BLOCK, (r + 1) * BLOCK), slice(r * PAIR, ROWS)
+                dv.append(dot(p_scr[h, rows, later], do_ref[h, later, :], 1, 0))
+                dk.append(dot(ds_scr[h, rows, later], q_ref[h, later, :], 1, 0))
+                earlier, lanes = slice(0, (r + 1) * BLOCK), slice(r * PAIR, (r + 1) * PAIR)
+                dqt.append(dot(keys[earlier], ds_scr[h, earlier, lanes], 0, 0))
+            dv, dk = jnp.concatenate(dv, axis=0), jnp.concatenate(dk, axis=0)
+            dqt = jnp.concatenate(dqt, axis=1)
+        else:
+            ds = ds_scr[h, :, used]
+            dv = dot(p_scr[h, :, used], do_ref[h, used, :], 1, 0)
+            dk = dot(ds, q_ref[h, used, :], 1, 0)
+            dqt = dot(keys, ds, 0, 0)
         if not opening:
             dqt = dqt + dqt_in[h]
         for m, out in enumerate(out_refs):
@@ -332,6 +343,7 @@
         out_specs=VMEM_SPEC,
         scratch_shapes=[pltpu.VMEM((SPAN // 4, KEY_VALUE_HEADS * HEAD_SIZE), jnp.bfloat16)] * 2
         + [pltpu.SemaphoreType.DMA((2,))],
+        cost_estimate=pl.CostEstimate(flops=1024, bytes_accessed=1 << 25, transcendentals=0),
         name="pack",
     )(key_states, value_inputs)
     own = lax.all_to_all(kv, MEMBER_AXES, 0, 0, tiled=True)
@@ -380,15 +392,19 @@
     def summed(part, arrived):
         return (part + arrived.astype(full)).astype(low16)
 
+    def after(arrived, value):
+        return lax.optimization_barrier((arrived, value))[1]
+
     rb = slab_shift(gb4, -1)
     ga3, gb3, dqt = grads((2, 4), tables, norm, (a3, b3), dqt, (low16, full), light=True)
     ra = slab_shift(ga3, -1)
-    g0, dqt = grads((14, 16), tables, norm, (a0, b0), dqt, (full,), light=True)
+    ga2, gb2, dqt = grads((6, 8), tables, norm, (a2, b2), dqt, (full, full), light=True)
     dqt, rb = lax.optimization_barrier((dqt, rb))
     rb = slab_shift(summed(gb3, rb), -1)
-    dqt, ra = lax.optimization_barrier((dqt, ra))
-    ga2, gb2, dqt = grads((6, 8), tables, norm, (a2, b2), dqt, (full, full))
-    ra = slab_shift(summed(ga2, ra), -1)
+    ra = summed(ga2, ra)
+    dqt = after(ra, dqt)
+    ra = slab_shift(ra, -1)
+    g0, dqt = grads((14, 16), tables, norm, (a0, b0), dqt, (full,), light=True)
     dqt, rb = lax.optimization_barrier((dqt, rb))
     rb = slab_shift(summed(gb2, rb), -1)
     ga1, gb1, mine, send = grads((10, 12), tables, norm, (a1, b1), dqt, (full, full), low_ref)

time: 127 us -> 127 us (level)
  transfers between devices with their start and end apart: 18 -> 18, of which waited for: 11 -> 10; matrix products, arithmetic and copies ran while one was open for 2% -> 3% of each run, Pallas kernels for 18% -> 17%
where the time goes in v5:
time: 127 us; the launch traced here: 126 us
  starting transfers between devices  53.6 us (42%)
  waiting for transfers between devices  41.1 us (32%)
  Pallas kernels  26.5 us (21%)
  other arithmetic  2.81 us (2%)
  local copies, waits for them, and re-layouts  1.37 us (1%)
    ppermute x14, starting transfers between devices, slab_shift(): lax.ppermute(x, SLAB_AXES, [(i, i + by) for i in range(count) if 0 <= i +...  43.5 us
    ppermute x14, waiting for transfers between devices, slab_shift(): lax.ppermute(x, SLAB_AXES, [(i, i + by) for i in range(count) if 0 <= i +...  25.3 us
    pallas_call x4, Pallas kernels, grads(): call(functools.partial(grads_kernel, first_blocks, opening, closing), 'gr...  12.8 us
    all_to_all x1, waiting for transfers between devices, to_owners(): lax.all_to_all(x.reshape(8, SPAN // 4, 2 * WIDTH), MEMBER_AXES, 0, 0, til...  8.94 us
    pallas_call x3, Pallas kernels, stats(): call(functools.partial(stats_kernel, first_blocks, opening, closing), 'st...  7.75 us
    all_to_all x1, waiting for transfers between devices, per_device(): own = lax.all_to_all(kv, MEMBER_AXES, 0, 0, tiled=True)  6.94 us
    all_to_all x1, starting transfers between devices, per_device(): own = lax.all_to_all(kv, MEMBER_AXES, 0, 0, tiled=True)  4.31 us
    all_to_all x1, starting transfers between devices, to_owners(): lax.all_to_all(x.reshape(8, SPAN // 4, 2 * WIDTH), MEMBER_AXES, 0, 0, til...  3.49 us
  transfers between devices with their start and end apart: 18, of which 10 were waited for; matrix products, arithmetic and copies ran while one was open for 3% of the time, Pallas kernels for 17%

profile of v5, /device:TPU:24, one launch (start us, length us, event | category | flops | bytes accessed | tf_op | source)
XLA Modules:
  0.0 126.4 jit_solution(18393396509038720594)
XLA Ops:
  0.7 1.9 %pack.1 = bf16[8,64,512]{2,1,0:T(8,128)(2,1)} custom-call(bf16[64,2048]{1,0:T(8,128)(2,1)} %k_ref.1, bf16[64,2048]{1,0:T(8,128)(2,1)} %v_ref.1), custom_call_target="tpu_custom_call" | custom-call | flops 1024 | bytes 33554432 | tf_op jit(solution)/shard_map/pack/pallas_call | solution.py:339
  2.6 4.3 %all-to-all-start = ((bf16[8,64,512]{2,1,0:T(8,128)(2,1)}), bf16[8,64,512]{2,1,0:T(8,128)(2,1)S(1)}, u32[]{:S(2)}, u32[]{:S(2)}) async-start(bf16[8,64,512]{2,1,0:T(8,128)(2,1)} %pack.1), calls=%async_computation | async-start | bytes 1048576 | tf_op jit(solution)/shard_map/all_to_all | solution.py:349
  7.0 0.8 pad_maximum_fusion
  7.9 2.0 %collective-permute-start = (bf16[2,256,512]{2,1,0:T(8,128)(2,1)}, bf16[2,256,512]{2,1,0:T(8,128)(2,1)S(1)}, u32[]{:S(2)}, u32[]{:S(2)}) collective-permute-start(bf16[2,256,512]{2,1,0:T(8,128)(2,1)} %pad_maximum_fusion), channel_id=1, source_target_pairs={{0,4},{4,0},{1,5},{5,1},{2,6},{6,2},{3,7},{7,3},{8,12},{12,8},{9,1... | collective-permute-start | bytes 1572872 | tf_op jit(solution)/shard_map/ppermute | solution.py:43
  10.0 0.1 pad_dynamic-slice_fusion.1
  10.0 6.9 %all-to-all-done = bf16[8,64,512]{2,1,0:T(8,128)(2,1)S(1)} async-done(((bf16[8,64,512]{2,1,0:T(8,128)(2,1)}), bf16[8,64,512]{2,1,0:T(8,128)(2,1)S(1)}, u32[]{:S(2)}, u32[]{:S(2)}) %all-to-all-start) | async-done | bytes 524320 | tf_op jit(solution)/shard_map/all_to_all | solution.py:349
  17.0 3.8 %collective-permute-start.1 = (bf16[256,512]{1,0:T(8,128)(2,1)S(1)}, bf16[256,512]{1,0:T(8,128)(2,1)S(1)}, u32[]{:S(2)}, u32[]{:S(2)}) collective-permute-start(bf16[256,512]{1,0:T(8,128)(2,1)S(1)} %bitcast.13), channel_id=1, source_target_pairs={{0,8},{8,16},{16,24},{24,32},{32,40},{40,48},{48,56},{56,64},{64,7... | collective-permute-start | bytes 786440 | tf_op jit(solution)/shard_map/ppermute | solution.py:39
  20.9 0.1 pad_dynamic-slice_fusion
  20.9 0.7 convert_reduce_fusion
  21.6 3.8 %collective-permute-start.3 = (bf16[256,512]{1,0:T(8,128)(2,1)S(1)}, bf16[256,512]{1,0:T(8,128)(2,1)S(1)}, u32[]{:S(2)}, u32[]{:S(2)}) collective-permute-start(bf16[256,512]{1,0:T(8,128)(2,1)S(1)} %bitcast.10), channel_id=1, source_target_pairs={{0,8},{8,16},{16,24},{24,32},{32,40},{40,48},{48,56},{56,64},{64,7... | collective-permute-start | bytes 786440 | tf_op jit(solution)/shard_map/ppermute | solution.py:39
  25.4 6.8 %collective-permute-done.1.refs_7_ = bf16[256,512]{1,0:T(8,128)(2,1)S(1)} collective-permute-done((bf16[256,512]{1,0:T(8,128)(2,1)S(1)}, bf16[256,512]{1,0:T(8,128)(2,1)S(1)}, u32[]{:S(2)}, u32[]{:S(2)}) %collective-permute-start.1) | collective-permute-done | bytes 262176 | tf_op jit(solution)/shard_map/ppermute | solution.py:39
  32.2 1.9 %collective-permute-start.2 = (bf16[256,512]{1,0:T(8,128)(2,1)S(1)}, bf16[256,512]{1,0:T(8,128)(2,1)S(1)}, u32[]{:S(2)}, u32[]{:S(2)}) collective-permute-start(bf16[256,512]{1,0:T(8,128)(2,1)S(1)} %collective-permute-done.1.refs_7_), channel_id=1, source_target_pairs={{0,8},{8,16},{16,24},{24,32},{32,40},{40,48},{48,56},{56,64},{64,7... | collective-permute-start | bytes 786440 | tf_op jit(solution)/shard_map/ppermute | solution.py:39
  34.1 0.1 copy.13
  34.2 0.1 rev.3
  34.4 0.2 rows.1
  34.6 2.1 %collective-permute-done.3.refs_6_ = bf16[256,512]{1,0:T(8,128)(2,1)S(1)} collective-permute-done((bf16[256,512]{1,0:T(8,128)(2,1)S(1)}, bf16[256,512]{1,0:T(8,128)(2,1)S(1)}, u32[]{:S(2)}, u32[]{:S(2)}) %collective-permute-start.3) | collective-permute-done | bytes 262176 | tf_op jit(solution)/shard_map/ppermute | solution.py:39
  36.7 1.9 %collective-permute-start.5 = (bf16[256,512]{1,0:T(8,128)(2,1)S(1)}, bf16[256,512]{1,0:T(8,128)(2,1)S(1)}, u32[]{:S(2)}, u32[]{:S(2)}) collective-permute-start(bf16[256,512]{1,0:T(8,128)(2,1)S(1)} %collective-permute-done.3.refs_6_), channel_id=1, source_target_pairs={{0,8},{8,16},{16,24},{24,32},{32,40},{40,48},{48,56},{56,64},{64,7... | collective-permute-start | bytes 786440 | tf_op jit(solution)/shard_map/ppermute | solution.py:39
  38.6 3.3 %stats.3.refs_6_ = f32[2,3,8,1024]{3,2,1,0:T(8,128)S(1)} custom-call(s32[4,14]{1,0:T(4,128)S(1)} %fusion.1.refs_0_.hit_ref.refs_1_, s32[1,512]{1,0:T(1,128)S(1)} %bitcast.16, bf16[2,1024,128]{2,1,0:T(8,128)(2,1)S(1)} %get-tuple-element.37.refs_2_.q_ref.refs_3_, bf16[2,1024,128]{2,1,0:T(8,128)(2,1)S(1)} %get-tuple-element.38.refs_3_.do_ref.refs_4_, ...), custom_call_target="tpu_custom_call" | custom-call | flops 1024 | bytes 196608 | tf_op jit(solution)/shard_map/stats/pallas_call | solution.py:197
  41.9 1.8 %collective-permute-done.2.refs_5_.refs_6_ = bf16[256,512]{1,0:T(8,128)(2,1)S(1)} collective-permute-done((bf16[256,512]{1,0:T(8,128)(2,1)S(1)}, bf16[256,512]{1,0:T(8,128)(2,1)S(1)}, u32[]{:S(2)}, u32[]{:S(2)}) %collective-permute-start.2) | collective-permute-done | bytes 262176 | tf_op jit(solution)/shard_map/ppermute | solution.py:39
  43.7 1.9 %collective-permute-start.4 = (bf16[256,512]{1,0:T(8,128)(2,1)S(1)}, bf16[256,512]{1,0:T(8,128)(2,1)S(1)}, u32[]{:S(2)}, u32[]{:S(2)}) collective-permute-start(bf16[256,512]{1,0:T(8,128)(2,1)S(1)} %collective-permute-done.2.refs_5_.refs_6_), channel_id=1, source_target_pairs={{0,8},{8,16},{16,24},{24,32},{32,40},{40,48},{48,56},{56,64},{64,7... | collective-permute-start | bytes 786440 | tf_op jit(solution)/shard_map/ppermute | solution.py:39
  45.6 4.1 %collective-permute-done.5.refs_4_.refs_5_ = bf16[256,512]{1,0:T(8,128)(2,1)S(1)} collective-permute-done((bf16[256,512]{1,0:T(8,128)(2,1)S(1)}, bf16[256,512]{1,0:T(8,128)(2,1)S(1)}, u32[]{:S(2)}, u32[]{:S(2)}) %collective-permute-start.5) | collective-permute-done | bytes 262176 | tf_op jit(solution)/shard_map/ppermute | solution.py:39
  49.7 1.9 %collective-permute-start.7 = (bf16[256,512]{1,0:T(8,128)(2,1)S(1)}, bf16[256,512]{1,0:T(8,128)(2,1)S(1)}, u32[]{:S(2)}, u32[]{:S(2)}) collective-permute-start(bf16[256,512]{1,0:T(8,128)(2,1)S(1)} %collective-permute-done.5.refs_4_.refs_5_), channel_id=1, source_target_pairs={{0,8},{8,16},{16,24},{24,32},{32,40},{40,48},{48,56},{56,64},{64,7... | collective-permute-start | bytes 786440 | tf_op jit(solution)/shard_map/ppermute | solution.py:39
  51.6 2.3 %stats.4.refs_6_ = f32[2,3,8,1024]{3,2,1,0:T(8,128)S(1)} custom-call(s32[4,14]{1,0:T(4,128)S(1)} %fusion.1.refs_0_.hit_ref.refs_1_, s32[1,512]{1,0:T(1,128)S(1)} %bitcast.17, bf16[2,1024,128]{2,1,0:T(8,128)(2,1)S(1)} %get-tuple-element.37.refs_2_.q_ref.refs_3_, bf16[2,1024,128]{2,1,0:T(8,128)(2,1)S(1)} %get-tuple-element.38.refs_3_.do_ref.refs_4_, ...), custom_call_target="tpu_custom_call" | custom-call | flops 1024 | bytes 196608 | tf_op jit(solution)/shard_map/stats/pallas_call | solution.py:197
  53.9 1.0 collective-permute-done.4.refs_5_.refs_6_
  54.9 2.0 %collective-permute-start.6 = (bf16[256,512]{1,0:T(8,128)(2,1)S(1)}, bf16[256,512]{1,0:T(8,128)(2,1)S(1)}, u32[]{:S(2)}, u32[]{:S(2)}) collective-permute-start(bf16[256,512]{1,0:T(8,128)(2,1)S(1)} %collective-permute-done.4.refs_5_.refs_6_), channel_id=1, source_target_pairs={{0,8},{8,16},{16,24},{24,32},{32,40},{40,48},{48,56},{56,64},{64,7... | collective-permute-start | bytes 786440 | tf_op jit(solution)/shard_map/ppermute | solution.py:39
  56.9 5.8 %collective-permute-done.7.refs_4_.refs_5_ = bf16[256,512]{1,0:T(8,128)(2,1)S(1)} collective-permute-done((bf16[256,512]{1,0:T(8,128)(2,1)S(1)}, bf16[256,512]{1,0:T(8,128)(2,1)S(1)}, u32[]{:S(2)}, u32[]{:S(2)}) %collective-permute-start.7) | collective-permute-done | bytes 262176 | tf_op jit(solution)/shard_map/ppermute | solution.py:39
  62.7 2.2 %stats.5.state = f32[2,3,8,1024]{3,2,1,0:T(8,128)S(1)} custom-call(s32[4,14]{1,0:T(4,128)S(1)} %fusion.1.refs_0_.hit_ref.refs_1_, s32[1,512]{1,0:T(1,128)S(1)} %bitcast.18, bf16[2,1024,128]{2,1,0:T(8,128)(2,1)S(1)} %get-tuple-element.37.refs_2_.q_ref.refs_3_, bf16[2,1024,128]{2,1,0:T(8,128)(2,1)S(1)} %get-tuple-element.38.refs_3_.do_ref.refs_4_, ...), custom_call_target="tpu_custom_call" | custom-call | flops 1024 | bytes 196608 | tf_op jit(solution)/shard_map/stats/pallas_call | solution.py:197
  64.9 0.8 collective-permute-done.6.piece
  65.7 1.7 %finish.1 = (f32[2,8,1024]{2,1,0:T(8,128)S(1)}, bf16[256,512]{1,0:T(8,128)(2,1)S(1)}, f32[2,128,1024]{2,1,0:T(8,128)S(1)}) custom-call(s32[4,14]{1,0:T(4,128)S(1)} %fusion.1.refs_0_.hit_ref.refs_1_, s32[1,512]{1,0:T(1,128)S(1)} %bitcast.19, bf16[2,1024,128]{2,1,0:T(8,128)(2,1)S(1)} %get-tuple-element.37.refs_2_.q_ref.refs_3_, ...), custom_call_target="tpu_custom_call" | custom-call | flops 1024 | bytes 1376256 | tf_op jit(solution)/shard_map/finish/pallas_call | solution.py:324
  67.4 2.5 %collective-permute-start.9 = (bf16[256,512]{1,0:T(8,128)(2,1)S(1)}, bf16[256,512]{1,0:T(8,128)(2,1)S(1)}, u32[]{:S(2)}, u32[]{:S(2)}) collective-permute-start(bf16[256,512]{1,0:T(8,128)(2,1)S(1)} %get-tuple-element.51), channel_id=1, source_target_pairs={{8,0},{16,8},{24,16},{32,24},{40,32},{48,40},{56,48},{64,56},{72,6... | collective-permute-start | bytes 786440 | tf_op jit(solution)/shard_map/ppermute | solution.py:39
  69.9 3.3 %grads.4 = (bf16[256,512]{1,0:T(8,128)(2,1)S(1)}, f32[256,512]{1,0:T(8,128)S(1)}, f32[2,128,1024]{2,1,0:T(8,128)S(1)}) custom-call(s32[4,14]{1,0:T(4,128)S(1)} %fusion.1.refs_0_.hit_ref.refs_1_, s32[1,512]{1,0:T(1,128)S(1)} %bitcast.20, bf16[2,1024,128]{2,1,0:T(8,128)(2,1)S(1)} %get-tuple-element.37.refs_2_.q_ref.refs_3_, ...), custom_call_target="tpu_custom_call", output_to_operand_aliasing={{2}: (7, {})} | custom-call | flops 1024 | bytes 1 | tf_op jit(solution)/shard_map/grads/pallas_call | solution.py:306
  73.3 2.9 %collective-permute-start.8 = (bf16[256,512]{1,0:T(8,128)(2,1)S(1)}, bf16[256,512]{1,0:T(8,128)(2,1)S(1)}, u32[]{:S(2)}, u32[]{:S(2)}) collective-permute-start(bf16[256,512]{1,0:T(8,128)(2,1)S(1)} %get-tuple-element.49), channel_id=1, source_target_pairs={{8,0},{16,8},{24,16},{32,24},{40,32},{48,40},{56,48},{64,56},{72,6... | collective-permute-start | bytes 786440 | tf_op jit(solution)/shard_map/ppermute | solution.py:39
  76.1 3.4 %grads.5 = (f32[256,512]{1,0:T(8,128)S(1)}, f32[256,512]{1,0:T(8,128)S(1)}, f32[2,128,1024]{2,1,0:T(8,128)S(1)}) custom-call(s32[4,14]{1,0:T(4,128)S(1)} %fusion.1.refs_0_.hit_ref.refs_1_, s32[1,512]{1,0:T(1,128)S(1)} %bitcast.21, bf16[2,1024,128]{2,1,0:T(8,128)(2,1)S(1)} %get-tuple-element.37.refs_2_.q_ref.refs_3_, ...), custom_call_target="tpu_custom_call", output_to_operand_aliasing={{2}: (7, {})} | custom-call | flops 1024 | bytes 1 | tf_op jit(solution)/shard_map/grads/pallas_call | solution.py:306
  79.6 2.9 %collective-permute-start.10 = (bf16[256,512]{1,0:T(8,128)(2,1)S(1)}, bf16[256,512]{1,0:T(8,128)(2,1)S(1)}, u32[]{:S(2)}, u32[]{:S(2)}) collective-permute-start(bf16[256,512]{1,0:T(8,128)(2,1)S(1)} %add_convert_fusion.5), channel_id=1, source_target_pairs={{8,0},{16,8},{24,16},{32,24},{40,32},{48,40},{56,48},{64,56},{72,6... | collective-permute-start | bytes 786440 | tf_op jit(solution)/shard_map/ppermute | solution.py:39
  82.7 5.0 %collective-permute-start.14 = (bf16[256,512]{1,0:T(8,128)(2,1)S(1)}, bf16[256,512]{1,0:T(8,128)(2,1)S(1)}, u32[]{:S(2)}, u32[]{:S(2)}) collective-permute-start(bf16[256,512]{1,0:T(8,128)(2,1)S(1)} %add_convert_fusion.6), channel_id=1, source_target_pairs={{8,0},{16,8},{24,16},{32,24},{40,32},{48,40},{56,48},{64,56},{72,6... | collective-permute-start | bytes 786440 | tf_op jit(solution)/shard_map/ppermute | solution.py:39
  87.6 2.6 %grads.6 = (f32[512,512]{1,0:T(8,128)S(1)}, f32[2,128,1024]{2,1,0:T(8,128)S(1)}) custom-call(s32[4,14]{1,0:T(4,128)S(1)} %fusion.1.refs_0_.hit_ref.refs_1_, s32[1,512]{1,0:T(1,128)S(1)} %bitcast.22, bf16[2,1024,128]{2,1,0:T(8,128)(2,1)S(1)} %get-tuple-element.37.refs_2_.q_ref.refs_3_, ...), custom_call_target="tpu_custom_call", output_to_operand_aliasing={{1}: (7, {})} | custom-call | flops 1024 | bytes 1 | tf_op jit(solution)/shard_map/grads/pallas_call | solution.py:306
  90.3 5.0 %collective-permute-start.12 = (bf16[256,512]{1,0:T(8,128)(2,1)S(1)}, bf16[256,512]{1,0:T(8,128)(2,1)S(1)}, u32[]{:S(2)}, u32[]{:S(2)}) collective-permute-start(bf16[256,512]{1,0:T(8,128)(2,1)S(1)} %add_convert_fusion.4), channel_id=1, source_target_pairs={{8,0},{16,8},{24,16},{32,24},{40,32},{48,40},{56,48},{64,56},{72,6... | collective-permute-start | bytes 786440 | tf_op jit(solution)/shard_map/ppermute | solution.py:39
  95.3 3.5 %grads.7 = (f32[256,512]{1,0:T(8,128)S(1)}, f32[256,512]{1,0:T(8,128)S(1)}, f32[256,512]{1,0:T(8,128)S(1)}, bf16[256,512]{1,0:T(8,128)(2,1)S(1)}) custom-call(s32[1]{0:T(128)} %bitcast.low_ref.refs_0_, s32[4,14]{1,0:T(4,128)S(1)} %fusion.1.refs_0_.hit_ref.refs_1_, s32[1,512]{1,0:T(1,128)S(1)} %bitcast.23, ...), custom_call_target="tpu_custom_call" | custom-call | flops 1024 | bytes 1835008 | tf_op jit(solution)/shard_map/grads/pallas_call | solution.py:306
  98.9 2.0 %collective-permute-start.15 = (bf16[256,512]{1,0:T(8,128)(2,1)S(1)}, bf16[256,512]{1,0:T(8,128)(2,1)S(1)}, u32[]{:S(2)}, u32[]{:S(2)}) collective-permute-start(bf16[256,512]{1,0:T(8,128)(2,1)S(1)} %add_convert_fusion.2), channel_id=1, source_target_pairs={{8,0},{16,8},{24,16},{32,24},{40,32},{48,40},{56,48},{64,56},{72,6... | collective-permute-start | bytes 786440 | tf_op jit(solution)/shard_map/ppermute | solution.py:39
  100.9 0.3 collective-permute-start.11
  101.3 5.9 %collective-permute-start.13 = (bf16[256,512]{1,0:T(8,128)(2,1)S(1)}, bf16[256,512]{1,0:T(8,128)(2,1)S(1)}, u32[]{:S(2)}, u32[]{:S(2)}) collective-permute-start(bf16[256,512]{1,0:T(8,128)(2,1)S(1)} %add_convert_fusion.3), channel_id=1, source_target_pairs={{8,0},{16,8},{24,16},{32,24},{40,32},{48,40},{56,48},{64,56},{72,6... | collective-permute-start | bytes 786440 | tf_op jit(solution)/shard_map/ppermute | solution.py:39
  107.3 0.8 dynamic_update_slice.6
  108.2 2.9 %collective-permute-done.13 = bf16[256,512]{1,0:T(8,128)(2,1)S(1)} collective-permute-done((bf16[256,512]{1,0:T(8,128)(2,1)S(1)}, bf16[256,512]{1,0:T(8,128)(2,1)S(1)}, u32[]{:S(2)}, u32[]{:S(2)}) %collective-permute-start.13) | collective-permute-done | bytes 262176 | tf_op jit(solution)/shard_map/ppermute | solution.py:39
  111.1 0.8 fusion
  111.9 3.5 %all-to-all-start.1 = ((bf16[8,64,512]{2,1,0:T(8,128)(2,1)}), bf16[8,64,512]{2,1,0:T(8,128)(2,1)S(1)}, u32[]{:S(2)}, u32[]{:S(2)}) async-start(bf16[8,64,512]{2,1,0:T(8,128)(2,1)} %bitcast.7), calls=%async_computation.1 | async-start | bytes 1048576 | tf_op jit(solution)/shard_map/all_to_all | solution.py:387
  115.4 1.0 columns.1
  116.4 8.9 %all-to-all-done.1.in_ref = bf16[8,64,512]{2,1,0:T(8,128)(2,1)S(1)} async-done(((bf16[8,64,512]{2,1,0:T(8,128)(2,1)}), bf16[8,64,512]{2,1,0:T(8,128)(2,1)S(1)}, u32[]{:S(2)}, u32[]{:S(2)}) %all-to-all-start.1) | async-done | bytes 524320 | tf_op jit(solution)/shard_map/all_to_all | solution.py:387
  125.4 1.0 unpack.1
  (27 shorter events, 0.7 us)
Async XLA Ops:
  0.6 9.2 %copy-start = (s32[2,128,14]{1,0,2:T(2,128)S(1)}, s32[2,128,14]{1,0,2:T(2,128)}, u32[]{:S(2)}) copy-start(s32[2,128,14]{1,0,2:T(2,128)} %param.11) | copy-start | bytes 43012
  0.6 6.3 %copy-start.2 = (bf16[256,1024]{1,0:T(8,128)(2,1)S(1)}, bf16[256,1024]{1,0:T(8,128)(2,1)}, u32[]{:S(2)}) copy-start(bf16[256,1024]{1,0:T(8,128)(2,1)} %do_ref.1) | copy-start | bytes 1572868
  0.7 6.3 %copy-start.1 = (bf16[256,1024]{1,0:T(8,128)(2,1)S(1)}, bf16[256,1024]{1,0:T(8,128)(2,1)}, u32[]{:S(2)}) copy-start(bf16[256,1024]{1,0:T(8,128)(2,1)} %q_ref.1) | copy-start | bytes 1572868
  2.6 14.4 %all-to-all-start = ((bf16[8,64,512]{2,1,0:T(8,128)(2,1)}), bf16[8,64,512]{2,1,0:T(8,128)(2,1)S(1)}, u32[]{:S(2)}, u32[]{:S(2)}) async-start(bf16[8,64,512]{2,1,0:T(8,128)(2,1)} %pack.1), calls=%async_computation | async-start | bytes 1048576 | tf_op jit(solution)/shard_map/all_to_all | solution.py:349
  6.9 3.0 %copy-start.3 = (s32[16384]{0:T(1024)S(1)}, s32[16384]{0:T(1024)}, u32[]{:S(2)}) copy-start(s32[16384]{0:T(1024)} %param.10) | copy-start | bytes 196612
  7.9 26.5 %collective-permute-start = (bf16[2,256,512]{2,1,0:T(8,128)(2,1)}, bf16[2,256,512]{2,1,0:T(8,128)(2,1)S(1)}, u32[]{:S(2)}, u32[]{:S(2)}) collective-permute-start(bf16[2,256,512]{2,1,0:T(8,128)(2,1)} %pad_maximum_fusion), channel_id=1, source_target_pairs={{0,4},{4,0},{1,5},{5,1},{2,6},{6,2},{3,7},{7,3},{8,12},{12,8},{9,1... | collective-permute-start | bytes 1572872 | tf_op jit(solution)/shard_map/ppermute | solution.py:43
  17.0 15.2 %collective-permute-start.1 = (bf16[256,512]{1,0:T(8,128)(2,1)S(1)}, bf16[256,512]{1,0:T(8,128)(2,1)S(1)}, u32[]{:S(2)}, u32[]{:S(2)}) collective-permute-start(bf16[256,512]{1,0:T(8,128)(2,1)S(1)} %bitcast.13), channel_id=1, source_target_pairs={{0,8},{8,16},{16,24},{24,32},{32,40},{40,48},{48,56},{56,64},{64,7... | collective-permute-start | bytes 786440 | tf_op jit(solution)/shard_map/ppermute | solution.py:39
  21.6 15.1 %collective-permute-start.3 = (bf16[256,512]{1,0:T(8,128)(2,1)S(1)}, bf16[256,512]{1,0:T(8,128)(2,1)S(1)}, u32[]{:S(2)}, u32[]{:S(2)}) collective-permute-start(bf16[256,512]{1,0:T(8,128)(2,1)S(1)} %bitcast.10), channel_id=1, source_target_pairs={{0,8},{8,16},{16,24},{24,32},{32,40},{40,48},{48,56},{56,64},{64,7... | collective-permute-start | bytes 786440 | tf_op jit(solution)/shard_map/ppermute | solution.py:39
  32.2 11.5 %collective-permute-start.2 = (bf16[256,512]{1,0:T(8,128)(2,1)S(1)}, bf16[256,512]{1,0:T(8,128)(2,1)S(1)}, u32[]{:S(2)}, u32[]{:S(2)}) collective-permute-start(bf16[256,512]{1,0:T(8,128)(2,1)S(1)} %collective-permute-done.1.refs_7_), channel_id=1, source_target_pairs={{0,8},{8,16},{16,24},{24,32},{32,40},{40,48},{48,56},{56,64},{64,7... | collective-permute-start | bytes 786440 | tf_op jit(solution)/shard_map/ppermute | solution.py:39
  36.7 13.0 %collective-permute-start.5 = (bf16[256,512]{1,0:T(8,128)(2,1)S(1)}, bf16[256,512]{1,0:T(8,128)(2,1)S(1)}, u32[]{:S(2)}, u32[]{:S(2)}) collective-permute-start(bf16[256,512]{1,0:T(8,128)(2,1)S(1)} %collective-permute-done.3.refs_6_), channel_id=1, source_target_pairs={{0,8},{8,16},{16,24},{24,32},{32,40},{40,48},{48,56},{56,64},{64,7... | collective-permute-start | bytes 786440 | tf_op jit(solution)/shard_map/ppermute | solution.py:39
  43.7 11.2 %collective-permute-start.4 = (bf16[256,512]{1,0:T(8,128)(2,1)S(1)}, bf16[256,512]{1,0:T(8,128)(2,1)S(1)}, u32[]{:S(2)}, u32[]{:S(2)}) collective-permute-start(bf16[256,512]{1,0:T(8,128)(2,1)S(1)} %collective-permute-done.2.refs_5_.refs_6_), channel_id=1, source_target_pairs={{0,8},{8,16},{16,24},{24,32},{32,40},{40,48},{48,56},{56,64},{64,7... | collective-permute-start | bytes 786440 | tf_op jit(solution)/shard_map/ppermute | solution.py:39
  49.7 13.0 %collective-permute-start.7 = (bf16[256,512]{1,0:T(8,128)(2,1)S(1)}, bf16[256,512]{1,0:T(8,128)(2,1)S(1)}, u32[]{:S(2)}, u32[]{:S(2)}) collective-permute-start(bf16[256,512]{1,0:T(8,128)(2,1)S(1)} %collective-permute-done.5.refs_4_.refs_5_), channel_id=1, source_target_pairs={{0,8},{8,16},{16,24},{24,32},{32,40},{40,48},{48,56},{56,64},{64,7... | collective-permute-start | bytes 786440 | tf_op jit(solution)/shard_map/ppermute | solution.py:39
  54.9 10.8 %collective-permute-start.6 = (bf16[256,512]{1,0:T(8,128)(2,1)S(1)}, bf16[256,512]{1,0:T(8,128)(2,1)S(1)}, u32[]{:S(2)}, u32[]{:S(2)}) collective-permute-start(bf16[256,512]{1,0:T(8,128)(2,1)S(1)} %collective-permute-done.4.refs_5_.refs_6_), channel_id=1, source_target_pairs={{0,8},{8,16},{16,24},{24,32},{32,40},{40,48},{48,56},{56,64},{64,7... | collective-permute-start | bytes 786440 | tf_op jit(solution)/shard_map/ppermute | solution.py:39
  67.4 12.2 %collective-permute-start.9 = (bf16[256,512]{1,0:T(8,128)(2,1)S(1)}, bf16[256,512]{1,0:T(8,128)(2,1)S(1)}, u32[]{:S(2)}, u32[]{:S(2)}) collective-permute-start(bf16[256,512]{1,0:T(8,128)(2,1)S(1)} %get-tuple-element.51), channel_id=1, source_target_pairs={{8,0},{16,8},{24,16},{32,24},{40,32},{48,40},{56,48},{64,56},{72,6... | collective-permute-start | bytes 786440 | tf_op jit(solution)/shard_map/ppermute | solution.py:39
  73.3 9.3 %collective-permute-start.8 = (bf16[256,512]{1,0:T(8,128)(2,1)S(1)}, bf16[256,512]{1,0:T(8,128)(2,1)S(1)}, u32[]{:S(2)}, u32[]{:S(2)}) collective-permute-start(bf16[256,512]{1,0:T(8,128)(2,1)S(1)} %get-tuple-element.49), channel_id=1, source_target_pairs={{8,0},{16,8},{24,16},{32,24},{40,32},{48,40},{56,48},{64,56},{72,6... | collective-permute-start | bytes 786440 | tf_op jit(solution)/shard_map/ppermute | solution.py:39
  79.6 10.6 %collective-permute-start.10 = (bf16[256,512]{1,0:T(8,128)(2,1)S(1)}, bf16[256,512]{1,0:T(8,128)(2,1)S(1)}, u32[]{:S(2)}, u32[]{:S(2)}) collective-permute-start(bf16[256,512]{1,0:T(8,128)(2,1)S(1)} %add_convert_fusion.5), channel_id=1, source_target_pairs={{8,0},{16,8},{24,16},{32,24},{40,32},{48,40},{56,48},{64,56},{72,6... | collective-permute-start | bytes 786440 | tf_op jit(solution)/shard_map/ppermute | solution.py:39
  82.7 16.2 %collective-permute-start.14 = (bf16[256,512]{1,0:T(8,128)(2,1)S(1)}, bf16[256,512]{1,0:T(8,128)(2,1)S(1)}, u32[]{:S(2)}, u32[]{:S(2)}) collective-permute-start(bf16[256,512]{1,0:T(8,128)(2,1)S(1)} %add_convert_fusion.6), channel_id=1, source_target_pairs={{8,0},{16,8},{24,16},{32,24},{40,32},{48,40},{56,48},{64,56},{72,6... | collective-permute-start | bytes 786440 | tf_op jit(solution)/shard_map/ppermute | solution.py:39
  90.3 11.0 %collective-permute-start.12 = (bf16[256,512]{1,0:T(8,128)(2,1)S(1)}, bf16[256,512]{1,0:T(8,128)(2,1)S(1)}, u32[]{:S(2)}, u32[]{:S(2)}) collective-permute-start(bf16[256,512]{1,0:T(8,128)(2,1)S(1)} %add_convert_fusion.4), channel_id=1, source_target_pairs={{8,0},{16,8},{24,16},{32,24},{40,32},{48,40},{56,48},{64,56},{72,6... | collective-permute-start | bytes 786440 | tf_op jit(solution)/shard_map/ppermute | solution.py:39
  98.9 8.3 %collective-permute-start.15 = (bf16[256,512]{1,0:T(8,128)(2,1)S(1)}, bf16[256,512]{1,0:T(8,128)(2,1)S(1)}, u32[]{:S(2)}, u32[]{:S(2)}) collective-permute-start(bf16[256,512]{1,0:T(8,128)(2,1)S(1)} %add_convert_fusion.2), channel_id=1, source_target_pairs={{8,0},{16,8},{24,16},{32,24},{40,32},{48,40},{56,48},{64,56},{72,6... | collective-permute-start | bytes 786440 | tf_op jit(solution)/shard_map/ppermute | solution.py:39
  100.9 7.3 %collective-permute-start.11 = (bf16[256,512]{1,0:T(8,128)(2,1)S(1)}, bf16[256,512]{1,0:T(8,128)(2,1)S(1)}, u32[]{:S(2)}, u32[]{:S(2)}) collective-permute-start(bf16[256,512]{1,0:T(8,128)(2,1)S(1)} %get-tuple-element.59), channel_id=1, source_target_pairs={{0,4},{4,0},{1,5},{5,1},{2,6},{6,2},{3,7},{7,3},{8,12},{12,8},{9,1... | collective-permute-start | bytes 786440 | tf_op jit(solution)/shard_map/ppermute | solution.py:43
  101.3 9.8 %collective-permute-start.13 = (bf16[256,512]{1,0:T(8,128)(2,1)S(1)}, bf16[256,512]{1,0:T(8,128)(2,1)S(1)}, u32[]{:S(2)}, u32[]{:S(2)}) collective-permute-start(bf16[256,512]{1,0:T(8,128)(2,1)S(1)} %add_convert_fusion.3), channel_id=1, source_target_pairs={{8,0},{16,8},{24,16},{32,24},{40,32},{48,40},{56,48},{64,56},{72,6... | collective-permute-start | bytes 786440 | tf_op jit(solution)/shard_map/ppermute | solution.py:39
  111.9 13.5 %all-to-all-start.1 = ((bf16[8,64,512]{2,1,0:T(8,128)(2,1)}), bf16[8,64,512]{2,1,0:T(8,128)(2,1)S(1)}, u32[]{:S(2)}, u32[]{:S(2)}) async-start(bf16[8,64,512]{2,1,0:T(8,128)(2,1)} %bitcast.7), calls=%async_computation.1 | async-start | bytes 1048576 | tf_op jit(solution)/shard_map/all_to_all | solution.py:387

commit v6 on v5

--- a/solution.py
+++ b/solution.py
@@ -343,7 +343,6 @@
         out_specs=VMEM_SPEC,
         scratch_shapes=[pltpu.VMEM((SPAN // 4, KEY_VALUE_HEADS * HEAD_SIZE), jnp.bfloat16)] * 2
         + [pltpu.SemaphoreType.DMA((2,))],
-        cost_estimate=pl.CostEstimate(flops=1024, bytes_accessed=1 << 25, transcendentals=0),
         name="pack",
     )(key_states, value_inputs)
     own = lax.all_to_all(kv, MEMBER_AXES, 0, 0, tiled=True)
@@ -392,19 +391,15 @@
     def summed(part, arrived):
         return (part + arrived.astype(full)).astype(low16)
 
-    def after(arrived, value):
-        return lax.optimization_barrier((arrived, value))[1]
-
     rb = slab_shift(gb4, -1)
     ga3, gb3, dqt = grads((2, 4), tables, norm, (a3, b3), dqt, (low16, full), light=True)
     ra = slab_shift(ga3, -1)
-    ga2, gb2, dqt = grads((6, 8), tables, norm, (a2, b2), dqt, (full, full), light=True)
+    g0, dqt = grads((14, 16), tables, norm, (a0, b0), dqt, (full,), light=True)
     dqt, rb = lax.optimization_barrier((dqt, rb))
     rb = slab_shift(summed(gb3, rb), -1)
-    ra = summed(ga2, ra)
-    dqt = after(ra, dqt)
-    ra = slab_shift(ra, -1)
-    g0, dqt = grads((14, 16), tables, norm, (a0, b0), dqt, (full,), light=True)
+    dqt, ra = lax.optimization_barrier((dqt, ra))
+    ga2, gb2, dqt = grads((6, 8), tables, norm, (a2, b2), dqt, (full, full))
+    ra = slab_shift(summed(ga2, ra), -1)
     dqt, rb = lax.optimization_barrier((dqt, rb))
     rb = slab_shift(summed(gb2, rb), -1)
     ga1, gb1, mine, send = grads((10, 12), tables, norm, (a1, b1), dqt, (full, full), low_ref)

time: 127 us -> 127 us (level)
  waiting for transfers between devices: 41.1 us -> 43 us
  starting transfers between devices: 53.6 us -> 52.3 us
    ppermute x14, starting transfers between devices: 43.5 us -> 41.8 us  [slab_shift(): lax.ppermute(x, SLAB_AXES, [(i, i + by) for i in range(count) if 0 <= i +...]
  transfers between devices with their start and end apart: 18 -> 18, of which waited for: 10 -> 12; matrix products, arithmetic and copies ran while one was open for 3% -> 2% of each run, Pallas kernels for 17% -> 17%
where the time goes in v6:
time: 127 us; the launch traced here: 126 us
  starting transfers between devices  52.3 us (41%)
  waiting for transfers between devices  43 us (34%)
  Pallas kernels  26.5 us (21%)
  other arithmetic  2 us (2%)
  local copies, waits for them, and re-layouts  1.37 us (1%)
    ppermute x14, starting transfers between devices, slab_shift(): lax.ppermute(x, SLAB_AXES, [(i, i + by) for i in range(count) if 0 <= i +...  41.8 us
    ppermute x14, waiting for transfers between devices, slab_shift(): lax.ppermute(x, SLAB_AXES, [(i, i + by) for i in range(count) if 0 <= i +...  26.3 us
    pallas_call x4, Pallas kernels, grads(): call(functools.partial(grads_kernel, first_blocks, opening, closing), 'gr...  12.8 us
    all_to_all x1, waiting for transfers between devices, to_owners(): lax.all_to_all(x.reshape(8, SPAN // 4, 2 * WIDTH), MEMBER_AXES, 0, 0, til...  9.02 us
    pallas_call x3, Pallas kernels, stats(): call(functools.partial(stats_kernel, first_blocks, opening, closing), 'st...  7.78 us
    all_to_all x1, waiting for transfers between devices, per_device(): own = lax.all_to_all(kv, MEMBER_AXES, 0, 0, tiled=True)  7.64 us
    all_to_all x1, starting transfers between devices, per_device(): own = lax.all_to_all(kv, MEMBER_AXES, 0, 0, tiled=True)  4.31 us
    all_to_all x1, starting transfers between devices, to_owners(): lax.all_to_all(x.reshape(8, SPAN // 4, 2 * WIDTH), MEMBER_AXES, 0, 0, til...  3.79 us
  transfers between devices with their start and end apart: 18, of which 12 were waited for; matrix products, arithmetic and copies ran while one was open for 2% of the time, Pallas kernels for 17%

profile of v6, /device:TPU:24, one launch (start us, length us, event | category | flops | bytes accessed | tf_op | source)
XLA Modules:
  0.0 126.2 jit_solution(8947147673778956827)
XLA Ops:
  0.7 1.9 %pack.1 = bf16[8,64,512]{2,1,0:T(8,128)(2,1)} custom-call(bf16[64,2048]{1,0:T(8,128)(2,1)} %k_ref.1, bf16[64,2048]{1,0:T(8,128)(2,1)} %v_ref.1), custom_call_target="tpu_custom_call" | custom-call | tf_op jit(solution)/shard_map/pack/pallas_call | solution.py:339
  2.6 4.3 %all-to-all-start = ((bf16[8,64,512]{2,1,0:T(8,128)(2,1)}), bf16[8,64,512]{2,1,0:T(8,128)(2,1)S(1)}, u32[]{:S(2)}, u32[]{:S(2)}) async-start(bf16[8,64,512]{2,1,0:T(8,128)(2,1)} %pack.1), calls=%async_computation | async-start | bytes 1048576 | tf_op jit(solution)/shard_map/all_to_all | solution.py:348
  7.1 2.1 %collective-permute-start = (bf16[2,256,512]{2,1,0:T(8,128)(2,1)S(1)}, bf16[2,256,512]{2,1,0:T(8,128)(2,1)S(1)}, u32[]{:S(2)}, u32[]{:S(2)}) collective-permute-start(bf16[2,256,512]{2,1,0:T(8,128)(2,1)S(1)} %pad_maximum_fusion), channel_id=1, source_target_pairs={{0,4},{4,0},{1,5},{5,1},{2,6},{6,2},{3,7},{7,3},{8,12},{12,8},{9,1... | collective-permute-start | bytes 1572872 | tf_op jit(solution)/shard_map/ppermute | solution.py:43
  9.3 0.1 pad_dynamic-slice_fusion.1
  9.3 7.6 %all-to-all-done = bf16[8,64,512]{2,1,0:T(8,128)(2,1)S(1)} async-done(((bf16[8,64,512]{2,1,0:T(8,128)(2,1)}), bf16[8,64,512]{2,1,0:T(8,128)(2,1)S(1)}, u32[]{:S(2)}, u32[]{:S(2)}) %all-to-all-start) | async-done | bytes 524320 | tf_op jit(solution)/shard_map/all_to_all | solution.py:348
  17.0 3.8 %collective-permute-start.1 = (bf16[256,512]{1,0:T(8,128)(2,1)S(1)}, bf16[256,512]{1,0:T(8,128)(2,1)S(1)}, u32[]{:S(2)}, u32[]{:S(2)}) collective-permute-start(bf16[256,512]{1,0:T(8,128)(2,1)S(1)} %bitcast.13), channel_id=1, source_target_pairs={{0,8},{8,16},{16,24},{24,32},{32,40},{40,48},{48,56},{56,64},{64,7... | collective-permute-start | bytes 786440 | tf_op jit(solution)/shard_map/ppermute | solution.py:39
  20.9 0.7 convert_reduce_fusion
  21.6 3.8 %collective-permute-start.3 = (bf16[256,512]{1,0:T(8,128)(2,1)S(1)}, bf16[256,512]{1,0:T(8,128)(2,1)S(1)}, u32[]{:S(2)}, u32[]{:S(2)}) collective-permute-start(bf16[256,512]{1,0:T(8,128)(2,1)S(1)} %bitcast.10), channel_id=1, source_target_pairs={{0,8},{8,16},{16,24},{24,32},{32,40},{40,48},{48,56},{56,64},{64,7... | collective-permute-start | bytes 786440 | tf_op jit(solution)/shard_map/ppermute | solution.py:39
  25.4 6.8 %collective-permute-done.1.refs_7_ = bf16[256,512]{1,0:T(8,128)(2,1)S(1)} collective-permute-done((bf16[256,512]{1,0:T(8,128)(2,1)S(1)}, bf16[256,512]{1,0:T(8,128)(2,1)S(1)}, u32[]{:S(2)}, u32[]{:S(2)}) %collective-permute-start.1) | collective-permute-done | bytes 262176 | tf_op jit(solution)/shard_map/ppermute | solution.py:39
  32.2 1.9 %collective-permute-start.2 = (bf16[256,512]{1,0:T(8,128)(2,1)S(1)}, bf16[256,512]{1,0:T(8,128)(2,1)S(1)}, u32[]{:S(2)}, u32[]{:S(2)}) collective-permute-start(bf16[256,512]{1,0:T(8,128)(2,1)S(1)} %collective-permute-done.1.refs_7_), channel_id=1, source_target_pairs={{0,8},{8,16},{16,24},{24,32},{32,40},{40,48},{48,56},{56,64},{64,7... | collective-permute-start | bytes 786440 | tf_op jit(solution)/shard_map/ppermute | solution.py:39
  34.1 0.1 copy.13
  34.2 0.1 rev.3
  34.4 0.2 rows.1
  34.6 2.1 %collective-permute-done.3.refs_6_ = bf16[256,512]{1,0:T(8,128)(2,1)S(1)} collective-permute-done((bf16[256,512]{1,0:T(8,128)(2,1)S(1)}, bf16[256,512]{1,0:T(8,128)(2,1)S(1)}, u32[]{:S(2)}, u32[]{:S(2)}) %collective-permute-start.3) | collective-permute-done | bytes 262176 | tf_op jit(solution)/shard_map/ppermute | solution.py:39
  36.7 1.9 %collective-permute-start.5 = (bf16[256,512]{1,0:T(8,128)(2,1)S(1)}, bf16[256,512]{1,0:T(8,128)(2,1)S(1)}, u32[]{:S(2)}, u32[]{:S(2)}) collective-permute-start(bf16[256,512]{1,0:T(8,128)(2,1)S(1)} %collective-permute-done.3.refs_6_), channel_id=1, source_target_pairs={{0,8},{8,16},{16,24},{24,32},{32,40},{40,48},{48,56},{56,64},{64,7... | collective-permute-start | bytes 786440 | tf_op jit(solution)/shard_map/ppermute | solution.py:39
  38.6 3.3 %stats.3.refs_6_ = f32[2,3,8,1024]{3,2,1,0:T(8,128)S(1)} custom-call(s32[4,14]{1,0:T(4,128)S(1)} %fusion.1.refs_0_.hit_ref.refs_1_, s32[1,512]{1,0:T(1,128)S(1)} %bitcast.16, bf16[2,1024,128]{2,1,0:T(8,128)(2,1)S(1)} %get-tuple-element.38.refs_2_.q_ref.refs_3_, bf16[2,1024,128]{2,1,0:T(8,128)(2,1)S(1)} %get-tuple-element.39.refs_3_.do_ref.refs_4_, ...), custom_call_target="tpu_custom_call" | custom-call | flops 1024 | bytes 196608 | tf_op jit(solution)/shard_map/stats/pallas_call | solution.py:197
  41.9 1.8 %collective-permute-done.2.refs_5_.refs_6_ = bf16[256,512]{1,0:T(8,128)(2,1)S(1)} collective-permute-done((bf16[256,512]{1,0:T(8,128)(2,1)S(1)}, bf16[256,512]{1,0:T(8,128)(2,1)S(1)}, u32[]{:S(2)}, u32[]{:S(2)}) %collective-permute-start.2) | collective-permute-done | bytes 262176 | tf_op jit(solution)/shard_map/ppermute | solution.py:39
  43.7 1.9 %collective-permute-start.4 = (bf16[256,512]{1,0:T(8,128)(2,1)S(1)}, bf16[256,512]{1,0:T(8,128)(2,1)S(1)}, u32[]{:S(2)}, u32[]{:S(2)}) collective-permute-start(bf16[256,512]{1,0:T(8,128)(2,1)S(1)} %collective-permute-done.2.refs_5_.refs_6_), channel_id=1, source_target_pairs={{0,8},{8,16},{16,24},{24,32},{32,40},{40,48},{48,56},{56,64},{64,7... | collective-permute-start | bytes 786440 | tf_op jit(solution)/shard_map/ppermute | solution.py:39
  45.6 4.1 %collective-permute-done.5.refs_4_.refs_5_ = bf16[256,512]{1,0:T(8,128)(2,1)S(1)} collective-permute-done((bf16[256,512]{1,0:T(8,128)(2,1)S(1)}, bf16[256,512]{1,0:T(8,128)(2,1)S(1)}, u32[]{:S(2)}, u32[]{:S(2)}) %collective-permute-start.5) | collective-permute-done | bytes 262176 | tf_op jit(solution)/shard_map/ppermute | solution.py:39
  49.7 1.9 %collective-permute-start.7 = (bf16[256,512]{1,0:T(8,128)(2,1)S(1)}, bf16[256,512]{1,0:T(8,128)(2,1)S(1)}, u32[]{:S(2)}, u32[]{:S(2)}) collective-permute-start(bf16[256,512]{1,0:T(8,128)(2,1)S(1)} %collective-permute-done.5.refs_4_.refs_5_), channel_id=1, source_target_pairs={{0,8},{8,16},{16,24},{24,32},{32,40},{40,48},{48,56},{56,64},{64,7... | collective-permute-start | bytes 786440 | tf_op jit(solution)/shard_map/ppermute | solution.py:39
  51.6 2.3 %stats.4.refs_6_ = f32[2,3,8,1024]{3,2,1,0:T(8,128)S(1)} custom-call(s32[4,14]{1,0:T(4,128)S(1)} %fusion.1.refs_0_.hit_ref.refs_1_, s32[1,512]{1,0:T(1,128)S(1)} %bitcast.17, bf16[2,1024,128]{2,1,0:T(8,128)(2,1)S(1)} %get-tuple-element.38.refs_2_.q_ref.refs_3_, bf16[2,1024,128]{2,1,0:T(8,128)(2,1)S(1)} %get-tuple-element.39.refs_3_.do_ref.refs_4_, ...), custom_call_target="tpu_custom_call" | custom-call | flops 1024 | bytes 196608 | tf_op jit(solution)/shard_map/stats/pallas_call | solution.py:197
  53.9 1.0 collective-permute-done.4.refs_5_.refs_6_
  54.9 2.1 %collective-permute-start.6 = (bf16[256,512]{1,0:T(8,128)(2,1)S(1)}, bf16[256,512]{1,0:T(8,128)(2,1)S(1)}, u32[]{:S(2)}, u32[]{:S(2)}) collective-permute-start(bf16[256,512]{1,0:T(8,128)(2,1)S(1)} %collective-permute-done.4.refs_5_.refs_6_), channel_id=1, source_target_pairs={{0,8},{8,16},{16,24},{24,32},{32,40},{40,48},{48,56},{56,64},{64,7... | collective-permute-start | bytes 786440 | tf_op jit(solution)/shard_map/ppermute | solution.py:39
  56.9 5.7 %collective-permute-done.7.refs_4_.refs_5_ = bf16[256,512]{1,0:T(8,128)(2,1)S(1)} collective-permute-done((bf16[256,512]{1,0:T(8,128)(2,1)S(1)}, bf16[256,512]{1,0:T(8,128)(2,1)S(1)}, u32[]{:S(2)}, u32[]{:S(2)}) %collective-permute-start.7) | collective-permute-done | bytes 262176 | tf_op jit(solution)/shard_map/ppermute | solution.py:39
  62.6 2.2 %stats.5.state = f32[2,3,8,1024]{3,2,1,0:T(8,128)S(1)} custom-call(s32[4,14]{1,0:T(4,128)S(1)} %fusion.1.refs_0_.hit_ref.refs_1_, s32[1,512]{1,0:T(1,128)S(1)} %bitcast.18, bf16[2,1024,128]{2,1,0:T(8,128)(2,1)S(1)} %get-tuple-element.38.refs_2_.q_ref.refs_3_, bf16[2,1024,128]{2,1,0:T(8,128)(2,1)S(1)} %get-tuple-element.39.refs_3_.do_ref.refs_4_, ...), custom_call_target="tpu_custom_call" | custom-call | flops 1024 | bytes 196608 | tf_op jit(solution)/shard_map/stats/pallas_call | solution.py:197
  64.8 0.8 collective-permute-done.6.piece
  65.6 1.7 %finish.1 = (f32[2,8,1024]{2,1,0:T(8,128)S(1)}, bf16[256,512]{1,0:T(8,128)(2,1)S(1)}, f32[2,128,1024]{2,1,0:T(8,128)S(1)}) custom-call(s32[4,14]{1,0:T(4,128)S(1)} %fusion.1.refs_0_.hit_ref.refs_1_, s32[1,512]{1,0:T(1,128)S(1)} %bitcast.19, bf16[2,1024,128]{2,1,0:T(8,128)(2,1)S(1)} %get-tuple-element.38.refs_2_.q_ref.refs_3_, ...), custom_call_target="tpu_custom_call" | custom-call | flops 1024 | bytes 1376256 | tf_op jit(solution)/shard_map/finish/pallas_call | solution.py:324
  67.4 2.5 %collective-permute-start.8 = (bf16[256,512]{1,0:T(8,128)(2,1)S(1)}, bf16[256,512]{1,0:T(8,128)(2,1)S(1)}, u32[]{:S(2)}, u32[]{:S(2)}) collective-permute-start(bf16[256,512]{1,0:T(8,128)(2,1)S(1)} %get-tuple-element.50), channel_id=1, source_target_pairs={{8,0},{16,8},{24,16},{32,24},{40,32},{48,40},{56,48},{64,56},{72,6... | collective-permute-start | bytes 786440 | tf_op jit(solution)/shard_map/ppermute | solution.py:39
  69.9 3.3 %grads.4 = (bf16[256,512]{1,0:T(8,128)(2,1)S(1)}, f32[256,512]{1,0:T(8,128)S(1)}, f32[2,128,1024]{2,1,0:T(8,128)S(1)}) custom-call(s32[4,14]{1,0:T(4,128)S(1)} %fusion.1.refs_0_.hit_ref.refs_1_, s32[1,512]{1,0:T(1,128)S(1)} %bitcast.20, bf16[2,1024,128]{2,1,0:T(8,128)(2,1)S(1)} %get-tuple-element.38.refs_2_.q_ref.refs_3_, ...), custom_call_target="tpu_custom_call", output_to_operand_aliasing={{2}: (7, {})} | custom-call | flops 1024 | bytes 1 | tf_op jit(solution)/shard_map/grads/pallas_call | solution.py:306
  73.2 2.9 %collective-permute-start.9 = (bf16[256,512]{1,0:T(8,128)(2,1)S(1)}, bf16[256,512]{1,0:T(8,128)(2,1)S(1)}, u32[]{:S(2)}, u32[]{:S(2)}) collective-permute-start(bf16[256,512]{1,0:T(8,128)(2,1)S(1)} %get-tuple-element.52), channel_id=1, source_target_pairs={{8,0},{16,8},{24,16},{32,24},{40,32},{48,40},{56,48},{64,56},{72,6... | collective-permute-start | bytes 786440 | tf_op jit(solution)/shard_map/ppermute | solution.py:39
  76.1 2.6 %grads.5 = (f32[512,512]{1,0:T(8,128)S(1)}, f32[2,128,1024]{2,1,0:T(8,128)S(1)}) custom-call(s32[4,14]{1,0:T(4,128)S(1)} %fusion.1.refs_0_.hit_ref.refs_1_, s32[1,512]{1,0:T(1,128)S(1)} %bitcast.21, bf16[2,1024,128]{2,1,0:T(8,128)(2,1)S(1)} %get-tuple-element.38.refs_2_.q_ref.refs_3_, ...), custom_call_target="tpu_custom_call", output_to_operand_aliasing={{1}: (7, {})} | custom-call | flops 1024 | bytes 1 | tf_op jit(solution)/shard_map/grads/pallas_call | solution.py:306
  78.8 2.9 %collective-permute-start.10 = (bf16[256,512]{1,0:T(8,128)(2,1)S(1)}, bf16[256,512]{1,0:T(8,128)(2,1)S(1)}, u32[]{:S(2)}, u32[]{:S(2)}) collective-permute-start(bf16[256,512]{1,0:T(8,128)(2,1)S(1)} %add_convert_fusion.6), channel_id=1, source_target_pairs={{8,0},{16,8},{24,16},{32,24},{40,32},{48,40},{56,48},{64,56},{72,6... | collective-permute-start | bytes 786440 | tf_op jit(solution)/shard_map/ppermute | solution.py:39
  81.8 0.7 collective-permute-done.9
  82.5 3.4 %grads.6 = (f32[256,512]{1,0:T(8,128)S(1)}, f32[256,512]{1,0:T(8,128)S(1)}, f32[2,128,1024]{2,1,0:T(8,128)S(1)}) custom-call(s32[4,14]{1,0:T(4,128)S(1)} %fusion.1.refs_0_.hit_ref.refs_1_, s32[1,512]{1,0:T(1,128)S(1)} %bitcast.22, bf16[2,1024,128]{2,1,0:T(8,128)(2,1)S(1)} %get-tuple-element.38.refs_2_.q_ref.refs_3_, ...), custom_call_target="tpu_custom_call", output_to_operand_aliasing={{2}: (7, {})} | custom-call | flops 1024 | bytes 2097152 | tf_op jit(solution)/shard_map/grads/pallas_call | solution.py:306
  85.9 4.9 %collective-permute-start.14 = (bf16[256,512]{1,0:T(8,128)(2,1)S(1)}, bf16[256,512]{1,0:T(8,128)(2,1)S(1)}, u32[]{:S(2)}, u32[]{:S(2)}) collective-permute-start(bf16[256,512]{1,0:T(8,128)(2,1)S(1)} %add_convert_fusion.3), channel_id=1, source_target_pairs={{8,0},{16,8},{24,16},{32,24},{40,32},{48,40},{56,48},{64,56},{72,6... | collective-permute-start | bytes 786440 | tf_op jit(solution)/shard_map/ppermute | solution.py:39
  91.0 2.8 %collective-permute-start.12 = (bf16[256,512]{1,0:T(8,128)(2,1)S(1)}, bf16[256,512]{1,0:T(8,128)(2,1)S(1)}, u32[]{:S(2)}, u32[]{:S(2)}) collective-permute-start(bf16[256,512]{1,0:T(8,128)(2,1)S(1)} %add_convert_fusion.5), channel_id=1, source_target_pairs={{8,0},{16,8},{24,16},{32,24},{40,32},{48,40},{56,48},{64,56},{72,6... | collective-permute-start | bytes 786440 | tf_op jit(solution)/shard_map/ppermute | solution.py:39
  93.8 3.5 %grads.7 = (f32[256,512]{1,0:T(8,128)S(1)}, f32[256,512]{1,0:T(8,128)S(1)}, f32[256,512]{1,0:T(8,128)S(1)}, bf16[256,512]{1,0:T(8,128)(2,1)S(1)}) custom-call(s32[1]{0:T(128)} %bitcast.low_ref.refs_0_, s32[4,14]{1,0:T(4,128)S(1)} %fusion.1.refs_0_.hit_ref.refs_1_, s32[1,512]{1,0:T(1,128)S(1)} %bitcast.23, ...), custom_call_target="tpu_custom_call" | custom-call | flops 1024 | bytes 1835008 | tf_op jit(solution)/shard_map/grads/pallas_call | solution.py:306
  97.4 4.4 %collective-permute-start.15 = (bf16[256,512]{1,0:T(8,128)(2,1)S(1)}, bf16[256,512]{1,0:T(8,128)(2,1)S(1)}, u32[]{:S(2)}, u32[]{:S(2)}) collective-permute-start(bf16[256,512]{1,0:T(8,128)(2,1)S(1)} %add_convert_fusion.2), channel_id=1, source_target_pairs={{8,0},{16,8},{24,16},{32,24},{40,32},{48,40},{56,48},{64,56},{72,6... | collective-permute-start | bytes 786440 | tf_op jit(solution)/shard_map/ppermute | solution.py:39
  101.8 0.3 collective-permute-start.11
  102.2 3.9 %collective-permute-start.13 = (bf16[256,512]{1,0:T(8,128)(2,1)S(1)}, bf16[256,512]{1,0:T(8,128)(2,1)S(1)}, u32[]{:S(2)}, u32[]{:S(2)}) collective-permute-start(bf16[256,512]{1,0:T(8,128)(2,1)S(1)} %add_convert_fusion.4), channel_id=1, source_target_pairs={{8,0},{16,8},{24,16},{32,24},{40,32},{48,40},{56,48},{64,56},{72,6... | collective-permute-start | bytes 786440 | tf_op jit(solution)/shard_map/ppermute | solution.py:39
  106.2 1.5 %collective-permute-done.15 = bf16[256,512]{1,0:T(8,128)(2,1)S(1)} collective-permute-done((bf16[256,512]{1,0:T(8,128)(2,1)S(1)}, bf16[256,512]{1,0:T(8,128)(2,1)S(1)}, u32[]{:S(2)}, u32[]{:S(2)}) %collective-permute-start.15) | collective-permute-done | bytes 262176 | tf_op jit(solution)/shard_map/ppermute | solution.py:39
  107.7 0.8 dynamic_update_slice.6
  108.6 1.9 %collective-permute-done.13 = bf16[256,512]{1,0:T(8,128)(2,1)S(1)} collective-permute-done((bf16[256,512]{1,0:T(8,128)(2,1)S(1)}, bf16[256,512]{1,0:T(8,128)(2,1)S(1)}, u32[]{:S(2)}, u32[]{:S(2)}) %collective-permute-start.13) | collective-permute-done | bytes 262176 | tf_op jit(solution)/shard_map/ppermute | solution.py:39
  110.5 0.8 fusion
  111.3 3.8 %all-to-all-start.1 = ((bf16[8,64,512]{2,1,0:T(8,128)(2,1)}), bf16[8,64,512]{2,1,0:T(8,128)(2,1)S(1)}, u32[]{:S(2)}, u32[]{:S(2)}) async-start(bf16[8,64,512]{2,1,0:T(8,128)(2,1)} %bitcast.7), calls=%async_computation.1 | async-start | bytes 1048576 | tf_op jit(solution)/shard_map/all_to_all | solution.py:386
  115.1 1.0 columns.1
  116.1 9.0 %all-to-all-done.1.in_ref = bf16[8,64,512]{2,1,0:T(8,128)(2,1)S(1)} async-done(((bf16[8,64,512]{2,1,0:T(8,128)(2,1)}), bf16[8,64,512]{2,1,0:T(8,128)(2,1)S(1)}, u32[]{:S(2)}, u32[]{:S(2)}) %all-to-all-start.1) | async-done | bytes 524320 | tf_op jit(solution)/shard_map/all_to_all | solution.py:386
  125.1 1.0 unpack.1
  (27 shorter events, 0.9 us)
Async XLA Ops:
  0.6 8.5 %copy-start = (s32[2,128,14]{1,0,2:T(2,128)S(1)}, s32[2,128,14]{1,0,2:T(2,128)}, u32[]{:S(2)}) copy-start(s32[2,128,14]{1,0,2:T(2,128)} %param.11) | copy-start | bytes 43012
  0.6 6.3 %copy-start.2 = (bf16[256,1024]{1,0:T(8,128)(2,1)S(1)}, bf16[256,1024]{1,0:T(8,128)(2,1)}, u32[]{:S(2)}) copy-start(bf16[256,1024]{1,0:T(8,128)(2,1)} %do_ref.1) | copy-start | bytes 1572868
  0.7 6.3 %copy-start.1 = (bf16[256,1024]{1,0:T(8,128)(2,1)S(1)}, bf16[256,1024]{1,0:T(8,128)(2,1)}, u32[]{:S(2)}) copy-start(bf16[256,1024]{1,0:T(8,128)(2,1)} %q_ref.1) | copy-start | bytes 1572868
  2.6 14.4 %all-to-all-start = ((bf16[8,64,512]{2,1,0:T(8,128)(2,1)}), bf16[8,64,512]{2,1,0:T(8,128)(2,1)S(1)}, u32[]{:S(2)}, u32[]{:S(2)}) async-start(bf16[8,64,512]{2,1,0:T(8,128)(2,1)} %pack.1), calls=%async_computation | async-start | bytes 1048576 | tf_op jit(solution)/shard_map/all_to_all | solution.py:348
  6.9 2.3 %copy-start.3 = (s32[16384]{0:T(1024)S(1)}, s32[16384]{0:T(1024)}, u32[]{:S(2)}) copy-start(s32[16384]{0:T(1024)} %param.10) | copy-start | bytes 196612
  7.1 27.3 %collective-permute-start = (bf16[2,256,512]{2,1,0:T(8,128)(2,1)S(1)}, bf16[2,256,512]{2,1,0:T(8,128)(2,1)S(1)}, u32[]{:S(2)}, u32[]{:S(2)}) collective-permute-start(bf16[2,256,512]{2,1,0:T(8,128)(2,1)S(1)} %pad_maximum_fusion), channel_id=1, source_target_pairs={{0,4},{4,0},{1,5},{5,1},{2,6},{6,2},{3,7},{7,3},{8,12},{12,8},{9,1... | collective-permute-start | bytes 1572872 | tf_op jit(solution)/shard_map/ppermute | solution.py:43
  17.0 15.2 %collective-permute-start.1 = (bf16[256,512]{1,0:T(8,128)(2,1)S(1)}, bf16[256,512]{1,0:T(8,128)(2,1)S(1)}, u32[]{:S(2)}, u32[]{:S(2)}) collective-permute-start(bf16[256,512]{1,0:T(8,128)(2,1)S(1)} %bitcast.13), channel_id=1, source_target_pairs={{0,8},{8,16},{16,24},{24,32},{32,40},{40,48},{48,56},{56,64},{64,7... | collective-permute-start | bytes 786440 | tf_op jit(solution)/shard_map/ppermute | solution.py:39
  21.6 15.1 %collective-permute-start.3 = (bf16[256,512]{1,0:T(8,128)(2,1)S(1)}, bf16[256,512]{1,0:T(8,128)(2,1)S(1)}, u32[]{:S(2)}, u32[]{:S(2)}) collective-permute-start(bf16[256,512]{1,0:T(8,128)(2,1)S(1)} %bitcast.10), channel_id=1, source_target_pairs={{0,8},{8,16},{16,24},{24,32},{32,40},{40,48},{48,56},{56,64},{64,7... | collective-permute-start | bytes 786440 | tf_op jit(solution)/shard_map/ppermute | solution.py:39
  32.2 11.5 %collective-permute-start.2 = (bf16[256,512]{1,0:T(8,128)(2,1)S(1)}, bf16[256,512]{1,0:T(8,128)(2,1)S(1)}, u32[]{:S(2)}, u32[]{:S(2)}) collective-permute-start(bf16[256,512]{1,0:T(8,128)(2,1)S(1)} %collective-permute-done.1.refs_7_), channel_id=1, source_target_pairs={{0,8},{8,16},{16,24},{24,32},{32,40},{40,48},{48,56},{56,64},{64,7... | collective-permute-start | bytes 786440 | tf_op jit(solution)/shard_map/ppermute | solution.py:39
  36.7 13.0 %collective-permute-start.5 = (bf16[256,512]{1,0:T(8,128)(2,1)S(1)}, bf16[256,512]{1,0:T(8,128)(2,1)S(1)}, u32[]{:S(2)}, u32[]{:S(2)}) collective-permute-start(bf16[256,512]{1,0:T(8,128)(2,1)S(1)} %collective-permute-done.3.refs_6_), channel_id=1, source_target_pairs={{0,8},{8,16},{16,24},{24,32},{32,40},{40,48},{48,56},{56,64},{64,7... | collective-permute-start | bytes 786440 | tf_op jit(solution)/shard_map/ppermute | solution.py:39
  43.7 11.2 %collective-permute-start.4 = (bf16[256,512]{1,0:T(8,128)(2,1)S(1)}, bf16[256,512]{1,0:T(8,128)(2,1)S(1)}, u32[]{:S(2)}, u32[]{:S(2)}) collective-permute-start(bf16[256,512]{1,0:T(8,128)(2,1)S(1)} %collective-permute-done.2.refs_5_.refs_6_), channel_id=1, source_target_pairs={{0,8},{8,16},{16,24},{24,32},{32,40},{40,48},{48,56},{56,64},{64,7... | collective-permute-start | bytes 786440 | tf_op jit(solution)/shard_map/ppermute | solution.py:39
  49.7 13.0 %collective-permute-start.7 = (bf16[256,512]{1,0:T(8,128)(2,1)S(1)}, bf16[256,512]{1,0:T(8,128)(2,1)S(1)}, u32[]{:S(2)}, u32[]{:S(2)}) collective-permute-start(bf16[256,512]{1,0:T(8,128)(2,1)S(1)} %collective-permute-done.5.refs_4_.refs_5_), channel_id=1, source_target_pairs={{0,8},{8,16},{16,24},{24,32},{32,40},{40,48},{48,56},{56,64},{64,7... | collective-permute-start | bytes 786440 | tf_op jit(solution)/shard_map/ppermute | solution.py:39
  54.9 10.8 %collective-permute-start.6 = (bf16[256,512]{1,0:T(8,128)(2,1)S(1)}, bf16[256,512]{1,0:T(8,128)(2,1)S(1)}, u32[]{:S(2)}, u32[]{:S(2)}) collective-permute-start(bf16[256,512]{1,0:T(8,128)(2,1)S(1)} %collective-permute-done.4.refs_5_.refs_6_), channel_id=1, source_target_pairs={{0,8},{8,16},{16,24},{24,32},{32,40},{40,48},{48,56},{56,64},{64,7... | collective-permute-start | bytes 786440 | tf_op jit(solution)/shard_map/ppermute | solution.py:39
  67.4 11.4 %collective-permute-start.8 = (bf16[256,512]{1,0:T(8,128)(2,1)S(1)}, bf16[256,512]{1,0:T(8,128)(2,1)S(1)}, u32[]{:S(2)}, u32[]{:S(2)}) collective-permute-start(bf16[256,512]{1,0:T(8,128)(2,1)S(1)} %get-tuple-element.50), channel_id=1, source_target_pairs={{8,0},{16,8},{24,16},{32,24},{40,32},{48,40},{56,48},{64,56},{72,6... | collective-permute-start | bytes 786440 | tf_op jit(solution)/shard_map/ppermute | solution.py:39
  73.2 9.2 %collective-permute-start.9 = (bf16[256,512]{1,0:T(8,128)(2,1)S(1)}, bf16[256,512]{1,0:T(8,128)(2,1)S(1)}, u32[]{:S(2)}, u32[]{:S(2)}) collective-permute-start(bf16[256,512]{1,0:T(8,128)(2,1)S(1)} %get-tuple-element.52), channel_id=1, source_target_pairs={{8,0},{16,8},{24,16},{32,24},{40,32},{48,40},{56,48},{64,56},{72,6... | collective-permute-start | bytes 786440 | tf_op jit(solution)/shard_map/ppermute | solution.py:39
  78.8 12.1 %collective-permute-start.10 = (bf16[256,512]{1,0:T(8,128)(2,1)S(1)}, bf16[256,512]{1,0:T(8,128)(2,1)S(1)}, u32[]{:S(2)}, u32[]{:S(2)}) collective-permute-start(bf16[256,512]{1,0:T(8,128)(2,1)S(1)} %add_convert_fusion.6), channel_id=1, source_target_pairs={{8,0},{16,8},{24,16},{32,24},{40,32},{48,40},{56,48},{64,56},{72,6... | collective-permute-start | bytes 786440 | tf_op jit(solution)/shard_map/ppermute | solution.py:39
  85.9 11.4 %collective-permute-start.14 = (bf16[256,512]{1,0:T(8,128)(2,1)S(1)}, bf16[256,512]{1,0:T(8,128)(2,1)S(1)}, u32[]{:S(2)}, u32[]{:S(2)}) collective-permute-start(bf16[256,512]{1,0:T(8,128)(2,1)S(1)} %add_convert_fusion.3), channel_id=1, source_target_pairs={{8,0},{16,8},{24,16},{32,24},{40,32},{48,40},{56,48},{64,56},{72,6... | collective-permute-start | bytes 786440 | tf_op jit(solution)/shard_map/ppermute | solution.py:39
  91.0 11.2 %collective-permute-start.12 = (bf16[256,512]{1,0:T(8,128)(2,1)S(1)}, bf16[256,512]{1,0:T(8,128)(2,1)S(1)}, u32[]{:S(2)}, u32[]{:S(2)}) collective-permute-start(bf16[256,512]{1,0:T(8,128)(2,1)S(1)} %add_convert_fusion.5), channel_id=1, source_target_pairs={{8,0},{16,8},{24,16},{32,24},{40,32},{48,40},{56,48},{64,56},{72,6... | collective-permute-start | bytes 786440 | tf_op jit(solution)/shard_map/ppermute | solution.py:39
  97.4 10.3 %collective-permute-start.15 = (bf16[256,512]{1,0:T(8,128)(2,1)S(1)}, bf16[256,512]{1,0:T(8,128)(2,1)S(1)}, u32[]{:S(2)}, u32[]{:S(2)}) collective-permute-start(bf16[256,512]{1,0:T(8,128)(2,1)S(1)} %add_convert_fusion.2), channel_id=1, source_target_pairs={{8,0},{16,8},{24,16},{32,24},{40,32},{48,40},{56,48},{64,56},{72,6... | collective-permute-start | bytes 786440 | tf_op jit(solution)/shard_map/ppermute | solution.py:39
  101.8 6.8 %collective-permute-start.11 = (bf16[256,512]{1,0:T(8,128)(2,1)S(1)}, bf16[256,512]{1,0:T(8,128)(2,1)S(1)}, u32[]{:S(2)}, u32[]{:S(2)}) collective-permute-start(bf16[256,512]{1,0:T(8,128)(2,1)S(1)} %get-tuple-element.59), channel_id=1, source_target_pairs={{0,4},{4,0},{1,5},{5,1},{2,6},{6,2},{3,7},{7,3},{8,12},{12,8},{9,1... | collective-permute-start | bytes 786440 | tf_op jit(solution)/shard_map/ppermute | solution.py:43
  102.2 8.3 %collective-permute-start.13 = (bf16[256,512]{1,0:T(8,128)(2,1)S(1)}, bf16[256,512]{1,0:T(8,128)(2,1)S(1)}, u32[]{:S(2)}, u32[]{:S(2)}) collective-permute-start(bf16[256,512]{1,0:T(8,128)(2,1)S(1)} %add_convert_fusion.4), channel_id=1, source_target_pairs={{8,0},{16,8},{24,16},{32,24},{40,32},{48,40},{56,48},{64,56},{72,6... | collective-permute-start | bytes 786440 | tf_op jit(solution)/shard_map/ppermute | solution.py:39
  111.3 13.8 %all-to-all-start.1 = ((bf16[8,64,512]{2,1,0:T(8,128)(2,1)}), bf16[8,64,512]{2,1,0:T(8,128)(2,1)S(1)}, u32[]{:S(2)}, u32[]{:S(2)}) async-start(bf16[8,64,512]{2,1,0:T(8,128)(2,1)} %bitcast.7), calls=%async_computation.1 | async-start | bytes 1048576 | tf_op jit(solution)/shard_map/all_to_all | solution.py:386

commit v7 on v6

--- a/solution.py
+++ b/solution.py
@@ -395,7 +395,7 @@
     ga3, gb3, dqt = grads((2, 4), tables, norm, (a3, b3), dqt, (low16, full), light=True)
     ra = slab_shift(ga3, -1)
     g0, dqt = grads((14, 16), tables, norm, (a0, b0), dqt, (full,), light=True)
-    dqt, rb = lax.optimization_barrier((dqt, rb))
+    dqt = lax.optimization_barrier((rb, dqt))[1]
     rb = slab_shift(summed(gb3, rb), -1)
     dqt, ra = lax.optimization_barrier((dqt, ra))
     ga2, gb2, dqt = grads((6, 8), tables, norm, (a2, b2), dqt, (full, full))

time: 127 us -> 128 us (level)
    ppermute x14, starting transfers between devices: 41.8 us -> 43.2 us  [slab_shift(): lax.ppermute(x, SLAB_AXES, [(i, i + by) for i in range(count) if 0 <= i +...]
  transfers between devices with their start and end apart: 18 -> 18, of which waited for: 12 -> 13; matrix products, arithmetic and copies ran while one was open for 2% -> 2% of each run, Pallas kernels for 17% -> 17%
where the time goes in v7:
time: 128 us
  starting transfers between devices  53.5 us (42%)
  waiting for transfers between devices  43.3 us (34%)
  Pallas kernels  26.6 us (21%)
  other arithmetic  2.02 us (2%)
  local copies, waits for them, and re-layouts  1.37 us (1%)
    ppermute x14, starting transfers between devices, slab_shift(): lax.ppermute(x, SLAB_AXES, [(i, i + by) for i in range(count) if 0 <= i +...  43.2 us
    ppermute x14, waiting for transfers between devices, slab_shift(): lax.ppermute(x, SLAB_AXES, [(i, i + by) for i in range(count) if 0 <= i +...  26.7 us
    pallas_call x4, Pallas kernels, grads(): call(functools.partial(grads_kernel, first_blocks, opening, closing), 'gr...  12.8 us
    all_to_all x1, waiting for transfers between devices, to_owners(): lax.all_to_all(x.reshape(8, SPAN // 4, 2 * WIDTH), MEMBER_AXES, 0, 0, til...  8.94 us
    pallas_call x3, Pallas kernels, stats(): call(functools.partial(stats_kernel, first_blocks, opening, closing), 'st...  7.78 us
    all_to_all x1, waiting for transfers between devices, per_device(): own = lax.all_to_all(kv, MEMBER_AXES, 0, 0, tiled=True)  7.64 us
    all_to_all x1, starting transfers between devices, per_device(): own = lax.all_to_all(kv, MEMBER_AXES, 0, 0, tiled=True)  4.31 us
    all_to_all x1, starting transfers between devices, to_owners(): lax.all_to_all(x.reshape(8, SPAN // 4, 2 * WIDTH), MEMBER_AXES, 0, 0, til...  3.49 us
  transfers between devices with their start and end apart: 18, of which 13 were waited for; matrix products, arithmetic and copies ran while one was open for 2% of the time, Pallas kernels for 17%

profile of v7, /device:TPU:24, one launch (start us, length us, event | category | flops | bytes accessed | tf_op | source)
XLA Modules:
  0.0 127.6 jit_solution(1113958596783851504)
XLA Ops:
  0.7 1.9 %pack.1 = bf16[8,64,512]{2,1,0:T(8,128)(2,1)} custom-call(bf16[64,2048]{1,0:T(8,128)(2,1)} %k_ref.1, bf16[64,2048]{1,0:T(8,128)(2,1)} %v_ref.1), custom_call_target="tpu_custom_call" | custom-call | tf_op jit(solution)/shard_map/pack/pallas_call | solution.py:339
  2.6 4.3 %all-to-all-start = ((bf16[8,64,512]{2,1,0:T(8,128)(2,1)}), bf16[8,64,512]{2,1,0:T(8,128)(2,1)S(1)}, u32[]{:S(2)}, u32[]{:S(2)}) async-start(bf16[8,64,512]{2,1,0:T(8,128)(2,1)} %pack.1), calls=%async_computation | async-start | bytes 1048576 | tf_op jit(solution)/shard_map/all_to_all | solution.py:348
  7.1 2.1 %collective-permute-start = (bf16[2,256,512]{2,1,0:T(8,128)(2,1)S(1)}, bf16[2,256,512]{2,1,0:T(8,128)(2,1)S(1)}, u32[]{:S(2)}, u32[]{:S(2)}) collective-permute-start(bf16[2,256,512]{2,1,0:T(8,128)(2,1)S(1)} %pad_maximum_fusion), channel_id=1, source_target_pairs={{0,4},{4,0},{1,5},{5,1},{2,6},{6,2},{3,7},{7,3},{8,12},{12,8},{9,1... | collective-permute-start | bytes 1572872 | tf_op jit(solution)/shard_map/ppermute | solution.py:43
  9.3 7.6 %all-to-all-done = bf16[8,64,512]{2,1,0:T(8,128)(2,1)S(1)} async-done(((bf16[8,64,512]{2,1,0:T(8,128)(2,1)}), bf16[8,64,512]{2,1,0:T(8,128)(2,1)S(1)}, u32[]{:S(2)}, u32[]{:S(2)}) %all-to-all-start) | async-done | bytes 524320 | tf_op jit(solution)/shard_map/all_to_all | solution.py:348
  17.0 3.8 %collective-permute-start.1 = (bf16[256,512]{1,0:T(8,128)(2,1)S(1)}, bf16[256,512]{1,0:T(8,128)(2,1)S(1)}, u32[]{:S(2)}, u32[]{:S(2)}) collective-permute-start(bf16[256,512]{1,0:T(8,128)(2,1)S(1)} %bitcast.13), channel_id=1, source_target_pairs={{0,8},{8,16},{16,24},{24,32},{32,40},{40,48},{48,56},{56,64},{64,7... | collective-permute-start | bytes 786440 | tf_op jit(solution)/shard_map/ppermute | solution.py:39
  20.9 0.7 convert_reduce_fusion
  21.6 3.8 %collective-permute-start.3 = (bf16[256,512]{1,0:T(8,128)(2,1)S(1)}, bf16[256,512]{1,0:T(8,128)(2,1)S(1)}, u32[]{:S(2)}, u32[]{:S(2)}) collective-permute-start(bf16[256,512]{1,0:T(8,128)(2,1)S(1)} %bitcast.10), channel_id=1, source_target_pairs={{0,8},{8,16},{16,24},{24,32},{32,40},{40,48},{48,56},{56,64},{64,7... | collective-permute-start | bytes 786440 | tf_op jit(solution)/shard_map/ppermute | solution.py:39
  25.4 6.8 %collective-permute-done.1.refs_7_ = bf16[256,512]{1,0:T(8,128)(2,1)S(1)} collective-permute-done((bf16[256,512]{1,0:T(8,128)(2,1)S(1)}, bf16[256,512]{1,0:T(8,128)(2,1)S(1)}, u32[]{:S(2)}, u32[]{:S(2)}) %collective-permute-start.1) | collective-permute-done | bytes 262176 | tf_op jit(solution)/shard_map/ppermute | solution.py:39
  32.2 1.9 %collective-permute-start.2 = (bf16[256,512]{1,0:T(8,128)(2,1)S(1)}, bf16[256,512]{1,0:T(8,128)(2,1)S(1)}, u32[]{:S(2)}, u32[]{:S(2)}) collective-permute-start(bf16[256,512]{1,0:T(8,128)(2,1)S(1)} %collective-permute-done.1.refs_7_), channel_id=1, source_target_pairs={{0,8},{8,16},{16,24},{24,32},{32,40},{40,48},{48,56},{56,64},{64,7... | collective-permute-start | bytes 786440 | tf_op jit(solution)/shard_map/ppermute | solution.py:39
  34.1 0.1 copy.13
  34.2 0.1 rev.3
  34.4 0.2 rows.1
  34.6 2.1 %collective-permute-done.3.refs_6_ = bf16[256,512]{1,0:T(8,128)(2,1)S(1)} collective-permute-done((bf16[256,512]{1,0:T(8,128)(2,1)S(1)}, bf16[256,512]{1,0:T(8,128)(2,1)S(1)}, u32[]{:S(2)}, u32[]{:S(2)}) %collective-permute-start.3) | collective-permute-done | bytes 262176 | tf_op jit(solution)/shard_map/ppermute | solution.py:39
  36.7 1.9 %collective-permute-start.5 = (bf16[256,512]{1,0:T(8,128)(2,1)S(1)}, bf16[256,512]{1,0:T(8,128)(2,1)S(1)}, u32[]{:S(2)}, u32[]{:S(2)}) collective-permute-start(bf16[256,512]{1,0:T(8,128)(2,1)S(1)} %collective-permute-done.3.refs_6_), channel_id=1, source_target_pairs={{0,8},{8,16},{16,24},{24,32},{32,40},{40,48},{48,56},{56,64},{64,7... | collective-permute-start | bytes 786440 | tf_op jit(solution)/shard_map/ppermute | solution.py:39
  38.6 3.3 %stats.3.refs_6_ = f32[2,3,8,1024]{3,2,1,0:T(8,128)S(1)} custom-call(s32[4,14]{1,0:T(4,128)S(1)} %fusion.1.refs_0_.hit_ref.refs_1_, s32[1,512]{1,0:T(1,128)S(1)} %bitcast.16, bf16[2,1024,128]{2,1,0:T(8,128)(2,1)S(1)} %get-tuple-element.37.refs_2_.q_ref.refs_3_, bf16[2,1024,128]{2,1,0:T(8,128)(2,1)S(1)} %get-tuple-element.38.refs_3_.do_ref.refs_4_, ...), custom_call_target="tpu_custom_call" | custom-call | flops 1024 | bytes 196608 | tf_op jit(solution)/shard_map/stats/pallas_call | solution.py:197
  41.9 1.8 %collective-permute-done.2.refs_5_.refs_6_ = bf16[256,512]{1,0:T(8,128)(2,1)S(1)} collective-permute-done((bf16[256,512]{1,0:T(8,128)(2,1)S(1)}, bf16[256,512]{1,0:T(8,128)(2,1)S(1)}, u32[]{:S(2)}, u32[]{:S(2)}) %collective-permute-start.2) | collective-permute-done | bytes 262176 | tf_op jit(solution)/shard_map/ppermute | solution.py:39
  43.7 1.9 %collective-permute-start.4 = (bf16[256,512]{1,0:T(8,128)(2,1)S(1)}, bf16[256,512]{1,0:T(8,128)(2,1)S(1)}, u32[]{:S(2)}, u32[]{:S(2)}) collective-permute-start(bf16[256,512]{1,0:T(8,128)(2,1)S(1)} %collective-permute-done.2.refs_5_.refs_6_), channel_id=1, source_target_pairs={{0,8},{8,16},{16,24},{24,32},{32,40},{40,48},{48,56},{56,64},{64,7... | collective-permute-start | bytes 786440 | tf_op jit(solution)/shard_map/ppermute | solution.py:39
  45.6 4.1 %collective-permute-done.5.refs_4_.refs_5_ = bf16[256,512]{1,0:T(8,128)(2,1)S(1)} collective-permute-done((bf16[256,512]{1,0:T(8,128)(2,1)S(1)}, bf16[256,512]{1,0:T(8,128)(2,1)S(1)}, u32[]{:S(2)}, u32[]{:S(2)}) %collective-permute-start.5) | collective-permute-done | bytes 262176 | tf_op jit(solution)/shard_map/ppermute | solution.py:39
  49.7 1.9 %collective-permute-start.7 = (bf16[256,512]{1,0:T(8,128)(2,1)S(1)}, bf16[256,512]{1,0:T(8,128)(2,1)S(1)}, u32[]{:S(2)}, u32[]{:S(2)}) collective-permute-start(bf16[256,512]{1,0:T(8,128)(2,1)S(1)} %collective-permute-done.5.refs_4_.refs_5_), channel_id=1, source_target_pairs={{0,8},{8,16},{16,24},{24,32},{32,40},{40,48},{48,56},{56,64},{64,7... | collective-permute-start | bytes 786440 | tf_op jit(solution)/shard_map/ppermute | solution.py:39
  51.6 2.3 %stats.4.refs_6_ = f32[2,3,8,1024]{3,2,1,0:T(8,128)S(1)} custom-call(s32[4,14]{1,0:T(4,128)S(1)} %fusion.1.refs_0_.hit_ref.refs_1_, s32[1,512]{1,0:T(1,128)S(1)} %bitcast.17, bf16[2,1024,128]{2,1,0:T(8,128)(2,1)S(1)} %get-tuple-element.37.refs_2_.q_ref.refs_3_, bf16[2,1024,128]{2,1,0:T(8,128)(2,1)S(1)} %get-tuple-element.38.refs_3_.do_ref.refs_4_, ...), custom_call_target="tpu_custom_call" | custom-call | flops 1024 | bytes 196608 | tf_op jit(solution)/shard_map/stats/pallas_call | solution.py:197
  53.9 1.0 collective-permute-done.4.refs_5_.refs_6_
  54.9 2.1 %collective-permute-start.6 = (bf16[256,512]{1,0:T(8,128)(2,1)S(1)}, bf16[256,512]{1,0:T(8,128)(2,1)S(1)}, u32[]{:S(2)}, u32[]{:S(2)}) collective-permute-start(bf16[256,512]{1,0:T(8,128)(2,1)S(1)} %collective-permute-done.4.refs_5_.refs_6_), channel_id=1, source_target_pairs={{0,8},{8,16},{16,24},{24,32},{32,40},{40,48},{48,56},{56,64},{64,7... | collective-permute-start | bytes 786440 | tf_op jit(solution)/shard_map/ppermute | solution.py:39
  56.9 5.7 %collective-permute-done.7.refs_4_.refs_5_ = bf16[256,512]{1,0:T(8,128)(2,1)S(1)} collective-permute-done((bf16[256,512]{1,0:T(8,128)(2,1)S(1)}, bf16[256,512]{1,0:T(8,128)(2,1)S(1)}, u32[]{:S(2)}, u32[]{:S(2)}) %collective-permute-start.7) | collective-permute-done | bytes 262176 | tf_op jit(solution)/shard_map/ppermute | solution.py:39
  62.6 2.2 %stats.5.state = f32[2,3,8,1024]{3,2,1,0:T(8,128)S(1)} custom-call(s32[4,14]{1,0:T(4,128)S(1)} %fusion.1.refs_0_.hit_ref.refs_1_, s32[1,512]{1,0:T(1,128)S(1)} %bitcast.18, bf16[2,1024,128]{2,1,0:T(8,128)(2,1)S(1)} %get-tuple-element.37.refs_2_.q_ref.refs_3_, bf16[2,1024,128]{2,1,0:T(8,128)(2,1)S(1)} %get-tuple-element.38.refs_3_.do_ref.refs_4_, ...), custom_call_target="tpu_custom_call" | custom-call | flops 1024 | bytes 196608 | tf_op jit(solution)/shard_map/stats/pallas_call | solution.py:197
  64.8 0.8 collective-permute-done.6.piece
  65.6 1.7 %finish.1 = (f32[2,8,1024]{2,1,0:T(8,128)S(1)}, bf16[256,512]{1,0:T(8,128)(2,1)S(1)}, f32[2,128,1024]{2,1,0:T(8,128)S(1)}) custom-call(s32[4,14]{1,0:T(4,128)S(1)} %fusion.1.refs_0_.hit_ref.refs_1_, s32[1,512]{1,0:T(1,128)S(1)} %bitcast.19, bf16[2,1024,128]{2,1,0:T(8,128)(2,1)S(1)} %get-tuple-element.37.refs_2_.q_ref.refs_3_, ...), custom_call_target="tpu_custom_call" | custom-call | flops 1024 | bytes 1376256 | tf_op jit(solution)/shard_map/finish/pallas_call | solution.py:324
  67.4 2.5 %collective-permute-start.8 = (bf16[256,512]{1,0:T(8,128)(2,1)S(1)}, bf16[256,512]{1,0:T(8,128)(2,1)S(1)}, u32[]{:S(2)}, u32[]{:S(2)}) collective-permute-start(bf16[256,512]{1,0:T(8,128)(2,1)S(1)} %get-tuple-element.46), channel_id=1, source_target_pairs={{8,0},{16,8},{24,16},{32,24},{40,32},{48,40},{56,48},{64,56},{72,6... | collective-permute-start | bytes 786440 | tf_op jit(solution)/shard_map/ppermute | solution.py:39
  69.9 3.3 %grads.4 = (bf16[256,512]{1,0:T(8,128)(2,1)S(1)}, f32[256,512]{1,0:T(8,128)S(1)}, f32[2,128,1024]{2,1,0:T(8,128)S(1)}) custom-call(s32[4,14]{1,0:T(4,128)S(1)} %fusion.1.refs_0_.hit_ref.refs_1_, s32[1,512]{1,0:T(1,128)S(1)} %bitcast.20, bf16[2,1024,128]{2,1,0:T(8,128)(2,1)S(1)} %get-tuple-element.37.refs_2_.q_ref.refs_3_, ...), custom_call_target="tpu_custom_call", output_to_operand_aliasing={{2}: (7, {})} | custom-call | flops 1024 | bytes 1 | tf_op jit(solution)/shard_map/grads/pallas_call | solution.py:306
  73.2 2.9 %collective-permute-start.9 = (bf16[256,512]{1,0:T(8,128)(2,1)S(1)}, bf16[256,512]{1,0:T(8,128)(2,1)S(1)}, u32[]{:S(2)}, u32[]{:S(2)}) collective-permute-start(bf16[256,512]{1,0:T(8,128)(2,1)S(1)} %get-tuple-element.51), channel_id=1, source_target_pairs={{8,0},{16,8},{24,16},{32,24},{40,32},{48,40},{56,48},{64,56},{72,6... | collective-permute-start | bytes 786440 | tf_op jit(solution)/shard_map/ppermute | solution.py:39
  76.2 0.4 collective-permute-done.8
  76.7 3.9 %collective-permute-start.10 = (bf16[256,512]{1,0:T(8,128)(2,1)S(1)}, bf16[256,512]{1,0:T(8,128)(2,1)S(1)}, u32[]{:S(2)}, u32[]{:S(2)}) collective-permute-start(bf16[256,512]{1,0:T(8,128)(2,1)S(1)} %add_convert_fusion.6), channel_id=1, source_target_pairs={{8,0},{16,8},{24,16},{32,24},{40,32},{48,40},{56,48},{64,56},{72,6... | collective-permute-start | bytes 786440 | tf_op jit(solution)/shard_map/ppermute | solution.py:39
  80.6 2.6 %grads.5 = (f32[512,512]{1,0:T(8,128)S(1)}, f32[2,128,1024]{2,1,0:T(8,128)S(1)}) custom-call(s32[4,14]{1,0:T(4,128)S(1)} %fusion.1.refs_0_.hit_ref.refs_1_, s32[1,512]{1,0:T(1,128)S(1)} %bitcast.21, bf16[2,1024,128]{2,1,0:T(8,128)(2,1)S(1)} %get-tuple-element.37.refs_2_.q_ref.refs_3_, ...), custom_call_target="tpu_custom_call", output_to_operand_aliasing={{1}: (7, {})} | custom-call | flops 1024 | bytes 1 | tf_op jit(solution)/shard_map/grads/pallas_call | solution.py:306
  83.2 0.9 collective-permute-done.9
  84.1 3.4 %grads.6 = (f32[256,512]{1,0:T(8,128)S(1)}, f32[256,512]{1,0:T(8,128)S(1)}, f32[2,128,1024]{2,1,0:T(8,128)S(1)}) custom-call(s32[4,14]{1,0:T(4,128)S(1)} %fusion.1.refs_0_.hit_ref.refs_1_, s32[1,512]{1,0:T(1,128)S(1)} %bitcast.22, bf16[2,1024,128]{2,1,0:T(8,128)(2,1)S(1)} %get-tuple-element.37.refs_2_.q_ref.refs_3_, ...), custom_call_target="tpu_custom_call", output_to_operand_aliasing={{2}: (7, {})} | custom-call | flops 1024 | bytes 2097152 | tf_op jit(solution)/shard_map/grads/pallas_call | solution.py:306
  87.5 4.6 %collective-permute-start.14 = (bf16[256,512]{1,0:T(8,128)(2,1)S(1)}, bf16[256,512]{1,0:T(8,128)(2,1)S(1)}, u32[]{:S(2)}, u32[]{:S(2)}) collective-permute-start(bf16[256,512]{1,0:T(8,128)(2,1)S(1)} %add_convert_fusion.3), channel_id=1, source_target_pairs={{8,0},{16,8},{24,16},{32,24},{40,32},{48,40},{56,48},{64,56},{72,6... | collective-permute-start | bytes 786440 | tf_op jit(solution)/shard_map/ppermute | solution.py:39
  92.3 1.9 %collective-permute-start.12 = (bf16[256,512]{1,0:T(8,128)(2,1)S(1)}, bf16[256,512]{1,0:T(8,128)(2,1)S(1)}, u32[]{:S(2)}, u32[]{:S(2)}) collective-permute-start(bf16[256,512]{1,0:T(8,128)(2,1)S(1)} %add_convert_fusion.5), channel_id=1, source_target_pairs={{8,0},{16,8},{24,16},{32,24},{40,32},{48,40},{56,48},{64,56},{72,6... | collective-permute-start | bytes 786440 | tf_op jit(solution)/shard_map/ppermute | solution.py:39
  94.2 3.5 %grads.7 = (f32[256,512]{1,0:T(8,128)S(1)}, f32[256,512]{1,0:T(8,128)S(1)}, f32[256,512]{1,0:T(8,128)S(1)}, bf16[256,512]{1,0:T(8,128)(2,1)S(1)}) custom-call(s32[1]{0:T(128)} %bitcast.low_ref.refs_0_, s32[4,14]{1,0:T(4,128)S(1)} %fusion.1.refs_0_.hit_ref.refs_1_, s32[1,512]{1,0:T(1,128)S(1)} %bitcast.23, ...), custom_call_target="tpu_custom_call" | custom-call | flops 1024 | bytes 1835008 | tf_op jit(solution)/shard_map/grads/pallas_call | solution.py:306
  97.8 5.0 %collective-permute-start.15 = (bf16[256,512]{1,0:T(8,128)(2,1)S(1)}, bf16[256,512]{1,0:T(8,128)(2,1)S(1)}, u32[]{:S(2)}, u32[]{:S(2)}) collective-permute-start(bf16[256,512]{1,0:T(8,128)(2,1)S(1)} %add_convert_fusion.2), channel_id=1, source_target_pairs={{8,0},{16,8},{24,16},{32,24},{40,32},{48,40},{56,48},{64,56},{72,6... | collective-permute-start | bytes 786440 | tf_op jit(solution)/shard_map/ppermute | solution.py:39
  102.8 0.3 collective-permute-start.11
  103.2 0.2 collective-permute-done.12
  103.5 5.0 %collective-permute-start.13 = (bf16[256,512]{1,0:T(8,128)(2,1)S(1)}, bf16[256,512]{1,0:T(8,128)(2,1)S(1)}, u32[]{:S(2)}, u32[]{:S(2)}) collective-permute-start(bf16[256,512]{1,0:T(8,128)(2,1)S(1)} %add_convert_fusion.4), channel_id=1, source_target_pairs={{8,0},{16,8},{24,16},{32,24},{40,32},{48,40},{56,48},{64,56},{72,6... | collective-permute-start | bytes 786440 | tf_op jit(solution)/shard_map/ppermute | solution.py:39
  108.6 0.8 dynamic_update_slice.6
  109.4 2.9 %collective-permute-done.13 = bf16[256,512]{1,0:T(8,128)(2,1)S(1)} collective-permute-done((bf16[256,512]{1,0:T(8,128)(2,1)S(1)}, bf16[256,512]{1,0:T(8,128)(2,1)S(1)}, u32[]{:S(2)}, u32[]{:S(2)}) %collective-permute-start.13) | collective-permute-done | bytes 262176 | tf_op jit(solution)/shard_map/ppermute | solution.py:39
  112.3 0.8 fusion
  113.1 3.5 %all-to-all-start.1 = ((bf16[8,64,512]{2,1,0:T(8,128)(2,1)}), bf16[8,64,512]{2,1,0:T(8,128)(2,1)S(1)}, u32[]{:S(2)}, u32[]{:S(2)}) async-start(bf16[8,64,512]{2,1,0:T(8,128)(2,1)} %bitcast.7), calls=%async_computation.1 | async-start | bytes 1048576 | tf_op jit(solution)/shard_map/all_to_all | solution.py:386
  116.6 1.0 columns.1
  117.7 8.9 %all-to-all-done.1.in_ref = bf16[8,64,512]{2,1,0:T(8,128)(2,1)S(1)} async-done(((bf16[8,64,512]{2,1,0:T(8,128)(2,1)}), bf16[8,64,512]{2,1,0:T(8,128)(2,1)S(1)}, u32[]{:S(2)}, u32[]{:S(2)}) %all-to-all-start.1) | async-done | bytes 524320 | tf_op jit(solution)/shard_map/all_to_all | solution.py:386
  126.6 1.0 unpack.1
  (27 shorter events, 1.0 us)
Async XLA Ops:
  0.6 8.5 %copy-start = (s32[2,128,14]{1,0,2:T(2,128)S(1)}, s32[2,128,14]{1,0,2:T(2,128)}, u32[]{:S(2)}) copy-start(s32[2,128,14]{1,0,2:T(2,128)} %param.11) | copy-start | bytes 43012
  0.6 6.3 %copy-start.2 = (bf16[256,1024]{1,0:T(8,128)(2,1)S(1)}, bf16[256,1024]{1,0:T(8,128)(2,1)}, u32[]{:S(2)}) copy-start(bf16[256,1024]{1,0:T(8,128)(2,1)} %do_ref.1) | copy-start | bytes 1572868
  0.7 6.3 %copy-start.1 = (bf16[256,1024]{1,0:T(8,128)(2,1)S(1)}, bf16[256,1024]{1,0:T(8,128)(2,1)}, u32[]{:S(2)}) copy-start(bf16[256,1024]{1,0:T(8,128)(2,1)} %q_ref.1) | copy-start | bytes 1572868
  2.6 14.4 %all-to-all-start = ((bf16[8,64,512]{2,1,0:T(8,128)(2,1)}), bf16[8,64,512]{2,1,0:T(8,128)(2,1)S(1)}, u32[]{:S(2)}, u32[]{:S(2)}) async-start(bf16[8,64,512]{2,1,0:T(8,128)(2,1)} %pack.1), calls=%async_computation | async-start | bytes 1048576 | tf_op jit(solution)/shard_map/all_to_all | solution.py:348
  6.9 2.3 %copy-start.3 = (s32[16384]{0:T(1024)S(1)}, s32[16384]{0:T(1024)}, u32[]{:S(2)}) copy-start(s32[16384]{0:T(1024)} %param.10) | copy-start | bytes 196612
  7.1 27.3 %collective-permute-start = (bf16[2,256,512]{2,1,0:T(8,128)(2,1)S(1)}, bf16[2,256,512]{2,1,0:T(8,128)(2,1)S(1)}, u32[]{:S(2)}, u32[]{:S(2)}) collective-permute-start(bf16[2,256,512]{2,1,0:T(8,128)(2,1)S(1)} %pad_maximum_fusion), channel_id=1, source_target_pairs={{0,4},{4,0},{1,5},{5,1},{2,6},{6,2},{3,7},{7,3},{8,12},{12,8},{9,1... | collective-permute-start | bytes 1572872 | tf_op jit(solution)/shard_map/ppermute | solution.py:43
  17.0 15.2 %collective-permute-start.1 = (bf16[256,512]{1,0:T(8,128)(2,1)S(1)}, bf16[256,512]{1,0:T(8,128)(2,1)S(1)}, u32[]{:S(2)}, u32[]{:S(2)}) collective-permute-start(bf16[256,512]{1,0:T(8,128)(2,1)S(1)} %bitcast.13), channel_id=1, source_target_pairs={{0,8},{8,16},{16,24},{24,32},{32,40},{40,48},{48,56},{56,64},{64,7... | collective-permute-start | bytes 786440 | tf_op jit(solution)/shard_map/ppermute | solution.py:39
  21.6 15.1 %collective-permute-start.3 = (bf16[256,512]{1,0:T(8,128)(2,1)S(1)}, bf16[256,512]{1,0:T(8,128)(2,1)S(1)}, u32[]{:S(2)}, u32[]{:S(2)}) collective-permute-start(bf16[256,512]{1,0:T(8,128)(2,1)S(1)} %bitcast.10), channel_id=1, source_target_pairs={{0,8},{8,16},{16,24},{24,32},{32,40},{40,48},{48,56},{56,64},{64,7... | collective-permute-start | bytes 786440 | tf_op jit(solution)/shard_map/ppermute | solution.py:39
  32.2 11.5 %collective-permute-start.2 = (bf16[256,512]{1,0:T(8,128)(2,1)S(1)}, bf16[256,512]{1,0:T(8,128)(2,1)S(1)}, u32[]{:S(2)}, u32[]{:S(2)}) collective-permute-start(bf16[256,512]{1,0:T(8,128)(2,1)S(1)} %collective-permute-done.1.refs_7_), channel_id=1, source_target_pairs={{0,8},{8,16},{16,24},{24,32},{32,40},{40,48},{48,56},{56,64},{64,7... | collective-permute-start | bytes 786440 | tf_op jit(solution)/shard_map/ppermute | solution.py:39
  36.7 13.0 %collective-permute-start.5 = (bf16[256,512]{1,0:T(8,128)(2,1)S(1)}, bf16[256,512]{1,0:T(8,128)(2,1)S(1)}, u32[]{:S(2)}, u32[]{:S(2)}) collective-permute-start(bf16[256,512]{1,0:T(8,128)(2,1)S(1)} %collective-permute-done.3.refs_6_), channel_id=1, source_target_pairs={{0,8},{8,16},{16,24},{24,32},{32,40},{40,48},{48,56},{56,64},{64,7... | collective-permute-start | bytes 786440 | tf_op jit(solution)/shard_map/ppermute | solution.py:39
  43.7 11.2 %collective-permute-start.4 = (bf16[256,512]{1,0:T(8,128)(2,1)S(1)}, bf16[256,512]{1,0:T(8,128)(2,1)S(1)}, u32[]{:S(2)}, u32[]{:S(2)}) collective-permute-start(bf16[256,512]{1,0:T(8,128)(2,1)S(1)} %collective-permute-done.2.refs_5_.refs_6_), channel_id=1, source_target_pairs={{0,8},{8,16},{16,24},{24,32},{32,40},{40,48},{48,56},{56,64},{64,7... | collective-permute-start | bytes 786440 | tf_op jit(solution)/shard_map/ppermute | solution.py:39
  49.7 13.0 %collective-permute-start.7 = (bf16[256,512]{1,0:T(8,128)(2,1)S(1)}, bf16[256,512]{1,0:T(8,128)(2,1)S(1)}, u32[]{:S(2)}, u32[]{:S(2)}) collective-permute-start(bf16[256,512]{1,0:T(8,128)(2,1)S(1)} %collective-permute-done.5.refs_4_.refs_5_), channel_id=1, source_target_pairs={{0,8},{8,16},{16,24},{24,32},{32,40},{40,48},{48,56},{56,64},{64,7... | collective-permute-start | bytes 786440 | tf_op jit(solution)/shard_map/ppermute | solution.py:39
  54.9 10.8 %collective-permute-start.6 = (bf16[256,512]{1,0:T(8,128)(2,1)S(1)}, bf16[256,512]{1,0:T(8,128)(2,1)S(1)}, u32[]{:S(2)}, u32[]{:S(2)}) collective-permute-start(bf16[256,512]{1,0:T(8,128)(2,1)S(1)} %collective-permute-done.4.refs_5_.refs_6_), channel_id=1, source_target_pairs={{0,8},{8,16},{16,24},{24,32},{32,40},{40,48},{48,56},{56,64},{64,7... | collective-permute-start | bytes 786440 | tf_op jit(solution)/shard_map/ppermute | solution.py:39
  67.4 9.2 %collective-permute-start.8 = (bf16[256,512]{1,0:T(8,128)(2,1)S(1)}, bf16[256,512]{1,0:T(8,128)(2,1)S(1)}, u32[]{:S(2)}, u32[]{:S(2)}) collective-permute-start(bf16[256,512]{1,0:T(8,128)(2,1)S(1)} %get-tuple-element.46), channel_id=1, source_target_pairs={{8,0},{16,8},{24,16},{32,24},{40,32},{48,40},{56,48},{64,56},{72,6... | collective-permute-start | bytes 786440 | tf_op jit(solution)/shard_map/ppermute | solution.py:39
  73.2 10.8 %collective-permute-start.9 = (bf16[256,512]{1,0:T(8,128)(2,1)S(1)}, bf16[256,512]{1,0:T(8,128)(2,1)S(1)}, u32[]{:S(2)}, u32[]{:S(2)}) collective-permute-start(bf16[256,512]{1,0:T(8,128)(2,1)S(1)} %get-tuple-element.51), channel_id=1, source_target_pairs={{8,0},{16,8},{24,16},{32,24},{40,32},{48,40},{56,48},{64,56},{72,6... | collective-permute-start | bytes 786440 | tf_op jit(solution)/shard_map/ppermute | solution.py:39
  76.7 15.5 %collective-permute-start.10 = (bf16[256,512]{1,0:T(8,128)(2,1)S(1)}, bf16[256,512]{1,0:T(8,128)(2,1)S(1)}, u32[]{:S(2)}, u32[]{:S(2)}) collective-permute-start(bf16[256,512]{1,0:T(8,128)(2,1)S(1)} %add_convert_fusion.6), channel_id=1, source_target_pairs={{8,0},{16,8},{24,16},{32,24},{40,32},{48,40},{56,48},{64,56},{72,6... | collective-permute-start | bytes 786440 | tf_op jit(solution)/shard_map/ppermute | solution.py:39
  87.5 10.2 %collective-permute-start.14 = (bf16[256,512]{1,0:T(8,128)(2,1)S(1)}, bf16[256,512]{1,0:T(8,128)(2,1)S(1)}, u32[]{:S(2)}, u32[]{:S(2)}) collective-permute-start(bf16[256,512]{1,0:T(8,128)(2,1)S(1)} %add_convert_fusion.3), channel_id=1, source_target_pairs={{8,0},{16,8},{24,16},{32,24},{40,32},{48,40},{56,48},{64,56},{72,6... | collective-permute-start | bytes 786440 | tf_op jit(solution)/shard_map/ppermute | solution.py:39
  92.3 11.1 %collective-permute-start.12 = (bf16[256,512]{1,0:T(8,128)(2,1)S(1)}, bf16[256,512]{1,0:T(8,128)(2,1)S(1)}, u32[]{:S(2)}, u32[]{:S(2)}) collective-permute-start(bf16[256,512]{1,0:T(8,128)(2,1)S(1)} %add_convert_fusion.5), channel_id=1, source_target_pairs={{8,0},{16,8},{24,16},{32,24},{40,32},{48,40},{56,48},{64,56},{72,6... | collective-permute-start | bytes 786440 | tf_op jit(solution)/shard_map/ppermute | solution.py:39
  97.8 10.6 %collective-permute-start.15 = (bf16[256,512]{1,0:T(8,128)(2,1)S(1)}, bf16[256,512]{1,0:T(8,128)(2,1)S(1)}, u32[]{:S(2)}, u32[]{:S(2)}) collective-permute-start(bf16[256,512]{1,0:T(8,128)(2,1)S(1)} %add_convert_fusion.2), channel_id=1, source_target_pairs={{8,0},{16,8},{24,16},{32,24},{40,32},{48,40},{56,48},{64,56},{72,6... | collective-permute-start | bytes 786440 | tf_op jit(solution)/shard_map/ppermute | solution.py:39
  102.8 6.6 %collective-permute-start.11 = (bf16[256,512]{1,0:T(8,128)(2,1)S(1)}, bf16[256,512]{1,0:T(8,128)(2,1)S(1)}, u32[]{:S(2)}, u32[]{:S(2)}) collective-permute-start(bf16[256,512]{1,0:T(8,128)(2,1)S(1)} %get-tuple-element.57), channel_id=1, source_target_pairs={{0,4},{4,0},{1,5},{5,1},{2,6},{6,2},{3,7},{7,3},{8,12},{12,8},{9,1... | collective-permute-start | bytes 786440 | tf_op jit(solution)/shard_map/ppermute | solution.py:43
  103.5 8.8 %collective-permute-start.13 = (bf16[256,512]{1,0:T(8,128)(2,1)S(1)}, bf16[256,512]{1,0:T(8,128)(2,1)S(1)}, u32[]{:S(2)}, u32[]{:S(2)}) collective-permute-start(bf16[256,512]{1,0:T(8,128)(2,1)S(1)} %add_convert_fusion.4), channel_id=1, source_target_pairs={{8,0},{16,8},{24,16},{32,24},{40,32},{48,40},{56,48},{64,56},{72,6... | collective-permute-start | bytes 786440 | tf_op jit(solution)/shard_map/ppermute | solution.py:39
  113.1 13.5 %all-to-all-start.1 = ((bf16[8,64,512]{2,1,0:T(8,128)(2,1)}), bf16[8,64,512]{2,1,0:T(8,128)(2,1)S(1)}, u32[]{:S(2)}, u32[]{:S(2)}) async-start(bf16[8,64,512]{2,1,0:T(8,128)(2,1)} %bitcast.7), calls=%async_computation.1 | async-start | bytes 1048576 | tf_op jit(solution)/shard_map/all_to_all | solution.py:386
